TPU v7x, 256 devices: a whole 4x4x8 slice. The times are simulated.
256 devices in a mesh: slab: 64 (over y_hi, z, x), cross: 4 (over y_lo, core).
Axes of the slice: x: 4, y: 4 (y_hi: 2, y_lo: 2; y = y_hi * 2 + y_lo), z: 8, core: 2. Of those that a mesh axis runs over, the one named last changes fastest.
Arguments:
- features: bfloat16 [128, 8, 30, 128], P('slab', 'cross'), may hold values from -6 to 6
- position: float32 [128, 8, 2, 128], P('slab', 'cross'), may hold values from -6 to 6
- velocity: float32 [128, 8, 2, 128], P('slab', 'cross'), may hold values from -6 to 6
- occupancy: int32 [128, 8], P('slab', 'cross'), may hold values from 32 to 128
- neighbor_codes: int32 [128, 8, 16, 128], P('slab', 'cross'), may hold values from 0 to 1151
- edge_mask: int32 [128, 8, 16, 128], P('slab', 'cross'), may hold values 0 or 1
- enc_first: bfloat16 [30, 128], replicated, may hold values from -1 to 1
- enc_second: bfloat16 [128, 128], replicated, may hold values from -0.5 to 0.5
- edge_recv: bfloat16 [3, 128, 512], replicated, may hold values from -0.5 to 0.5
- edge_send: bfloat16 [3, 128, 512], replicated, may hold values from -0.5 to 0.5
- edge_geo: float32 [3, 3, 512], replicated, may hold values from -3.5 to 3.5
- edge_out: bfloat16 [3, 512, 128], replicated, may hold values from -0.25 to 0.25
- node_first: bfloat16 [3, 256, 128], replicated, may hold values from -0.375 to 0.375
- node_second: bfloat16 [3, 128, 128], replicated, may hold values from -0.5 to 0.5
- dec_first: bfloat16 [128, 128], replicated, may hold values from -0.5 to 0.5
- dec_second: bfloat16 [128, 2], replicated, may hold values from -0.5 to 0.5
Outputs:
- new_velocity: float32 [128, 8, 2, 128], P('slab', 'cross')
- new_position: float32 [128, 8, 2, 128], P('slab', 'cross')
All inputs are finite; a program needn't handle non-finite values. No bound on the sum of `edge_mask` on one device may be relied on, other than what follows from the above.
Results may differ from a plain program's by a relative error of at most 0.015.
Values may be sent and summed in bfloat16 or wider, within the bound.
No kernel may reach another device: no remote copies, remote signals or barrier semaphores. Data moves between devices by JAX's collectives and lax.ppermute only.
A program may use at most 64 MiB of HBM per device.

v0:
```python
import jax
import jax.numpy as jnp
from jax import lax
from jax.sharding import PartitionSpec as P

time_step = 0.5


def extended(block, sides, width):
    for axis, dim in sides:
        count = lax.axis_size(axis)
        forward = [(i, i + 1) for i in range(count - 1)]
        backward = [(target, source) for source, target in forward]
        low = lax.ppermute(
            lax.slice_in_dim(block, block.shape[dim] - width, None, axis=dim), axis, forward
        )
        high = lax.ppermute(lax.slice_in_dim(block, 0, width, axis=dim), axis, backward)
        block = jnp.concatenate([low, block, high], axis=dim)
    return block


def layer_norm(values):
    center = values - jnp.mean(values, axis=-1, keepdims=True)
    spread = jnp.mean(center * center, axis=-1, keepdims=True)
    return center * lax.rsqrt(spread + 1e-05)


def border(values):
    return extended(values, (("slab", 0), ("cross", 1)), 1)


def windows(padded, size_x, size_y):
    pieces = []
    for shift_x in range(3):
        for shift_y in range(3):
            pieces.append(padded[shift_x : shift_x + size_x, shift_y : shift_y + size_y])
    return jnp.stack(pieces, axis=2)


def message_step(
    latent,
    padded_latent,
    geo_window,
    geometry,
    codes,
    edge_mask,
    recv_weight,
    send_weight,
    geo_weight,
    out_weight,
    first_weight,
    second_weight,
):
    size_x, size_y, slot_count, width = latent.shape
    knb = codes.shape[2]
    bins = size_x * size_y
    lat_window = windows(padded_latent, size_x, size_y).reshape(bins, 9 * slot_count, width)
    own_latent = latent.reshape(bins, slot_count, width)
    own_geo = geometry.reshape(bins, 3, slot_count)
    code_bins = codes.reshape(bins, knb * slot_count)
    mask_bins = edge_mask.reshape(bins, knb, slot_count)

    def one_bin(items):
        lat_win, geo_win, own_lat, own_g, code_row, mask_row = items
        choices_iota = lax.broadcasted_iota(jnp.int32, (1, 9 * slot_count), 1)
        selector = (code_row[:, None] == choices_iota).astype(jnp.bfloat16)
        sender_lat = jnp.dot(selector, lat_win, preferred_element_type=jnp.float32).astype(
            jnp.bfloat16
        )
        other = lax.dot_general(
            geo_win,
            selector.astype(jnp.float32),
            (((1,), (1,)), ((), ())),
            precision=lax.Precision.HIGHEST,
        )
        sender = jnp.dot(sender_lat, send_weight, preferred_element_type=jnp.float32).astype(
            jnp.bfloat16
        )
        recv_proj = jnp.dot(own_lat, recv_weight, preferred_element_type=jnp.float32).astype(
            jnp.bfloat16
        )
        other_x = other[0].reshape(knb, slot_count)
        other_y = other[1].reshape(knb, slot_count)
        other_live = other[2].reshape(knb, slot_count)
        delta_x = other_x - own_g[0][None, :]
        delta_y = other_y - own_g[1][None, :]
        distance = delta_x * delta_x + delta_y * delta_y
        geo_term = (
            delta_x[:, :, None] * geo_weight[0]
            + delta_y[:, :, None] * geo_weight[1]
            + distance[:, :, None] * geo_weight[2]
        )
        hidden = jax.nn.relu(
            recv_proj.astype(jnp.float32)[None]
            + sender.reshape(knb, slot_count, -1).astype(jnp.float32)
            + geo_term
        ).astype(jnp.bfloat16)
        message = jnp.dot(
            hidden.reshape(knb * slot_count, -1), out_weight, preferred_element_type=jnp.float32
        ).reshape(knb, slot_count, width)
        valid = mask_row.astype(jnp.float32) * own_g[2][None, :] * other_live
        return jnp.sum(valid[:, :, None] * message, axis=0)

    total = lax.map(one_bin, (lat_window, geo_window, own_latent, own_geo, code_bins, mask_bins))
    summed = total.reshape(-1, width).astype(jnp.bfloat16)
    flat = latent.reshape(-1, width)
    joined = jnp.dot(flat, first_weight[:width], preferred_element_type=jnp.float32) + jnp.dot(
        summed, first_weight[width:], preferred_element_type=jnp.float32
    )
    joined = jax.nn.relu(joined).astype(jnp.bfloat16)
    update = jnp.dot(joined, second_weight, preferred_element_type=jnp.float32)
    result = (flat.astype(jnp.float32) + layer_norm(update)).astype(jnp.bfloat16)
    return result.reshape(latent.shape)


def shards(
    features,
    position,
    velocity,
    occupancy,
    neighbor_codes,
    edge_mask,
    enc_first,
    enc_second,
    edge_recv,
    edge_send,
    edge_geo,
    edge_out,
    node_first,
    node_second,
    dec_first,
    dec_second,
):
    size_x, size_y, count_two, slot_count = position.shape
    slot_index = lax.broadcasted_iota(jnp.int32, (size_x, size_y, 1, slot_count), 3)
    live = (slot_index < occupancy[:, :, None, None]).astype(jnp.float32)
    geometry = jnp.concatenate([position, live], axis=2)
    padded_geo = extended(geometry, (("slab", 0), ("cross", 1)), 1)
    geo_window = windows(padded_geo, size_x, size_y)
    geo_window = jnp.transpose(geo_window, (0, 1, 3, 2, 4)).reshape(
        size_x * size_y, 3, 9 * slot_count
    )
    enc_hidden = jax.nn.relu(
        jnp.einsum("xyfs,fh->xysh", features, enc_first, preferred_element_type=jnp.float32)
    ).astype(jnp.bfloat16)
    width = enc_second.shape[0]
    latent = layer_norm(
        jnp.dot(enc_hidden.reshape(-1, width), enc_second, preferred_element_type=jnp.float32)
    ).astype(jnp.bfloat16)
    latent = latent.reshape(size_x, size_y, slot_count, width)
    for layer_index in range(edge_recv.shape[0]):
        padded_latent = border(latent)
        latent = message_step(
            latent,
            padded_latent,
            geo_window,
            geometry,
            neighbor_codes,
            edge_mask,
            edge_recv[layer_index],
            edge_send[layer_index],
            edge_geo[layer_index],
            edge_out[layer_index],
            node_first[layer_index],
            node_second[layer_index],
        )
    dec_hidden = jax.nn.relu(
        jnp.dot(latent.reshape(-1, width), dec_first, preferred_element_type=jnp.float32)
    ).astype(jnp.bfloat16)
    accel = jnp.dot(dec_hidden, dec_second, preferred_element_type=jnp.float32)
    accel = jnp.transpose(accel.reshape(size_x, size_y, slot_count, 2), (0, 1, 3, 2)) * live
    new_velocity = velocity + time_step * accel
    new_position = position + time_step * new_velocity
    return (new_velocity, new_position)


def solution(mesh):
    return jax.shard_map(
        shards,
        mesh=mesh,
        in_specs=(
            P("slab", "cross", None, None),
            P("slab", "cross", None, None),
            P("slab", "cross", None, None),
            P("slab", "cross"),
            P("slab", "cross", None, None),
            P("slab", "cross", None, None),
            P(),
            P(),
            P(),
            P(),
            P(),
            P(),
            P(),
            P(),
            P(),
            P(),
        ),
        out_specs=(P("slab", "cross", None, None), P("slab", "cross", None, None)),
        check_vma=False,
    )
```

profile of v0, /device:TPU:17, one launch (start us, length us, event | category | flops | bytes accessed | tf_op | source)
XLA Modules:
  0.0 204.5 jit_solution(9962813367707010078)
XLA Ops:
  5.7 8.3 %collective-permute-start.5 = (bf16[1,2,128,128]{3,2,1,0:T(8,128)(2,1)S(1)}, bf16[1,2,128,128]{3,2,1,0:T(8,128)(2,1)S(1)}, u32[]{:S(2)}, u32[]{:S(2)}) collective-permute-start(bf16[1,2,128,128]{3,2,1,0:T(8,128)(2,1)S(1)} %bitcast.581), channel_id=1, source_target_pairs={{4,0},{8,4},{12,8},{16,12},{20,16},{24,20},{28,24},{32,28},{36,32}... | collective-permute-start | bytes 196616 | tf_op jit(solution)/shard_map/ppermute | solution.py:17
  17.4 9.1 %collective-permute-start.1 = (f32[1,2,3,128]{3,2,1,0:T(4,128)S(1)}, f32[1,2,3,128]{3,2,1,0:T(4,128)S(1)}, u32[]{:S(2)}, u32[]{:S(2)}) collective-permute-start(f32[1,2,3,128]{3,2,1,0:T(4,128)S(1)} %get-tuple-element.372), channel_id=1, source_target_pairs={{4,0},{8,4},{12,8},{16,12},{20,16},{24,20},{28,24},{32,28},{36,32}... | collective-permute-start | bytes 9224 | tf_op jit(solution)/shard_map/ppermute | solution.py:17
  28.7 5.2 %collective-permute-start.2 = (f32[4,1,3,128]{3,2,1,0:T(4,128)S(1)}, f32[4,1,3,128]{3,2,1,0:T(4,128)S(1)}, u32[]{:S(2)}, u32[]{:S(2)}) collective-permute-start(f32[4,1,3,128]{3,2,1,0:T(4,128)S(1)} %get-tuple-element.368), channel_id=1, source_target_pairs={{0,1},{1,2},{2,3},{4,5},{5,6},{6,7},{8,9},{9,10},{10,11},{12,13},{... | collective-permute-start | bytes 18440 | tf_op jit(solution)/shard_map/ppermute | solution.py:14
  43.5 3.8 %collective-permute-done.7 = bf16[4,1,128,128]{3,2,1,0:T(8,128)(2,1)S(1)} collective-permute-done((bf16[4,1,128,128]{3,2,1,0:T(8,128)(2,1)S(1)}, bf16[4,1,128,128]{3,2,1,0:T(8,128)(2,1)S(1)}, u32[]{:S(2)}, u32[]{:S(2)}) %collective-permute-start.7) | collective-permute-done | bytes 131104 | tf_op jit(solution)/shard_map/ppermute | solution.py:17
  48.2 35.6 %while.30 = (s32[]{:T(128)}, bf16[4,128,128]{2,1,0:T(8,128)(2,1)S(1)}, s32[4,16,128]{2,1,0:T(8,128)S(1)}, f32[4,3,128]{2,1,0:T(4,128)S(1)}, f32[4,3,1152]{2,1,0:...) while((s32[]{:T(128)}, ...), condition=%wide.region_4.5_spmd, body=%wide.region_2.4_spmd.sunk | while | flops 1259732992 | bytes 6868633 | solution.py:104
  48.3 4.3 %fusion.253 = f32[3,2048]{1,0:T(4,128)S(1)} fusion(s32[2048]{0:T(1024)S(1)} %bitcast.565, f32[4,3,1152]{2,1,0:T(4,128)S(1)} %get-tuple-element.705, s32[]{:T(128)} %get-tuple-element.688), kind=kOutput, calls=%fused_computation.2.clone.1 | convolution fusion | flops 87293952 | bytes 51204 | tf_op jit(solution)/shard_map/while/body/eval_jaxpr/dot_general | solution.py:70
  57.2 4.3 %fusion.253 = f32[3,2048]{1,0:T(4,128)S(1)} fusion(s32[2048]{0:T(1024)S(1)} %bitcast.565, f32[4,3,1152]{2,1,0:T(4,128)S(1)} %get-tuple-element.705, s32[]{:T(128)} %get-tuple-element.688), kind=kOutput, calls=%fused_computation.2.clone.1 | convolution fusion | flops 87293952 | bytes 51204 | tf_op jit(solution)/shard_map/while/body/eval_jaxpr/dot_general | solution.py:70
  66.1 4.3 %fusion.253 = f32[3,2048]{1,0:T(4,128)S(1)} fusion(s32[2048]{0:T(1024)S(1)} %bitcast.565, f32[4,3,1152]{2,1,0:T(4,128)S(1)} %get-tuple-element.705, s32[]{:T(128)} %get-tuple-element.688), kind=kOutput, calls=%fused_computation.2.clone.1 | convolution fusion | flops 87293952 | bytes 51204 | tf_op jit(solution)/shard_map/while/body/eval_jaxpr/dot_general | solution.py:70
  75.0 4.3 %fusion.253 = f32[3,2048]{1,0:T(4,128)S(1)} fusion(s32[2048]{0:T(1024)S(1)} %bitcast.565, f32[4,3,1152]{2,1,0:T(4,128)S(1)} %get-tuple-element.705, s32[]{:T(128)} %get-tuple-element.688), kind=kOutput, calls=%fused_computation.2.clone.1 | convolution fusion | flops 87293952 | bytes 51204 | tf_op jit(solution)/shard_map/while/body/eval_jaxpr/dot_general | solution.py:70
  88.3 9.1 %collective-permute-start.9 = (bf16[1,2,128,128]{3,2,1,0:T(8,128)(2,1)S(1)}, bf16[1,2,128,128]{3,2,1,0:T(8,128)(2,1)S(1)}, u32[]{:S(2)}, u32[]{:S(2)}) collective-permute-start(bf16[1,2,128,128]{3,2,1,0:T(8,128)(2,1)S(1)} %bitcast.583), channel_id=1, source_target_pairs={{4,0},{8,4},{12,8},{16,12},{20,16},{24,20},{28,24},{32,28},{36,32}... | collective-permute-start | bytes 196616 | tf_op jit(solution)/shard_map/ppermute | solution.py:17
  104.0 4.0 %collective-permute-done.11 = bf16[4,1,128,128]{3,2,1,0:T(8,128)(2,1)S(1)} collective-permute-done((bf16[4,1,128,128]{3,2,1,0:T(8,128)(2,1)S(1)}, bf16[4,1,128,128]{3,2,1,0:T(8,128)(2,1)S(1)}, u32[]{:S(2)}, u32[]{:S(2)}) %collective-permute-start.11) | collective-permute-done | bytes 131104 | tf_op jit(solution)/shard_map/ppermute | solution.py:17
  108.4 35.6 %while.31 = (s32[]{:T(128)}, bf16[4,128,128]{2,1,0:T(8,128)(2,1)S(1)}, s32[4,16,128]{2,1,0:T(8,128)S(1)}, f32[4,3,128]{2,1,0:T(4,128)S(1)}, f32[4,3,1152]{2,1,0:...) while((s32[]{:T(128)}, ...), condition=%wide.region_9.10_spmd, body=%wide.region_7.9_spmd.sunk | while | flops 1259732992 | bytes 6868633 | solution.py:104
  108.4 4.3 %fusion.269 = f32[3,2048]{1,0:T(4,128)S(1)} fusion(s32[2048]{0:T(1024)S(1)} %bitcast.567, f32[4,3,1152]{2,1,0:T(4,128)S(1)} %get-tuple-element.744, s32[]{:T(128)} %get-tuple-element.727), kind=kOutput, calls=%fused_computation.36.clone.1 | convolution fusion | flops 87293952 | bytes 51204 | tf_op jit(solution)/shard_map/while/body/eval_jaxpr/dot_general | solution.py:70
  117.3 4.3 %fusion.269 = f32[3,2048]{1,0:T(4,128)S(1)} fusion(s32[2048]{0:T(1024)S(1)} %bitcast.567, f32[4,3,1152]{2,1,0:T(4,128)S(1)} %get-tuple-element.744, s32[]{:T(128)} %get-tuple-element.727), kind=kOutput, calls=%fused_computation.36.clone.1 | convolution fusion | flops 87293952 | bytes 51204 | tf_op jit(solution)/shard_map/while/body/eval_jaxpr/dot_general | solution.py:70
  126.2 4.3 %fusion.269 = f32[3,2048]{1,0:T(4,128)S(1)} fusion(s32[2048]{0:T(1024)S(1)} %bitcast.567, f32[4,3,1152]{2,1,0:T(4,128)S(1)} %get-tuple-element.744, s32[]{:T(128)} %get-tuple-element.727), kind=kOutput, calls=%fused_computation.36.clone.1 | convolution fusion | flops 87293952 | bytes 51204 | tf_op jit(solution)/shard_map/while/body/eval_jaxpr/dot_general | solution.py:70
  135.1 4.3 %fusion.269 = f32[3,2048]{1,0:T(4,128)S(1)} fusion(s32[2048]{0:T(1024)S(1)} %bitcast.567, f32[4,3,1152]{2,1,0:T(4,128)S(1)} %get-tuple-element.744, s32[]{:T(128)} %get-tuple-element.727), kind=kOutput, calls=%fused_computation.36.clone.1 | convolution fusion | flops 87293952 | bytes 51204 | tf_op jit(solution)/shard_map/while/body/eval_jaxpr/dot_general | solution.py:70
  146.9 9.1 %collective-permute-start.13 = (bf16[1,2,128,128]{3,2,1,0:T(8,128)(2,1)S(1)}, bf16[1,2,128,128]{3,2,1,0:T(8,128)(2,1)S(1)}, u32[]{:S(2)}, u32[]{:S(2)}) collective-permute-start(bf16[1,2,128,128]{3,2,1,0:T(8,128)(2,1)S(1)} %bitcast.584), channel_id=1, source_target_pairs={{4,0},{8,4},{12,8},{16,12},{20,16},{24,20},{28,24},{32,28},{36,32}... | collective-permute-start | bytes 196616 | tf_op jit(solution)/shard_map/ppermute | solution.py:17
  157.3 3.2 %collective-permute-start.14 = (bf16[4,1,128,128]{3,2,1,0:T(8,128)(2,1)S(1)}, bf16[4,1,128,128]{3,2,1,0:T(8,128)(2,1)S(1)}, u32[]{:S(2)}, u32[]{:S(2)}) collective-permute-start(bf16[4,1,128,128]{3,2,1,0:T(8,128)(2,1)S(1)} %get-tuple-element.349), channel_id=1, source_target_pairs={{0,1},{1,2},{2,3},{4,5},{5,6},{6,7},{8,9},{9,10},{10,11},{12,13},{... | collective-permute-start | bytes 393224 | tf_op jit(solution)/shard_map/ppermute | solution.py:14
  162.9 4.0 %collective-permute-done.15 = bf16[4,1,128,128]{3,2,1,0:T(8,128)(2,1)S(1)} collective-permute-done((bf16[4,1,128,128]{3,2,1,0:T(8,128)(2,1)S(1)}, bf16[4,1,128,128]{3,2,1,0:T(8,128)(2,1)S(1)}, u32[]{:S(2)}, u32[]{:S(2)}) %collective-permute-start.15) | collective-permute-done | bytes 131104 | tf_op jit(solution)/shard_map/ppermute | solution.py:17
  167.3 35.3 %while.32 = (s32[]{:T(128)}, bf16[4,128,128]{2,1,0:T(8,128)(2,1)S(1)}, s32[4,16,128]{2,1,0:T(8,128)S(1)}, f32[4,3,128]{2,1,0:T(4,128)S(1)}, f32[4,3,1152]{2,1,0:...) while((s32[]{:T(128)}, ...), condition=%wide.region_14.15_spmd, body=%wide.region_12.14_spmd.sunk | while | flops 1259732992 | bytes 6868633 | solution.py:104
  167.4 4.3 %fusion.285 = f32[3,2048]{1,0:T(4,128)S(1)} fusion(s32[2048]{0:T(1024)S(1)} %bitcast.569, f32[4,3,1152]{2,1,0:T(4,128)S(1)} %get-tuple-element.783, s32[]{:T(128)} %get-tuple-element.766), kind=kOutput, calls=%fused_computation.70.clone.1 | convolution fusion | flops 87293952 | bytes 51204 | tf_op jit(solution)/shard_map/while/body/eval_jaxpr/dot_general | solution.py:70
  176.2 4.3 %fusion.285 = f32[3,2048]{1,0:T(4,128)S(1)} fusion(s32[2048]{0:T(1024)S(1)} %bitcast.569, f32[4,3,1152]{2,1,0:T(4,128)S(1)} %get-tuple-element.783, s32[]{:T(128)} %get-tuple-element.766), kind=kOutput, calls=%fused_computation.70.clone.1 | convolution fusion | flops 87293952 | bytes 51204 | tf_op jit(solution)/shard_map/while/body/eval_jaxpr/dot_general | solution.py:70
  185.0 4.3 %fusion.285 = f32[3,2048]{1,0:T(4,128)S(1)} fusion(s32[2048]{0:T(1024)S(1)} %bitcast.569, f32[4,3,1152]{2,1,0:T(4,128)S(1)} %get-tuple-element.783, s32[]{:T(128)} %get-tuple-element.766), kind=kOutput, calls=%fused_computation.70.clone.1 | convolution fusion | flops 87293952 | bytes 51204 | tf_op jit(solution)/shard_map/while/body/eval_jaxpr/dot_general | solution.py:70
  193.8 4.3 %fusion.285 = f32[3,2048]{1,0:T(4,128)S(1)} fusion(s32[2048]{0:T(1024)S(1)} %bitcast.569, f32[4,3,1152]{2,1,0:T(4,128)S(1)} %get-tuple-element.783, s32[]{:T(128)} %get-tuple-element.766), kind=kOutput, calls=%fused_computation.70.clone.1 | convolution fusion | flops 87293952 | bytes 51204 | tf_op jit(solution)/shard_map/while/body/eval_jaxpr/dot_general | solution.py:70
  (314 shorter events, 94.6 us)
Async XLA Ops:
  0.7 27.8 %copy-start.3 = (bf16[3,128,512]{2,1,0:T(8,128)(2,1)S(1)}, bf16[3,128,512]{2,1,0:T(8,128)(2,1)}, u32[]{:S(2)}) copy-start(bf16[3,128,512]{2,1,0:T(8,128)(2,1)} %param.30) | copy-start | bytes 1179652
  0.7 27.8 %copy-start.2 = (bf16[3,128,512]{2,1,0:T(8,128)(2,1)S(1)}, bf16[3,128,512]{2,1,0:T(8,128)(2,1)}, u32[]{:S(2)}) copy-start(bf16[3,128,512]{2,1,0:T(8,128)(2,1)} %param.31) | copy-start | bytes 1179652
  1.8 34.1 %copy-start.7 = (s32[2,2,16,128]{3,2,1,0:T(8,128)S(1)}, s32[2,2,16,128]{3,2,1,0:T(8,128)}, u32[]{:S(2)}) copy-start(s32[2,2,16,128]{3,2,1,0:T(8,128)} %param.26) | copy-start | bytes 98308
  2.6 36.4 %collective-permute-start.4 = (bf16[1,2,128,128]{3,2,1,0:T(8,128)(2,1)S(1)}, bf16[1,2,128,128]{3,2,1,0:T(8,128)(2,1)S(1)}, u32[]{:S(2)}, u32[]{:S(2)}) collective-permute-start(bf16[1,2,128,128]{3,2,1,0:T(8,128)(2,1)S(1)} %bitcast.582), channel_id=1, source_target_pairs={{0,4},{4,8},{8,12},{12,16},{16,20},{20,24},{24,28},{28,32},{32,36}... | collective-permute-start | bytes 196616 | tf_op jit(solution)/shard_map/ppermute | solution.py:14
  5.7 33.3 %collective-permute-start.5 = (bf16[1,2,128,128]{3,2,1,0:T(8,128)(2,1)S(1)}, bf16[1,2,128,128]{3,2,1,0:T(8,128)(2,1)S(1)}, u32[]{:S(2)}, u32[]{:S(2)}) collective-permute-start(bf16[1,2,128,128]{3,2,1,0:T(8,128)(2,1)S(1)} %bitcast.581), channel_id=1, source_target_pairs={{4,0},{8,4},{12,8},{16,12},{20,16},{24,20},{28,24},{32,28},{36,32}... | collective-permute-start | bytes 196616 | tf_op jit(solution)/shard_map/ppermute | solution.py:17
  15.4 13.2 %collective-permute-start = (f32[1,2,3,128]{3,2,1,0:T(4,128)S(1)}, f32[1,2,3,128]{3,2,1,0:T(4,128)S(1)}, u32[]{:S(2)}, u32[]{:S(2)}) collective-permute-start(f32[1,2,3,128]{3,2,1,0:T(4,128)S(1)} %get-tuple-element.371), channel_id=1, source_target_pairs={{0,4},{4,8},{8,12},{12,16},{16,20},{20,24},{24,28},{28,32},{32,36}... | collective-permute-start | bytes 9224 | tf_op jit(solution)/shard_map/ppermute | solution.py:14
  17.4 11.3 %collective-permute-start.1 = (f32[1,2,3,128]{3,2,1,0:T(4,128)S(1)}, f32[1,2,3,128]{3,2,1,0:T(4,128)S(1)}, u32[]{:S(2)}, u32[]{:S(2)}) collective-permute-start(f32[1,2,3,128]{3,2,1,0:T(4,128)S(1)} %get-tuple-element.372), channel_id=1, source_target_pairs={{4,0},{8,4},{12,8},{16,12},{20,16},{24,20},{28,24},{32,28},{36,32}... | collective-permute-start | bytes 9224 | tf_op jit(solution)/shard_map/ppermute | solution.py:17
  28.7 7.2 %collective-permute-start.2 = (f32[4,1,3,128]{3,2,1,0:T(4,128)S(1)}, f32[4,1,3,128]{3,2,1,0:T(4,128)S(1)}, u32[]{:S(2)}, u32[]{:S(2)}) collective-permute-start(f32[4,1,3,128]{3,2,1,0:T(4,128)S(1)} %get-tuple-element.368), channel_id=1, source_target_pairs={{0,1},{1,2},{2,3},{4,5},{5,6},{6,7},{8,9},{9,10},{10,11},{12,13},{... | collective-permute-start | bytes 18440 | tf_op jit(solution)/shard_map/ppermute | solution.py:14
  33.9 5.0 %collective-permute-start.3 = (f32[4,1,3,128]{3,2,1,0:T(4,128)S(1)}, f32[4,1,3,128]{3,2,1,0:T(4,128)S(1)}, u32[]{:S(2)}, u32[]{:S(2)}) collective-permute-start(f32[4,1,3,128]{3,2,1,0:T(4,128)S(1)} %get-tuple-element.367), channel_id=1, source_target_pairs={{1,0},{2,1},{3,2},{5,4},{6,5},{7,6},{9,8},{10,9},{11,10},{13,12},{... | collective-permute-start | bytes 18440 | tf_op jit(solution)/shard_map/ppermute | solution.py:17
  39.1 4.4 %collective-permute-start.6 = (bf16[4,1,128,128]{3,2,1,0:T(8,128)(2,1)S(1)}, bf16[4,1,128,128]{3,2,1,0:T(8,128)(2,1)S(1)}, u32[]{:S(2)}, u32[]{:S(2)}) collective-permute-start(bf16[4,1,128,128]{3,2,1,0:T(8,128)(2,1)S(1)} %get-tuple-element.357), channel_id=1, source_target_pairs={{0,1},{1,2},{2,3},{4,5},{5,6},{6,7},{8,9},{9,10},{10,11},{12,13},{... | collective-permute-start | bytes 393224 | tf_op jit(solution)/shard_map/ppermute | solution.py:14
  41.1 6.3 %collective-permute-start.7 = (bf16[4,1,128,128]{3,2,1,0:T(8,128)(2,1)S(1)}, bf16[4,1,128,128]{3,2,1,0:T(8,128)(2,1)S(1)}, u32[]{:S(2)}, u32[]{:S(2)}) collective-permute-start(bf16[4,1,128,128]{3,2,1,0:T(8,128)(2,1)S(1)} %get-tuple-element.356), channel_id=1, source_target_pairs={{1,0},{2,1},{3,2},{5,4},{6,5},{7,6},{9,8},{10,9},{11,10},{13,12},{... | collective-permute-start | bytes 393224 | tf_op jit(solution)/shard_map/ppermute | solution.py:17
  86.4 11.0 %collective-permute-start.8 = (bf16[1,2,128,128]{3,2,1,0:T(8,128)(2,1)S(1)}, bf16[1,2,128,128]{3,2,1,0:T(8,128)(2,1)S(1)}, u32[]{:S(2)}, u32[]{:S(2)}) collective-permute-start(bf16[1,2,128,128]{3,2,1,0:T(8,128)(2,1)S(1)} %bitcast.585), channel_id=1, source_target_pairs={{0,4},{4,8},{8,12},{12,16},{16,20},{20,24},{24,28},{28,32},{32,36}... | collective-permute-start | bytes 196616 | tf_op jit(solution)/shard_map/ppermute | solution.py:14
  88.3 10.4 %collective-permute-start.9 = (bf16[1,2,128,128]{3,2,1,0:T(8,128)(2,1)S(1)}, bf16[1,2,128,128]{3,2,1,0:T(8,128)(2,1)S(1)}, u32[]{:S(2)}, u32[]{:S(2)}) collective-permute-start(bf16[1,2,128,128]{3,2,1,0:T(8,128)(2,1)S(1)} %bitcast.583), channel_id=1, source_target_pairs={{4,0},{8,4},{12,8},{16,12},{20,16},{24,20},{28,24},{32,28},{36,32}... | collective-permute-start | bytes 196616 | tf_op jit(solution)/shard_map/ppermute | solution.py:17
  98.8 5.2 %collective-permute-start.10 = (bf16[4,1,128,128]{3,2,1,0:T(8,128)(2,1)S(1)}, bf16[4,1,128,128]{3,2,1,0:T(8,128)(2,1)S(1)}, u32[]{:S(2)}, u32[]{:S(2)}) collective-permute-start(bf16[4,1,128,128]{3,2,1,0:T(8,128)(2,1)S(1)} %get-tuple-element.353), channel_id=1, source_target_pairs={{0,1},{1,2},{2,3},{4,5},{5,6},{6,7},{8,9},{9,10},{10,11},{12,13},{... | collective-permute-start | bytes 393224 | tf_op jit(solution)/shard_map/ppermute | solution.py:14
  101.7 6.3 %collective-permute-start.11 = (bf16[4,1,128,128]{3,2,1,0:T(8,128)(2,1)S(1)}, bf16[4,1,128,128]{3,2,1,0:T(8,128)(2,1)S(1)}, u32[]{:S(2)}, u32[]{:S(2)}) collective-permute-start(bf16[4,1,128,128]{3,2,1,0:T(8,128)(2,1)S(1)} %get-tuple-element.352), channel_id=1, source_target_pairs={{1,0},{2,1},{3,2},{5,4},{6,5},{7,6},{9,8},{10,9},{11,10},{13,12},{... | collective-permute-start | bytes 393224 | tf_op jit(solution)/shard_map/ppermute | solution.py:17
  108.4 35.6 %copy-start.6 = (bf16[3,128,128]{2,1,0:T(8,128)(2,1)S(1)}, bf16[3,128,128]{2,1,0:T(8,128)(2,1)}, u32[]{:S(2)}) copy-start(bf16[3,128,128]{2,1,0:T(8,128)(2,1)} %param.35) | copy-start | bytes 294916
  108.4 47.6 %copy-start.11 = (s32[2,2]{1,0:T(2,128)S(1)}, s32[2,2]{1,0:T(2,128)}, u32[]{:S(2)}) copy-start(s32[2,2]{1,0:T(2,128)} %param.25) | copy-start | bytes 52
  144.9 11.1 %collective-permute-start.12 = (bf16[1,2,128,128]{3,2,1,0:T(8,128)(2,1)S(1)}, bf16[1,2,128,128]{3,2,1,0:T(8,128)(2,1)S(1)}, u32[]{:S(2)}, u32[]{:S(2)}) collective-permute-start(bf16[1,2,128,128]{3,2,1,0:T(8,128)(2,1)S(1)} %bitcast.586), channel_id=1, source_target_pairs={{0,4},{4,8},{8,12},{12,16},{16,20},{20,24},{24,28},{28,32},{32,36}... | collective-permute-start | bytes 196616 | tf_op jit(solution)/shard_map/ppermute | solution.py:14
  146.9 10.4 %collective-permute-start.13 = (bf16[1,2,128,128]{3,2,1,0:T(8,128)(2,1)S(1)}, bf16[1,2,128,128]{3,2,1,0:T(8,128)(2,1)S(1)}, u32[]{:S(2)}, u32[]{:S(2)}) collective-permute-start(bf16[1,2,128,128]{3,2,1,0:T(8,128)(2,1)S(1)} %bitcast.584), channel_id=1, source_target_pairs={{4,0},{8,4},{12,8},{16,12},{20,16},{24,20},{28,24},{32,28},{36,32}... | collective-permute-start | bytes 196616 | tf_op jit(solution)/shard_map/ppermute | solution.py:17
  157.3 5.6 %collective-permute-start.14 = (bf16[4,1,128,128]{3,2,1,0:T(8,128)(2,1)S(1)}, bf16[4,1,128,128]{3,2,1,0:T(8,128)(2,1)S(1)}, u32[]{:S(2)}, u32[]{:S(2)}) collective-permute-start(bf16[4,1,128,128]{3,2,1,0:T(8,128)(2,1)S(1)} %get-tuple-element.349), channel_id=1, source_target_pairs={{0,1},{1,2},{2,3},{4,5},{5,6},{6,7},{8,9},{9,10},{10,11},{12,13},{... | collective-permute-start | bytes 393224 | tf_op jit(solution)/shard_map/ppermute | solution.py:14
  160.6 6.3 %collective-permute-start.15 = (bf16[4,1,128,128]{3,2,1,0:T(8,128)(2,1)S(1)}, bf16[4,1,128,128]{3,2,1,0:T(8,128)(2,1)S(1)}, u32[]{:S(2)}, u32[]{:S(2)}) collective-permute-start(bf16[4,1,128,128]{3,2,1,0:T(8,128)(2,1)S(1)} %get-tuple-element.348), channel_id=1, source_target_pairs={{1,0},{2,1},{3,2},{5,4},{6,5},{7,6},{9,8},{10,9},{11,10},{13,12},{... | collective-permute-start | bytes 393224 | tf_op jit(solution)/shard_map/ppermute | solution.py:17
  167.3 36.1 %copy-start.8 = (bf16[128,128]{1,0:T(8,128)(2,1)S(1)}, bf16[128,128]{1,0:T(8,128)(2,1)}, u32[]{:S(2)}) copy-start(bf16[128,128]{1,0:T(8,128)(2,1)} %param.36) | copy-start | bytes 98308
  167.3 36.1 %copy-start.13 = (bf16[128,2]{0,1:T(2,128)(2,1)S(1)}, bf16[128,2]{0,1:T(2,128)(2,1)}, u32[]{:S(2)}) copy-start(bf16[128,2]{0,1:T(2,128)(2,1)} %param.37) | copy-start | bytes 1540
  167.3 36.5 %copy-start.12 = (f32[2,2,2,128]{3,2,1,0:T(2,128)S(1)}, f32[2,2,2,128]{3,2,1,0:T(2,128)}, u32[]{:S(2)}) copy-start(f32[2,2,2,128]{3,2,1,0:T(2,128)} %param.24) | copy-start | bytes 12292
  (6 other events, 99.0 us)
where the time goes:
time: 205 us; the launch traced here: 204 us
  matrix products  108 us (53%)
  starting transfers between devices  66.3 us (32%)
  waiting for transfers between devices  17.3 us (8%)
  other arithmetic  5.42 us (3%)
  local copies, waits for them, and re-layouts  4.52 us (2%)
    dot_general x12, matrix products, one_bin(): lax.dot_general(geo_win, selector.astype(jnp.float32), (((1,), (1,)), (()...  51.2 us
    ppermute x8, starting transfers between devices, extended(): lax.ppermute(lax.slice_in_dim(block, 0, width, axis=dim), axis, backward)  44.1 us
    dot_general x12, matrix products, one_bin(): jnp.dot(selector, lat_win, preferred_element_type=jnp.float32)  23.5 us
    ppermute x8, starting transfers between devices, extended(): lax.ppermute(lax.slice_in_dim(block, block.shape[dim] - width, None, axis...  22.2 us
    dot_general x12, matrix products, one_bin(): jnp.dot(sender_lat, send_weight, preferred_element_type=jnp.float32)  18.5 us
    ppermute x8, waiting for transfers between devices, extended(): lax.ppermute(lax.slice_in_dim(block, 0, width, axis=dim), axis, backward)  17.3 us
    dot_general x12, matrix products, one_bin(): jnp.dot(hidden.reshape(knb * slot_count, -1), out_weight, preferred_eleme...  8.58 us
  transfers between devices with their start and end apart: 16, of which 6 were waited for; matrix products, arithmetic and copies ran while one was open for 2% of the time, Pallas kernels for 0%

commit v1 on v0

v1 whole, which is shorter than its diff:
```python
import functools

import jax
import jax.numpy as jnp
from jax import lax
from jax.experimental import pallas as pl
from jax.experimental.pallas import tpu as pltpu
from jax.sharding import PartitionSpec as P

time_step = 0.5
LAT = 128
EH = 512
KNB = 16
SLOTS = 128
PACK = 48
GEO = 16
BLOCKED = -(2.0**40)
bf16 = jnp.bfloat16
f32 = jnp.float32


def tdot(left, right):
    return lax.dot_general(left, right, (((0,), (0,)), ((), ())), preferred_element_type=f32)


def split(values):
    high = values.astype(bf16)
    low = (values - high.astype(f32)).astype(bf16)
    return high, low


def split3(values):
    high = values.astype(bf16)
    rest = values - high.astype(f32)
    mid = rest.astype(bf16)
    low = (rest - mid.astype(f32)).astype(bf16)
    return high, mid, low


def norm_rows(values):
    center = values - jnp.mean(values, axis=0, keepdims=True)
    spread = jnp.mean(center * center, axis=0, keepdims=True)
    return center * lax.rsqrt(spread + 1e-05)


def place(own, low, high, left, right, win, depth):
    for i in range(4):
        win[i, 0] = left[i, 0]
        win[i, 3] = right[i, 0]
        for j in range(2):
            if i == 0:
                win[i, j + 1] = low[0, j]
            elif i == 3:
                win[i, j + 1] = high[0, j]
            else:
                win[i, j + 1] = own[i - 1, j]


def one_hot(codes, pair):
    row = jnp.concatenate([codes[2 * pair : 2 * pair + 1], codes[2 * pair + 1 : 2 * pair + 2]], axis=1)
    window = row >> 7
    slot = row & (SLOTS - 1)
    iota = lax.broadcasted_iota(jnp.int32, (SLOTS, 2 * SLOTS), 0).astype(jnp.int16)
    parts = []
    for w in range(9):
        wanted = jnp.where(window == w, slot, -1).astype(jnp.int16)
        hit = iota == jnp.broadcast_to(wanted, (SLOTS, 2 * SLOTS))
        parts.append(jnp.where(hit, jnp.ones((), bf16), jnp.zeros((), bf16)))
    return jnp.concatenate(parts, axis=0)


def step_kernel(first, last, *refs):
    refs = list(refs)
    own, low, high, left, right = [refs.pop(0) for _ in range(5)]
    codes_ref = refs.pop(0)
    if first:
        mask_ref, position = refs.pop(0), refs.pop(0)
        enc_first, enc_second = refs.pop(0), refs.pop(0)
    else:
        geo_in = refs.pop(0)
    recv_w, send_w, geo_w, out_w, first_w, second_w = [refs.pop(0) for _ in range(6)]
    if last:
        occupancy, position, velocity, dec_first, dec_second = [refs.pop(0) for _ in range(5)]
        out_velocity, out_position = refs.pop(0), refs.pop(0)
    else:
        out_latent = refs.pop(0)
    if first:
        geo_out = refs.pop(0)
        pack = refs.pop(0)
    win, full_w, recv_all, sums = refs
    if first:
        place(own, low, high, left, right, pack, PACK)
        weight = jnp.concatenate([enc_first[...], jnp.zeros((PACK - 30, LAT), bf16)], axis=0)
        for i in range(4):
            raw = jnp.concatenate([pack[i, j] for j in range(4)], axis=1)
            hidden = jnp.maximum(tdot(weight, raw), 0.0).astype(bf16)
            latent = norm_rows(tdot(enc_second[...], hidden)).astype(bf16)
            for j in range(4):
                win[i, j] = latent[:, j * SLOTS : (j + 1) * SLOTS]
    else:
        place(own, low, high, left, right, win, LAT)
    own_all = jnp.concatenate([win[1 + b // 2, 1 + b % 2] for b in range(4)], axis=1)
    recv_all[...] = -tdot(recv_w[...], own_all)
    geo_high, geo_low = split(geo_w[...])
    rows = []
    for c in range(3):
        rows += [geo_high[c : c + 1], geo_high[c : c + 1], geo_low[c : c + 1], geo_low[c : c + 1]]
    rows.append(jnp.full((1, EH), BLOCKED, bf16))
    rows.append(jnp.zeros((GEO - 13, EH), bf16))
    full_w[pl.ds(0, LAT), :] = send_w[...]
    full_w[pl.ds(LAT, GEO), :] = jnp.concatenate(rows, axis=0)

    for b in range(4):
        a, c = b // 2, b % 2
        codes = codes_ref[a, c]
        window_lat = jnp.concatenate([win[a + w // 3, c + w % 3] for w in range(9)], axis=1)
        if first:
            window_geo = jnp.concatenate([pack[a + w // 3, c + w % 3, 32:48, :] for w in range(9)], axis=1)
            window_lat = jnp.concatenate([window_lat, window_geo], axis=0)
        bound = recv_all[:, b * SLOTS : (b + 1) * SLOTS]
        total = None
        for pair in range(KNB // 2):
            hot = one_hot(codes, pair)
            sender = jnp.dot(window_lat, hot, preferred_element_type=f32)
            if first:
                got = sender[LAT:]
                other_x = got[0:1] + got[1:2] + got[2:3]
                other_y = got[3:4] + got[4:5] + got[5:6]
                own_x = position[a, c, 0:1]
                own_y = position[a, c, 1:2]
                own_live = pack[a + 1, c + 1, 38:39, :].astype(f32)
                twice = lambda v: jnp.concatenate([v, v], axis=1)
                delta_x = other_x - twice(own_x)
                delta_y = other_y - twice(own_y)
                distance = delta_x * delta_x + delta_y * delta_y
                mask = jnp.concatenate([mask_ref[a, c, 2 * pair : 2 * pair + 1], mask_ref[a, c, 2 * pair + 1 : 2 * pair + 2]], axis=1)
                valid = mask.astype(f32) * twice(own_live) * got[6:7]
                pieces = []
                for v in (delta_x, delta_y, distance):
                    v_high = v.astype(bf16).astype(f32)
                    v_low = v - v_high
                    pieces += [v_high, v_low, v_high, v_low]
                pieces.append(1.0 - valid)
                pieces.append(jnp.zeros((GEO - 13, 2 * SLOTS), f32))
                geo = jnp.concatenate(pieces, axis=0).astype(bf16)
                geo_out[b, :, pair * 2 * SLOTS : (pair + 1) * 2 * SLOTS] = geo
                sender = sender[:LAT]
            else:
                geo = geo_in[b, :, pair * 2 * SLOTS : (pair + 1) * 2 * SLOTS]
            right_side = jnp.concatenate([sender.astype(bf16), geo], axis=0)
            hidden = tdot(full_w[...], right_side)
            part = jnp.maximum(hidden[:, :SLOTS], bound) + jnp.maximum(hidden[:, SLOTS:], bound)
            total = part if total is None else total + part
        sums[:, b * SLOTS : (b + 1) * SLOTS] = (total - KNB * bound).astype(bf16)

    summed = tdot(out_w[...], sums[...]).astype(bf16)
    joined = tdot(first_w[...], jnp.concatenate([own_all, summed], axis=0))
    joined = jnp.maximum(joined, 0.0).astype(bf16)
    update = norm_rows(tdot(second_w[...], joined))
    latent = (own_all.astype(f32) + update).astype(bf16)
    if not last:
        for b in range(4):
            out_latent[b // 2, b % 2] = latent[:, b * SLOTS : (b + 1) * SLOTS]
    else:
        hidden = jnp.maximum(tdot(dec_first[...], latent), 0.0).astype(bf16)
        accel = tdot(dec_second[...], hidden)
        lane = lax.broadcasted_iota(jnp.int32, (2, SLOTS), 1)
        for b in range(4):
            a, c = b // 2, b % 2
            live = (lane < occupancy[a, c]).astype(f32)
            speed = velocity[a, c] + time_step * (accel[:, b * SLOTS : (b + 1) * SLOTS] * live)
            out_velocity[a, c] = speed
            out_position[a, c] = position[a, c] + time_step * speed


def shifted(count, by):
    return [(i, i + by) for i in range(count) if 0 <= i + by < count]


def exchange(block):
    slabs, cross = lax.axis_size("slab"), lax.axis_size("cross")
    low = lax.ppermute(block[1:], "slab", shifted(slabs, 1))
    high = lax.ppermute(block[:1], "slab", shifted(slabs, -1))
    first = jnp.concatenate([low[:, :1], block[:, :1], high[:, :1]], axis=0)
    second = jnp.concatenate([low[:, 1:], block[:, 1:], high[:, 1:]], axis=0)
    left = lax.ppermute(second, "cross", shifted(cross, 1))
    right = lax.ppermute(first, "cross", shifted(cross, -1))
    return block, low, high, left, right


def call(first, last, *operands):
    vmem = pl.BlockSpec(memory_space=pltpu.VMEM)
    specs = [vmem] * len(operands)
    if last:
        specs[-5] = pl.BlockSpec(memory_space=pltpu.SMEM)
        out = [jax.ShapeDtypeStruct((2, 2, 2, SLOTS), f32)] * 2
    else:
        out = [jax.ShapeDtypeStruct((2, 2, LAT, SLOTS), bf16)]
    scratch = [
        pltpu.VMEM((4, 4, LAT, SLOTS), bf16),
        pltpu.VMEM((LAT + GEO, EH), bf16),
        pltpu.VMEM((EH, 4 * SLOTS), f32),
        pltpu.VMEM((EH, 4 * SLOTS), bf16),
    ]
    if first:
        out.append(jax.ShapeDtypeStruct((4, GEO, KNB * SLOTS), bf16))
        scratch.insert(0, pltpu.VMEM((4, 4, PACK, SLOTS), bf16))
    return pl.pallas_call(
        functools.partial(step_kernel, first, last),
        out_shape=out,
        in_specs=specs,
        out_specs=[vmem] * len(out),
        scratch_shapes=scratch,
        compiler_params=pltpu.CompilerParams(vmem_limit_bytes=48 << 20),
        name="first_step" if first else "last_step" if last else "middle_step",
    )(*operands)


def shards(
    features,
    position,
    velocity,
    occupancy,
    neighbor_codes,
    edge_mask,
    enc_first,
    enc_second,
    edge_recv,
    edge_send,
    edge_geo,
    edge_out,
    node_first,
    node_second,
    dec_first,
    dec_second,
):
    size_x, size_y = position.shape[:2]
    slot_index = lax.broadcasted_iota(jnp.int32, (size_x, size_y, 1, SLOTS), 3)
    live = (slot_index < occupancy[:, :, None, None]).astype(bf16)
    xs = split3(position[:, :, 0:1])
    ys = split3(position[:, :, 1:2])
    blank = jnp.zeros((size_x, size_y, 2, SLOTS), bf16)
    tail = jnp.zeros((size_x, size_y, PACK - 39, SLOTS), bf16)
    raw = jnp.concatenate([features, blank, *xs, *ys, live, tail], axis=2)
    weights = lambda t: (edge_recv[t], edge_send[t], edge_geo[t], edge_out[t], node_first[t], node_second[t])
    latent, geo = call(True, False, *exchange(raw), neighbor_codes, edge_mask, position, enc_first, enc_second, *weights(0))
    (latent,) = call(False, False, *exchange(latent), neighbor_codes, geo, *weights(1))
    return tuple(
        call(
            False,
            True,
            *exchange(latent),
            neighbor_codes,
            geo,
            *weights(2),
            occupancy,
            position,
            velocity,
            dec_first,
            dec_second,
        )
    )


def solution(mesh):
    tile = P("slab", "cross", None, None)
    return jax.shard_map(
        shards,
        mesh=mesh,
        in_specs=(tile, tile, tile, P("slab", "cross"), tile, tile) + (P(),) * 10,
        out_specs=(tile, tile),
        check_vma=False,
    )
```

time: 205 us -> 117 us (0.57)
  matrix products: 108 us -> 0 us
  Pallas kernels: 0 us -> 46.7 us
  starting transfers between devices: 66.3 us -> 55.5 us
  waiting for transfers between devices: 17.3 us -> 6.99 us
  other arithmetic: 5.42 us -> 0.96 us
    dot_general x69 -> x0, matrix products: 108 us -> none  [the longest x12 51.2 us: one_bin(): lax.dot_general(geo_win, selector.astype(jnp.float32), (((1,), (1,)), (()...]
    pallas_call x0 -> x3, Pallas kernels: none -> 46.7 us  [call(): pl.pallas_call(functools.partial(step_kernel, first, last), out_shape=out...]
    ppermute x16 -> x12, starting transfers between devices: 66.3 us -> 55.5 us  [the longest x3 26.6 us: exchange(): high = lax.ppermute(block[:1], 'slab', shifted(slabs, -1))]
    ppermute x16 -> x12, waiting for transfers between devices: 17.3 us -> 6.99 us  [the longest x3 3.62 us: exchange(): left = lax.ppermute(second, 'cross', shifted(cross, 1))]
  transfers between devices with their start and end apart: 16 -> 12, of which waited for: 6 -> 7; matrix products, arithmetic and copies ran while one was open for 2% -> 1% of each run, Pallas kernels for 0% -> 0%
where the time goes in v1:
time: 117 us; the launch traced here: 115 us
  starting transfers between devices  55.5 us (47%)
  Pallas kernels  46.7 us (40%)
  waiting for transfers between devices  6.99 us (6%)
  local copies, waits for them, and re-layouts  4.14 us (4%)
    pallas_call x3, Pallas kernels, call(): pl.pallas_call(functools.partial(step_kernel, first, last), out_shape=out...  46.7 us
    ppermute x3, starting transfers between devices, exchange(): high = lax.ppermute(block[:1], 'slab', shifted(slabs, -1))  26.6 us
    ppermute x3, starting transfers between devices, exchange(): left = lax.ppermute(second, 'cross', shifted(cross, 1))  15.3 us
    ppermute x3, starting transfers between devices, exchange(): low = lax.ppermute(block[1:], 'slab', shifted(slabs, 1))  6.96 us
    ppermute x3, starting transfers between devices, exchange(): right = lax.ppermute(first, 'cross', shifted(cross, -1))  6.7 us
    ppermute x3, waiting for transfers between devices, exchange(): left = lax.ppermute(second, 'cross', shifted(cross, 1))  3.62 us
    unnamed x30, local copies, waits for them, and re-layouts  2.62 us
    ppermute x3, waiting for transfers between devices, exchange(): high = lax.ppermute(block[:1], 'slab', shifted(slabs, -1))  2.57 us
  transfers between devices with their start and end apart: 12, of which 7 were waited for; matrix products, arithmetic and copies ran while one was open for 1% of the time, Pallas kernels for 0%

profile of v1, /device:TPU:17, one launch (start us, length us, event | category | flops | bytes accessed | tf_op | source)
XLA Modules:
  0.0 115.5 jit_solution(10151790637357397636)
XLA Ops:
  0.6 0.8 subtract_convert_fusion
  1.5 0.8 copy.18
  2.6 3.1 %collective-permute-start = (bf16[1,2,48,128]{3,2,1,0:T(8,128)(2,1)S(1)}, bf16[1,2,48,128]{3,2,1,0:T(8,128)(2,1)S(1)}, u32[]{:S(2)}, u32[]{:S(2)}) collective-permute-start(bf16[1,2,48,128]{3,2,1,0:T(8,128)(2,1)S(1)} %get-tuple-element.40), channel_id=1, source_target_pairs={{0,4},{4,8},{8,12},{12,16},{16,20},{20,24},{24,28},{28,32},{32,36}... | collective-permute-start | bytes 73736 | tf_op jit(solution)/shard_map/ppermute | solution.py:182
  5.7 8.4 %collective-permute-start.1 = (bf16[1,2,48,128]{3,2,1,0:T(8,128)(2,1)S(1)}, bf16[1,2,48,128]{3,2,1,0:T(8,128)(2,1)S(1)}, u32[]{:S(2)}, u32[]{:S(2)}) collective-permute-start(bf16[1,2,48,128]{3,2,1,0:T(8,128)(2,1)S(1)} %get-tuple-element.39), channel_id=1, source_target_pairs={{4,0},{8,4},{12,8},{16,12},{20,16},{24,20},{28,24},{32,28},{36,32}... | collective-permute-start | bytes 73736 | tf_op jit(solution)/shard_map/ppermute | solution.py:183
  14.1 1.1 slice_bitcast_fusion
  15.3 0.9 copy-done.8
  16.4 2.9 %collective-permute-start.3 = (bf16[4,1,48,128]{3,2,1,0:T(8,128)(2,1)S(1)}, bf16[4,1,48,128]{3,2,1,0:T(8,128)(2,1)S(1)}, u32[]{:S(2)}, u32[]{:S(2)}) collective-permute-start(bf16[4,1,48,128]{3,2,1,0:T(8,128)(2,1)S(1)} %pad_maximum_fusion.5), channel_id=1, source_target_pairs={{1,0},{2,1},{3,2},{5,4},{6,5},{7,6},{9,8},{10,9},{11,10},{13,12},{... | collective-permute-start | bytes 147464 | tf_op jit(solution)/shard_map/ppermute | solution.py:187
  19.4 3.7 %collective-permute-start.2 = (bf16[4,1,48,128]{3,2,1,0:T(8,128)(2,1)S(1)}, bf16[4,1,48,128]{3,2,1,0:T(8,128)(2,1)S(1)}, u32[]{:S(2)}, u32[]{:S(2)}) collective-permute-start(bf16[4,1,48,128]{3,2,1,0:T(8,128)(2,1)S(1)} %pad_maximum_fusion.4), channel_id=1, source_target_pairs={{0,1},{1,2},{2,3},{4,5},{5,6},{6,7},{8,9},{9,10},{10,11},{12,13},{... | collective-permute-start | bytes 147464 | tf_op jit(solution)/shard_map/ppermute | solution.py:186
  23.1 1.1 collective-permute-done.2.refs_3_
  24.2 16.4 %first_step.1 = (bf16[2,2,128,128]{3,2,1,0:T(8,128)(2,1)S(1)}, bf16[4,16,2048]{2,1,0:T(8,128)(2,1)S(1)}) custom-call(bf16[2,2,48,128]{3,2,1,0:T(8,128)(2,1)S(1)} %concatenate.21.refs_0_, bf16[1,2,48,128]{3,2,1,0:T(8,128)(2,1)S(1)} %collective-permute-done.refs_1_, bf16[1,2,48,128]{3,2,1,0:T(8,128)(2,1)S(1)} %collective-permute-done.1.refs_2_, ...), custom_call_target="tpu_custom_call" | custom-call | tf_op jit(solution)/shard_map/first_step/pallas_call | solution.py:208
  40.6 1.9 %collective-permute-start.4 = (bf16[1,2,128,128]{3,2,1,0:T(8,128)(2,1)S(1)}, bf16[1,2,128,128]{3,2,1,0:T(8,128)(2,1)S(1)}, u32[]{:S(2)}, u32[]{:S(2)}) collective-permute-start(bf16[1,2,128,128]{3,2,1,0:T(8,128)(2,1)S(1)} %get-tuple-element.25), channel_id=1, source_target_pairs={{0,4},{4,8},{8,12},{12,16},{16,20},{20,24},{24,28},{28,32},{32,36}... | collective-permute-start | bytes 196616 | tf_op jit(solution)/shard_map/ppermute | solution.py:182
  42.6 9.1 %collective-permute-start.5 = (bf16[1,2,128,128]{3,2,1,0:T(8,128)(2,1)S(1)}, bf16[1,2,128,128]{3,2,1,0:T(8,128)(2,1)S(1)}, u32[]{:S(2)}, u32[]{:S(2)}) collective-permute-start(bf16[1,2,128,128]{3,2,1,0:T(8,128)(2,1)S(1)} %get-tuple-element.24), channel_id=1, source_target_pairs={{4,0},{8,4},{12,8},{16,12},{20,16},{24,20},{28,24},{32,28},{36,32}... | collective-permute-start | bytes 196616 | tf_op jit(solution)/shard_map/ppermute | solution.py:183
  51.7 1.3 %collective-permute-done.5.refs_2_ = bf16[1,2,128,128]{3,2,1,0:T(8,128)(2,1)S(1)} collective-permute-done((bf16[1,2,128,128]{3,2,1,0:T(8,128)(2,1)S(1)}, bf16[1,2,128,128]{3,2,1,0:T(8,128)(2,1)S(1)}, u32[]{:S(2)}, u32[]{:S(2)}) %collective-permute-start.5) | collective-permute-done | bytes 65568 | tf_op jit(solution)/shard_map/ppermute | solution.py:183
  53.0 1.9 %collective-permute-start.7 = (bf16[4,1,128,128]{3,2,1,0:T(8,128)(2,1)S(1)}, bf16[4,1,128,128]{3,2,1,0:T(8,128)(2,1)S(1)}, u32[]{:S(2)}, u32[]{:S(2)}) collective-permute-start(bf16[4,1,128,128]{3,2,1,0:T(8,128)(2,1)S(1)} %pad_maximum_fusion.1), channel_id=1, source_target_pairs={{1,0},{2,1},{3,2},{5,4},{6,5},{7,6},{9,8},{10,9},{11,10},{13,12},{... | collective-permute-start | bytes 393224 | tf_op jit(solution)/shard_map/ppermute | solution.py:187
  55.0 5.6 %collective-permute-start.6 = (bf16[4,1,128,128]{3,2,1,0:T(8,128)(2,1)S(1)}, bf16[4,1,128,128]{3,2,1,0:T(8,128)(2,1)S(1)}, u32[]{:S(2)}, u32[]{:S(2)}) collective-permute-start(bf16[4,1,128,128]{3,2,1,0:T(8,128)(2,1)S(1)} %pad_maximum_fusion), channel_id=1, source_target_pairs={{0,1},{1,2},{2,3},{4,5},{5,6},{6,7},{8,9},{9,10},{10,11},{12,13},{... | collective-permute-start | bytes 393224 | tf_op jit(solution)/shard_map/ppermute | solution.py:186
  61.1 1.2 %collective-permute-done.6.refs_3_ = bf16[4,1,128,128]{3,2,1,0:T(8,128)(2,1)S(1)} collective-permute-done((bf16[4,1,128,128]{3,2,1,0:T(8,128)(2,1)S(1)}, bf16[4,1,128,128]{3,2,1,0:T(8,128)(2,1)S(1)}, u32[]{:S(2)}, u32[]{:S(2)}) %collective-permute-start.6) | collective-permute-done | bytes 131104 | tf_op jit(solution)/shard_map/ppermute | solution.py:186
  62.3 14.5 %middle_step.1.refs_0_ = bf16[2,2,128,128]{3,2,1,0:T(8,128)(2,1)S(1)} custom-call(bf16[2,2,128,128]{3,2,1,0:T(8,128)(2,1)S(1)} %get-tuple-element.4.refs_0_, bf16[1,2,128,128]{3,2,1,0:T(8,128)(2,1)S(1)} %collective-permute-done.4.refs_1_, bf16[1,2,128,128]{3,2,1,0:T(8,128)(2,1)S(1)} %collective-permute-done.5.refs_2_, ...), custom_call_target="tpu_custom_call" | custom-call | tf_op jit(solution)/shard_map/middle_step/pallas_call | solution.py:208
  76.8 1.9 %collective-permute-start.8 = (bf16[1,2,128,128]{3,2,1,0:T(8,128)(2,1)S(1)}, bf16[1,2,128,128]{3,2,1,0:T(8,128)(2,1)S(1)}, u32[]{:S(2)}, u32[]{:S(2)}) collective-permute-start(bf16[1,2,128,128]{3,2,1,0:T(8,128)(2,1)S(1)} %get-tuple-element.21), channel_id=1, source_target_pairs={{0,4},{4,8},{8,12},{12,16},{16,20},{20,24},{24,28},{28,32},{32,36}... | collective-permute-start | bytes 196616 | tf_op jit(solution)/shard_map/ppermute | solution.py:182
  78.7 9.1 %collective-permute-start.9 = (bf16[1,2,128,128]{3,2,1,0:T(8,128)(2,1)S(1)}, bf16[1,2,128,128]{3,2,1,0:T(8,128)(2,1)S(1)}, u32[]{:S(2)}, u32[]{:S(2)}) collective-permute-start(bf16[1,2,128,128]{3,2,1,0:T(8,128)(2,1)S(1)} %get-tuple-element.20), channel_id=1, source_target_pairs={{4,0},{8,4},{12,8},{16,12},{20,16},{24,20},{28,24},{32,28},{36,32}... | collective-permute-start | bytes 196616 | tf_op jit(solution)/shard_map/ppermute | solution.py:183
  87.9 1.3 %collective-permute-done.9.refs_2_ = bf16[1,2,128,128]{3,2,1,0:T(8,128)(2,1)S(1)} collective-permute-done((bf16[1,2,128,128]{3,2,1,0:T(8,128)(2,1)S(1)}, bf16[1,2,128,128]{3,2,1,0:T(8,128)(2,1)S(1)}, u32[]{:S(2)}, u32[]{:S(2)}) %collective-permute-start.9) | collective-permute-done | bytes 65568 | tf_op jit(solution)/shard_map/ppermute | solution.py:183
  89.2 1.9 %collective-permute-start.11 = (bf16[4,1,128,128]{3,2,1,0:T(8,128)(2,1)S(1)}, bf16[4,1,128,128]{3,2,1,0:T(8,128)(2,1)S(1)}, u32[]{:S(2)}, u32[]{:S(2)}) collective-permute-start(bf16[4,1,128,128]{3,2,1,0:T(8,128)(2,1)S(1)} %pad_maximum_fusion.3), channel_id=1, source_target_pairs={{1,0},{2,1},{3,2},{5,4},{6,5},{7,6},{9,8},{10,9},{11,10},{13,12},{... | collective-permute-start | bytes 393224 | tf_op jit(solution)/shard_map/ppermute | solution.py:187
  91.2 6.0 %collective-permute-start.10 = (bf16[4,1,128,128]{3,2,1,0:T(8,128)(2,1)S(1)}, bf16[4,1,128,128]{3,2,1,0:T(8,128)(2,1)S(1)}, u32[]{:S(2)}, u32[]{:S(2)}) collective-permute-start(bf16[4,1,128,128]{3,2,1,0:T(8,128)(2,1)S(1)} %pad_maximum_fusion.2), channel_id=1, source_target_pairs={{0,1},{1,2},{2,3},{4,5},{5,6},{6,7},{8,9},{9,10},{10,11},{12,13},{... | collective-permute-start | bytes 393224 | tf_op jit(solution)/shard_map/ppermute | solution.py:186
  97.6 1.3 %collective-permute-done.10.refs_3_ = bf16[4,1,128,128]{3,2,1,0:T(8,128)(2,1)S(1)} collective-permute-done((bf16[4,1,128,128]{3,2,1,0:T(8,128)(2,1)S(1)}, bf16[4,1,128,128]{3,2,1,0:T(8,128)(2,1)S(1)}, u32[]{:S(2)}, u32[]{:S(2)}) %collective-permute-start.10) | collective-permute-done | bytes 131104 | tf_op jit(solution)/shard_map/ppermute | solution.py:186
  99.6 15.9 %last_step.1 = (f32[2,2,2,128]{3,2,1,0:T(2,128)}, f32[2,2,2,128]{3,2,1,0:T(2,128)}) custom-call(bf16[2,2,128,128]{3,2,1,0:T(8,128)(2,1)S(1)} %middle_step.1.refs_0_, bf16[1,2,128,128]{3,2,1,0:T(8,128)(2,1)S(1)} %collective-permute-done.8.refs_1_, bf16[1,2,128,128]{3,2,1,0:T(8,128)(2,1)S(1)} %collective-permute-done.9.refs_2_, ...), custom_call_target="tpu_custom_call" | custom-call | tf_op jit(solution)/shard_map/last_step/pallas_call | solution.py:208
  (62 shorter events, 2.3 us)
Async XLA Ops:
  0.6 0.8 copy-start.1
  2.6 13.8 %collective-permute-start = (bf16[1,2,48,128]{3,2,1,0:T(8,128)(2,1)S(1)}, bf16[1,2,48,128]{3,2,1,0:T(8,128)(2,1)S(1)}, u32[]{:S(2)}, u32[]{:S(2)}) collective-permute-start(bf16[1,2,48,128]{3,2,1,0:T(8,128)(2,1)S(1)} %get-tuple-element.40), channel_id=1, source_target_pairs={{0,4},{4,8},{8,12},{12,16},{16,20},{20,24},{24,28},{28,32},{32,36}... | collective-permute-start | bytes 73736 | tf_op jit(solution)/shard_map/ppermute | solution.py:182
  5.7 9.5 %copy-start.10 = (bf16[3,256,128]{2,1,0:T(8,128)(2,1)S(1)}, bf16[3,256,128]{2,1,0:T(8,128)(2,1)}, u32[]{:S(2)}) copy-start(bf16[3,256,128]{2,1,0:T(8,128)(2,1)} %param.28) | copy-start | bytes 589828
  5.7 10.7 %collective-permute-start.1 = (bf16[1,2,48,128]{3,2,1,0:T(8,128)(2,1)S(1)}, bf16[1,2,48,128]{3,2,1,0:T(8,128)(2,1)S(1)}, u32[]{:S(2)}, u32[]{:S(2)}) collective-permute-start(bf16[1,2,48,128]{3,2,1,0:T(8,128)(2,1)S(1)} %get-tuple-element.39), channel_id=1, source_target_pairs={{4,0},{8,4},{12,8},{16,12},{20,16},{24,20},{28,24},{32,28},{36,32}... | collective-permute-start | bytes 73736 | tf_op jit(solution)/shard_map/ppermute | solution.py:183
  14.1 1.2 %copy-start.11 = (bf16[3,128,128]{2,1,0:T(8,128)(2,1)S(1)}, bf16[3,128,128]{2,1,0:T(8,128)(2,1)}, u32[]{:S(2)}) copy-start(bf16[3,128,128]{2,1,0:T(8,128)(2,1)} %param.29) | copy-start | bytes 294916
  14.1 1.2 %copy-start.9 = (bf16[3,128,512]{2,1,0:T(8,128)(2,1)S(1)}, bf16[3,128,512]{2,1,0:T(8,128)(2,1)}, u32[]{:S(2)}) copy-start(bf16[3,128,512]{2,1,0:T(8,128)(2,1)} %param.24) | copy-start | bytes 1179652
  15.3 1.0 copy-start.8
  16.4 6.7 %collective-permute-start.3 = (bf16[4,1,48,128]{3,2,1,0:T(8,128)(2,1)S(1)}, bf16[4,1,48,128]{3,2,1,0:T(8,128)(2,1)S(1)}, u32[]{:S(2)}, u32[]{:S(2)}) collective-permute-start(bf16[4,1,48,128]{3,2,1,0:T(8,128)(2,1)S(1)} %pad_maximum_fusion.5), channel_id=1, source_target_pairs={{1,0},{2,1},{3,2},{5,4},{6,5},{7,6},{9,8},{10,9},{11,10},{13,12},{... | collective-permute-start | bytes 147464 | tf_op jit(solution)/shard_map/ppermute | solution.py:187
  19.3 3.8 %copy-start.12 = (f32[3,3,512]{2,1,0:T(4,128)S(1)}, f32[3,3,512]{2,1,0:T(4,128)}, u32[]{:S(2)}) copy-start(f32[3,3,512]{2,1,0:T(4,128)} %param.26) | copy-start | bytes 55300
  19.3 4.9 %copy-start.2 = (s32[2,2,16,128]{3,2,1,0:T(8,128)S(1)}, s32[2,2,16,128]{3,2,1,0:T(8,128)}, u32[]{:S(2)}) copy-start(s32[2,2,16,128]{3,2,1,0:T(8,128)} %refs_6_.1) | copy-start | bytes 98308
  19.3 4.9 %copy-start.3 = (bf16[128,128]{1,0:T(8,128)(2,1)S(1)}, bf16[128,128]{1,0:T(8,128)(2,1)}, u32[]{:S(2)}) copy-start(bf16[128,128]{1,0:T(8,128)(2,1)} %refs_9_.1) | copy-start | bytes 98308
  19.3 4.9 %copy-start = (s32[2,2,16,128]{3,2,1,0:T(8,128)S(1)}, s32[2,2,16,128]{3,2,1,0:T(8,128)}, u32[]{:S(2)}) copy-start(s32[2,2,16,128]{3,2,1,0:T(8,128)} %refs_5_.5) | copy-start | bytes 98308
  19.4 4.9 %collective-permute-start.2 = (bf16[4,1,48,128]{3,2,1,0:T(8,128)(2,1)S(1)}, bf16[4,1,48,128]{3,2,1,0:T(8,128)(2,1)S(1)}, u32[]{:S(2)}, u32[]{:S(2)}) collective-permute-start(bf16[4,1,48,128]{3,2,1,0:T(8,128)(2,1)S(1)} %pad_maximum_fusion.4), channel_id=1, source_target_pairs={{0,1},{1,2},{2,3},{4,5},{5,6},{6,7},{8,9},{9,10},{10,11},{12,13},{... | collective-permute-start | bytes 147464 | tf_op jit(solution)/shard_map/ppermute | solution.py:186
  23.1 1.1 copy-start.5
  40.6 11.0 %collective-permute-start.4 = (bf16[1,2,128,128]{3,2,1,0:T(8,128)(2,1)S(1)}, bf16[1,2,128,128]{3,2,1,0:T(8,128)(2,1)S(1)}, u32[]{:S(2)}, u32[]{:S(2)}) collective-permute-start(bf16[1,2,128,128]{3,2,1,0:T(8,128)(2,1)S(1)} %get-tuple-element.25), channel_id=1, source_target_pairs={{0,4},{4,8},{8,12},{12,16},{16,20},{20,24},{24,28},{28,32},{32,36}... | collective-permute-start | bytes 196616 | tf_op jit(solution)/shard_map/ppermute | solution.py:182
  42.6 10.4 %collective-permute-start.5 = (bf16[1,2,128,128]{3,2,1,0:T(8,128)(2,1)S(1)}, bf16[1,2,128,128]{3,2,1,0:T(8,128)(2,1)S(1)}, u32[]{:S(2)}, u32[]{:S(2)}) collective-permute-start(bf16[1,2,128,128]{3,2,1,0:T(8,128)(2,1)S(1)} %get-tuple-element.24), channel_id=1, source_target_pairs={{4,0},{8,4},{12,8},{16,12},{20,16},{24,20},{28,24},{32,28},{36,32}... | collective-permute-start | bytes 196616 | tf_op jit(solution)/shard_map/ppermute | solution.py:183
  53.0 8.0 %collective-permute-start.7 = (bf16[4,1,128,128]{3,2,1,0:T(8,128)(2,1)S(1)}, bf16[4,1,128,128]{3,2,1,0:T(8,128)(2,1)S(1)}, u32[]{:S(2)}, u32[]{:S(2)}) collective-permute-start(bf16[4,1,128,128]{3,2,1,0:T(8,128)(2,1)S(1)} %pad_maximum_fusion.1), channel_id=1, source_target_pairs={{1,0},{2,1},{3,2},{5,4},{6,5},{7,6},{9,8},{10,9},{11,10},{13,12},{... | collective-permute-start | bytes 393224 | tf_op jit(solution)/shard_map/ppermute | solution.py:187
  55.0 7.3 %collective-permute-start.6 = (bf16[4,1,128,128]{3,2,1,0:T(8,128)(2,1)S(1)}, bf16[4,1,128,128]{3,2,1,0:T(8,128)(2,1)S(1)}, u32[]{:S(2)}, u32[]{:S(2)}) collective-permute-start(bf16[4,1,128,128]{3,2,1,0:T(8,128)(2,1)S(1)} %pad_maximum_fusion), channel_id=1, source_target_pairs={{0,1},{1,2},{2,3},{4,5},{5,6},{6,7},{8,9},{9,10},{10,11},{12,13},{... | collective-permute-start | bytes 393224 | tf_op jit(solution)/shard_map/ppermute | solution.py:186
  76.8 11.1 %collective-permute-start.8 = (bf16[1,2,128,128]{3,2,1,0:T(8,128)(2,1)S(1)}, bf16[1,2,128,128]{3,2,1,0:T(8,128)(2,1)S(1)}, u32[]{:S(2)}, u32[]{:S(2)}) collective-permute-start(bf16[1,2,128,128]{3,2,1,0:T(8,128)(2,1)S(1)} %get-tuple-element.21), channel_id=1, source_target_pairs={{0,4},{4,8},{8,12},{12,16},{16,20},{20,24},{24,28},{28,32},{32,36}... | collective-permute-start | bytes 196616 | tf_op jit(solution)/shard_map/ppermute | solution.py:182
  78.7 10.4 %collective-permute-start.9 = (bf16[1,2,128,128]{3,2,1,0:T(8,128)(2,1)S(1)}, bf16[1,2,128,128]{3,2,1,0:T(8,128)(2,1)S(1)}, u32[]{:S(2)}, u32[]{:S(2)}) collective-permute-start(bf16[1,2,128,128]{3,2,1,0:T(8,128)(2,1)S(1)} %get-tuple-element.20), channel_id=1, source_target_pairs={{4,0},{8,4},{12,8},{16,12},{20,16},{24,20},{28,24},{32,28},{36,32}... | collective-permute-start | bytes 196616 | tf_op jit(solution)/shard_map/ppermute | solution.py:183
  89.2 8.5 %collective-permute-start.11 = (bf16[4,1,128,128]{3,2,1,0:T(8,128)(2,1)S(1)}, bf16[4,1,128,128]{3,2,1,0:T(8,128)(2,1)S(1)}, u32[]{:S(2)}, u32[]{:S(2)}) collective-permute-start(bf16[4,1,128,128]{3,2,1,0:T(8,128)(2,1)S(1)} %pad_maximum_fusion.3), channel_id=1, source_target_pairs={{1,0},{2,1},{3,2},{5,4},{6,5},{7,6},{9,8},{10,9},{11,10},{13,12},{... | collective-permute-start | bytes 393224 | tf_op jit(solution)/shard_map/ppermute | solution.py:187
  91.1 6.1 %copy-start.13 = (bf16[128,2]{0,1:T(2,128)(2,1)S(1)}, bf16[128,2]{0,1:T(2,128)(2,1)}, u32[]{:S(2)}) copy-start(bf16[128,2]{0,1:T(2,128)(2,1)} %param.31) | copy-start | bytes 1540
  91.1 7.8 %copy-start.4 = (bf16[128,128]{1,0:T(8,128)(2,1)S(1)}, bf16[128,128]{1,0:T(8,128)(2,1)}, u32[]{:S(2)}) copy-start(bf16[128,128]{1,0:T(8,128)(2,1)} %refs_16_.1) | copy-start | bytes 98308
  91.2 7.7 %collective-permute-start.10 = (bf16[4,1,128,128]{3,2,1,0:T(8,128)(2,1)S(1)}, bf16[4,1,128,128]{3,2,1,0:T(8,128)(2,1)S(1)}, u32[]{:S(2)}, u32[]{:S(2)}) collective-permute-start(bf16[4,1,128,128]{3,2,1,0:T(8,128)(2,1)S(1)} %pad_maximum_fusion.2), channel_id=1, source_target_pairs={{0,1},{1,2},{2,3},{4,5},{5,6},{6,7},{8,9},{9,10},{10,11},{12,13},{... | collective-permute-start | bytes 393224 | tf_op jit(solution)/shard_map/ppermute | solution.py:186
  (2 other events, 1.5 us)

commit v2 on v1

v2 whole, which is shorter than its diff:
```python
import functools

import jax
import jax.numpy as jnp
from jax import lax
from jax.experimental import pallas as pl
from jax.experimental.pallas import tpu as pltpu
from jax.sharding import PartitionSpec as P

time_step = 0.5
LAT = 128
EH = 512
INF = 30
KNB = 16
SLOTS = 128
PACK = 48
GEO = 16
WIDE = 8
BLOCKED = -(2.0**40)
bf16 = jnp.bfloat16
f32 = jnp.float32
i32 = jnp.int32


def tdot(left, right):
    return lax.dot_general(left, right, (((0,), (0,)), ((), ())), preferred_element_type=f32)


def split3(values):
    high = values.astype(bf16).astype(f32)
    rest = values - high
    mid = rest.astype(bf16).astype(f32)
    return [high, mid, rest - mid]


def norm_rows(values):
    center = values - jnp.mean(values, axis=0, keepdims=True)
    spread = jnp.mean(center * center, axis=0, keepdims=True)
    return center * lax.rsqrt(spread + 1e-05)


def parities():
    return lax.rem(lax.axis_index("slab"), 2), lax.rem(lax.axis_index("cross"), 2)


def lane_rows(values, first, count):
    return jnp.concatenate([values[k : k + 1] for k in range(first, first + count)], axis=1)


def repeated(values, count):
    return jnp.concatenate([values] * count, axis=1)


def prepare_kernel(features, position, occupancy, codes, mask, raw, own_codes, send_a, send_b):
    p, q = parities()
    lane = lax.broadcasted_iota(i32, (1, SLOTS), 1)
    for a in range(2):
        for c in range(2):
            live = (lane < occupancy[a, c]).astype(f32)
            rows = [features[a, c].astype(f32), jnp.zeros((2, SLOTS), f32)]
            rows += split3(position[a, c, 0:1]) + split3(position[a, c, 1:2])
            rows += [live, jnp.zeros((PACK - 39, SLOTS), f32)]
            raw[a, c] = jnp.concatenate(rows, axis=0).astype(bf16)
            own_codes[a, c] = jnp.where(mask[a, c] > 0, codes[a, c], (codes[a, c] & (SLOTS - 1)) - SLOTS)
    for near, far, out in ((1 - p, p, send_a), (p, 1 - p, send_b)):
        for c in range(2):
            out[c, 0:PACK] = raw[near, c]
            out[c, PACK : 2 * PACK] = raw[far, c]
            code = own_codes[near, c]
            out[c, 2 * PACK : 2 * PACK + KNB] = (code >> 7).astype(f32).astype(bf16)
            out[c, 2 * PACK + KNB :] = (code & (SLOTS - 1)).astype(f32).astype(bf16)


def pack_raw_kernel(own, got_a, got_b, send_c, send_d):
    p, q = parities()
    for j, out in ((1 - q, send_c), (q, send_d)):
        out[2] = own[0, j]
        out[3] = own[1, j]
        for side, got in ((1 - p, got_a), (p, got_b)):
            out[1 + 3 * side] = got[j, 0:PACK]
            out[5 * side] = got[j, PACK : 2 * PACK]


def pack_kernel(own, got_a, got_b, send_c, send_d):
    p, q = parities()
    for j, out in ((1 - q, send_c), (q, send_d)):
        out[1] = own[0, j]
        out[2] = own[1, j]
        out[3 * (1 - p)] = got_a[j]
        out[3 * p] = got_b[j]


def one_hot(codes):
    wide = codes.shape[1]
    window = codes >> 7
    slot = codes & (SLOTS - 1)
    iota = lax.broadcasted_iota(i32, (SLOTS, wide), 0).astype(jnp.int16)
    parts = []
    for w in range(9):
        wanted = jnp.where(window == w, slot, -1).astype(jnp.int16)
        hit = iota == jnp.broadcast_to(wanted, (SLOTS, wide))
        parts.append(jnp.where(hit, jnp.ones((), bf16), jnp.zeros((), bf16)))
    return jnp.concatenate(parts, axis=0)


def edge_weight(send_w, geo_w, full_w):
    values = geo_w[...]
    high = values.astype(bf16)
    low = (values - high.astype(f32)).astype(bf16)
    rows = []
    for c in range(3):
        rows += [high[c : c + 1], high[c : c + 1], low[c : c + 1], low[c : c + 1]]
    rows.append(jnp.full((1, EH), BLOCKED, bf16))
    rows.append(jnp.zeros((GEO - 13, EH), bf16))
    full_w[0:LAT, :] = send_w[...]
    full_w[LAT:, :] = jnp.concatenate(rows, axis=0)


def geometry_rows(got, own_x, own_y, own_live):
    delta_x = got[0:1] + got[1:2] + got[2:3] - own_x
    delta_y = got[3:4] + got[4:5] + got[5:6] - own_y
    distance = delta_x * delta_x + delta_y * delta_y
    pieces = []
    for v in (delta_x, delta_y, distance):
        high = v.astype(bf16).astype(f32)
        pieces += [high, v - high, high, v - high]
    pieces.append(1.0 - own_live * got[6:7])
    pieces.append(jnp.zeros((GEO - 13, got.shape[1]), f32))
    return jnp.concatenate(pieces, axis=0).astype(bf16)


def edge_sum(full_w, right_side, bound, total):
    hidden = tdot(full_w[...], right_side)
    for k in range(right_side.shape[1] // SLOTS):
        part = jnp.maximum(hidden[:, k * SLOTS : (k + 1) * SLOTS], bound)
        total = part if total is None else total + part
    return total


def node_update(own_all, sums, out_w, first_w, second_w):
    summed = tdot(out_w, sums).astype(bf16)
    joined = tdot(first_w, jnp.concatenate([own_all, summed], axis=0))
    joined = jnp.maximum(joined, 0.0).astype(bf16)
    update = norm_rows(tdot(second_w, joined))
    return (own_all.astype(f32) + update).astype(bf16)


def first_kernel(
    own, got_a, got_b, got_c, got_d, own_codes, enc_first, enc_second, recv_w, send_w, geo_w, out_w, first_w, second_w,
    latent_out, geo_out, send_c, send_d, pack, codes_all, win, own_win, full_w, recv_all, sums,
):
    p, q = parities()
    for c in range(2):
        for a in range(2):
            pack[2 + a, 1 + c] = own[a, c]
            codes_all[1 + a, c] = own_codes[a, c]
        for side, got in ((1 - p, got_a), (p, got_b)):
            pack[1 + 3 * side, 1 + c] = got[c, 0:PACK]
            pack[5 * side, 1 + c] = got[c, PACK : 2 * PACK]
            window = got[c, 2 * PACK : 2 * PACK + KNB].astype(f32)
            slot = got[c, 2 * PACK + KNB :].astype(f32)
            codes_all[3 * side, c] = (window * SLOTS + slot).astype(i32)
    for i in range(6):
        pack[i, 3 * (1 - q)] = got_c[i]
        pack[i, 3 * q] = got_d[i]
    weight = jnp.concatenate([enc_first[...], jnp.zeros((PACK - INF, LAT), bf16)], axis=0)
    for i in range(6):
        raw = jnp.concatenate([pack[i, j] for j in range(4)], axis=1)
        hidden = jnp.maximum(tdot(weight, raw), 0.0).astype(bf16)
        latent = norm_rows(tdot(enc_second[...], hidden)).astype(bf16)
        for j in range(4):
            win[i, j] = latent[:, j * SLOTS : (j + 1) * SLOTS]
    own_all = jnp.concatenate([win[1 + b // 2, 1 + b % 2] for b in range(8)], axis=1)
    recv_all[...] = -tdot(recv_w[0], own_all)
    edge_weight(send_w.at[0], geo_w.at[0], full_w)

    def one_bin(b, carry):
        a, c = lax.div(b, 2), lax.rem(b, 2)
        codes = codes_all[a, c]
        lats = jnp.concatenate([win[a + w // 3, c + w % 3] for w in range(9)], axis=1)
        geos = jnp.concatenate([pack[a + w // 3, c + w % 3, 32:PACK, :] for w in range(9)], axis=1)
        stacked = jnp.concatenate([lats, geos], axis=0)
        me = pack[a + 1, c + 1, 32:PACK, :].astype(f32)
        own_x = repeated(me[0:1] + me[1:2] + me[2:3], WIDE)
        own_y = repeated(me[3:4] + me[4:5] + me[5:6], WIDE)
        own_live = repeated(me[6:7], WIDE)
        columns = pl.ds(pl.multiple_of(b * SLOTS, SLOTS), SLOTS)
        bound = recv_all[:, columns]
        total = None
        for part in range(KNB // WIDE):
            hot = one_hot(lane_rows(codes, part * WIDE, WIDE))
            got = jnp.dot(stacked, hot, preferred_element_type=f32)
            geo = geometry_rows(got[LAT:], own_x, own_y, own_live)
            geo_out[b, :, part * WIDE * SLOTS : (part + 1) * WIDE * SLOTS] = geo
            total = edge_sum(full_w, jnp.concatenate([got[:LAT].astype(bf16), geo], axis=0), bound, total)
        sums[:, columns] = (total - KNB * bound).astype(bf16)
        return carry

    lax.fori_loop(0, 8, one_bin, 0)
    latent = node_update(own_all, sums[...], out_w[0], first_w[0], second_w[0])
    for b in range(8):
        latent_out[b // 2, b % 2] = latent[:, b * SLOTS : (b + 1) * SLOTS]
    for i in range(4):
        send_c[i] = latent_out[i, 1 - q]
        send_d[i] = latent_out[i, q]


def later_step(t, win, own_codes, geo, recv_w, send_w, geo_w, out_w, first_w, second_w, full_w, recv_all, sums):
    own_all = jnp.concatenate([win[1 + b // 2, 1 + b % 2] for b in range(4)], axis=1)
    recv_all[...] = -tdot(recv_w[t], own_all)
    edge_weight(send_w.at[t], geo_w.at[t], full_w)
    for b in range(4):
        a, c = b // 2, b % 2
        codes = own_codes[a, c]
        lats = jnp.concatenate([win[a + w // 3, c + w % 3] for w in range(9)], axis=1)
        bound = recv_all[:, b * SLOTS : (b + 1) * SLOTS]
        total = None
        for part in range(KNB // WIDE):
            hot = one_hot(lane_rows(codes, part * WIDE, WIDE))
            got = jnp.dot(lats, hot, preferred_element_type=f32).astype(bf16)
            rows = geo[2 + b, :, part * WIDE * SLOTS : (part + 1) * WIDE * SLOTS]
            total = edge_sum(full_w, jnp.concatenate([got, rows], axis=0), bound, total)
        sums[:, b * SLOTS : (b + 1) * SLOTS] = (total - KNB * bound).astype(bf16)
    return node_update(own_all, sums[...], out_w[t], first_w[t], second_w[t])


def middle_kernel(
    wide, got_c, got_d, own_codes, geo, recv_w, send_w, geo_w, out_w, first_w, second_w,
    latent_out, send_a, send_b, win, full_w, recv_all, sums,
):
    p, q = parities()
    for i in range(4):
        win[i, 1] = wide[i, 0]
        win[i, 2] = wide[i, 1]
        win[i, 3 * (1 - q)] = got_c[i]
        win[i, 3 * q] = got_d[i]
    latent = later_step(1, win, own_codes, geo, recv_w, send_w, geo_w, out_w, first_w, second_w, full_w, recv_all, sums)
    for b in range(4):
        latent_out[b // 2, b % 2] = latent[:, b * SLOTS : (b + 1) * SLOTS]
    for c in range(2):
        send_a[c] = latent_out[1 - p, c]
        send_b[c] = latent_out[p, c]


def last_kernel(
    own, got_a, got_b, got_c, got_d, own_codes, geo, recv_w, send_w, geo_w, out_w, first_w, second_w,
    occupancy, position, velocity, dec_first, dec_second,
    out_velocity, out_position, win, full_w, recv_all, sums,
):
    p, q = parities()
    for c in range(2):
        win[1, 1 + c] = own[0, c]
        win[2, 1 + c] = own[1, c]
        win[3 * (1 - p), 1 + c] = got_a[c]
        win[3 * p, 1 + c] = got_b[c]
    for i in range(4):
        win[i, 3 * (1 - q)] = got_c[i]
        win[i, 3 * q] = got_d[i]
    latent = later_step(2, win, own_codes, geo, recv_w, send_w, geo_w, out_w, first_w, second_w, full_w, recv_all, sums)
    hidden = jnp.maximum(tdot(dec_first[...], latent), 0.0).astype(bf16)
    accel = tdot(dec_second[...], hidden)
    lane = lax.broadcasted_iota(i32, (2, SLOTS), 1)
    for b in range(4):
        a, c = b // 2, b % 2
        live = (lane < occupancy[a, c]).astype(f32)
        speed = velocity[a, c] + time_step * (accel[:, b * SLOTS : (b + 1) * SLOTS] * live)
        out_velocity[a, c] = speed
        out_position[a, c] = position[a, c] + time_step * speed


def run(kernel, name, out, scratch, operands, scalar=None):
    vmem = pl.BlockSpec(memory_space=pltpu.VMEM)
    specs = [vmem] * len(operands)
    if scalar is not None:
        specs[scalar] = pl.BlockSpec(memory_space=pltpu.SMEM)
    return pl.pallas_call(
        kernel,
        out_shape=[jax.ShapeDtypeStruct(shape, dtype) for shape, dtype in out],
        in_specs=specs,
        out_specs=[vmem] * len(out),
        scratch_shapes=[pltpu.VMEM(shape, dtype) for shape, dtype in scratch],
        compiler_params=pltpu.CompilerParams(vmem_limit_bytes=40 << 20),
        name=name,
    )(*operands)


def swaps(count, start):
    pairs = []
    for low in range(start, count - 1, 2):
        pairs += [(low, low + 1), (low + 1, low)]
    return pairs


def swap(block, axis, start):
    return lax.ppermute(block, axis, swaps(lax.axis_size(axis), start))


def shards(
    features,
    position,
    velocity,
    occupancy,
    neighbor_codes,
    edge_mask,
    enc_first,
    enc_second,
    edge_recv,
    edge_send,
    edge_geo,
    edge_out,
    node_first,
    node_second,
    dec_first,
    dec_second,
):
    weights = (edge_recv, edge_send, edge_geo, edge_out, node_first, node_second)
    tile = (LAT, SLOTS)
    side = ((2, *tile), bf16)
    column = ((4, *tile), bf16)
    raw_column = ((6, PACK, SLOTS), bf16)

    def scratch(bins):
        return [((LAT + GEO, EH), bf16), ((EH, bins * SLOTS), f32), ((EH, bins * SLOTS), bf16)]

    raw, own_codes, send_a, send_b = run(
        prepare_kernel,
        "prepare",
        [((2, 2, PACK, SLOTS), bf16), ((2, 2, KNB, SLOTS), i32), side, side],
        [],
        (features, position, occupancy, neighbor_codes, edge_mask),
        2,
    )
    got_b, got_a = swap(send_b, "slab", 1), swap(send_a, "slab", 0)
    send_c, send_d = run(pack_raw_kernel, "pack_raw", [raw_column] * 2, [], (raw, got_a, got_b))
    got_d, got_c = swap(send_d, "cross", 1), swap(send_c, "cross", 0)
    wide, geo, send_c, send_d = run(
        first_kernel,
        "first_step",
        [((4, 2, *tile), bf16), ((8, GEO, KNB * SLOTS), bf16), column, column],
        [
            ((6, 4, PACK, SLOTS), bf16),
            ((4, 2, KNB, SLOTS), i32),
            ((6, 4, *tile), bf16),
            ((8, *tile), bf16),
            *scratch(8),
        ],
        (raw, got_a, got_b, got_c, got_d, own_codes, enc_first, enc_second, *weights),
    )
    got_d, got_c = swap(send_d, "cross", 1), swap(send_c, "cross", 0)
    latent, send_a, send_b = run(
        middle_kernel,
        "middle_step",
        [((2, 2, *tile), bf16), side, side],
        [((4, 4, *tile), bf16), *scratch(4)],
        (wide, got_c, got_d, own_codes, geo, *weights),
    )
    got_b, got_a = swap(send_b, "slab", 1), swap(send_a, "slab", 0)
    send_c, send_d = run(pack_kernel, "pack", [column] * 2, [], (latent, got_a, got_b))
    got_d, got_c = swap(send_d, "cross", 1), swap(send_c, "cross", 0)
    operands = (latent, got_a, got_b, got_c, got_d, own_codes, geo, *weights)
    return tuple(
        run(
            last_kernel,
            "last_step",
            [((2, 2, 2, SLOTS), f32)] * 2,
            [((4, 4, *tile), bf16), *scratch(4)],
            (*operands, occupancy, position, velocity, dec_first, dec_second),
            len(operands),
        )
    )


def solution(mesh):
    tile = P("slab", "cross", None, None)
    return jax.shard_map(
        shards,
        mesh=mesh,
        in_specs=(tile, tile, tile, P("slab", "cross"), tile, tile) + (P(),) * 10,
        out_specs=(tile, tile),
        check_vma=False,
    )
```

time: 117 us -> 81.8 us (0.70)
  starting transfers between devices: 55.5 us -> 32.3 us
  Pallas kernels: 46.7 us -> 28.6 us
  waiting for transfers between devices: 6.99 us -> 11.7 us
  local copies, waits for them, and re-layouts: 4.14 us -> 7.54 us
    ppermute x12 -> x10, starting transfers between devices: 55.5 us -> 32.3 us  [swap(): return lax.ppermute(block, axis, swaps(lax.axis_size(axis), start))]
    pallas_call x3 -> x6, Pallas kernels: 46.7 us -> 28.6 us  [run(): pl.pallas_call(kernel, out_shape=[jax.ShapeDtypeStruct(shape, dtype) for...]
    unnamed x30 -> x42, local copies, waits for them, and re-layouts: 2.62 us -> 7.54 us
    ppermute x12 -> x10, waiting for transfers between devices: 6.99 us -> 11.7 us  [swap(): return lax.ppermute(block, axis, swaps(lax.axis_size(axis), start))]
    squeeze x5 -> x0, local copies, waits for them, and re-layouts: 1.2 us -> none  [the longest x1 1.11 us: shards(): edge_out[t]]
  transfers between devices with their start and end apart: 12 -> 10, of which waited for: 7 -> 5; matrix products, arithmetic and copies ran while one was open for 1% -> 0% of each run, Pallas kernels for 0% -> 0%
where the time goes in v2:
time: 81.8 us; the launch traced here: 81 us
  starting transfers between devices  32.3 us (39%)
  Pallas kernels  28.6 us (35%)
  waiting for transfers between devices  11.7 us (14%)
  local copies, waits for them, and re-layouts  7.54 us (9%)
  between operations  0.85 us (1%)
    ppermute x10, starting transfers between devices, swap(): return lax.ppermute(block, axis, swaps(lax.axis_size(axis), start))  32.3 us
    pallas_call x6, Pallas kernels, run(): pl.pallas_call(kernel, out_shape=[jax.ShapeDtypeStruct(shape, dtype) for...  28.6 us
    ppermute x10, waiting for transfers between devices, swap(): return lax.ppermute(block, axis, swaps(lax.axis_size(axis), start))  11.7 us
    unnamed x42, local copies, waits for them, and re-layouts  7.54 us
  transfers between devices with their start and end apart: 10, of which 5 were waited for; matrix products, arithmetic and copies ran while one was open for 0% of the time, Pallas kernels for 0%

profile of v2, /device:TPU:17, one launch (start us, length us, event | category | flops | bytes accessed | tf_op | source)
XLA Modules:
  0.0 81.0 jit_solution(147548465509092124)
XLA Ops:
  0.6 0.8 copy.18.features
  1.5 0.8 copy-done.11
  2.2 0.7 copy-done.13
  2.9 0.7 copy-done.16
  4.2 1.3 %collective-permute-start = (bf16[2,128,128]{2,1,0:T(8,128)(2,1)S(1)}, bf16[2,128,128]{2,1,0:T(8,128)(2,1)S(1)}, u32[]{:S(2)}, u32[]{:S(2)}) collective-permute-start(bf16[2,128,128]{2,1,0:T(8,128)(2,1)S(1)} %get-tuple-element.18), channel_id=1, source_target_pairs={{0,4},{4,0},{8,12},{12,8},{16,20},{20,16},{24,28},{28,24},{32,36},... | collective-permute-start | bytes 196616 | tf_op jit(solution)/shard_map/ppermute | solution.py:295
  5.5 8.8 %collective-permute-start.1 = (bf16[2,128,128]{2,1,0:T(8,128)(2,1)S(1)}, bf16[2,128,128]{2,1,0:T(8,128)(2,1)S(1)}, u32[]{:S(2)}, u32[]{:S(2)}) collective-permute-start(bf16[2,128,128]{2,1,0:T(8,128)(2,1)S(1)} %get-tuple-element.19), channel_id=1, source_target_pairs={{4,8},{8,4},{12,16},{16,12},{20,24},{24,20},{28,32},{32,28},{36,40... | collective-permute-start | bytes 196616 | tf_op jit(solution)/shard_map/ppermute | solution.py:295
  14.3 1.9 %collective-permute-done.1.got_b = bf16[2,128,128]{2,1,0:T(8,128)(2,1)S(1)} collective-permute-done((bf16[2,128,128]{2,1,0:T(8,128)(2,1)S(1)}, bf16[2,128,128]{2,1,0:T(8,128)(2,1)S(1)}, u32[]{:S(2)}, u32[]{:S(2)}) %collective-permute-start.1) | collective-permute-done | bytes 65568 | tf_op jit(solution)/shard_map/ppermute | solution.py:295
  16.2 2.2 %collective-permute-start.2 = (bf16[6,48,128]{2,1,0:T(8,128)(2,1)S(1)}, bf16[6,48,128]{2,1,0:T(8,128)(2,1)S(1)}, u32[]{:S(2)}, u32[]{:S(2)}) collective-permute-start(bf16[6,48,128]{2,1,0:T(8,128)(2,1)S(1)} %get-tuple-element.20), channel_id=1, source_target_pairs={{0,1},{1,0},{2,3},{3,2},{4,5},{5,4},{6,7},{7,6},{8,9},{9,8},{10,11... | collective-permute-start | bytes 221192 | tf_op jit(solution)/shard_map/ppermute | solution.py:295
  18.4 3.1 %collective-permute-start.3 = (bf16[6,48,128]{2,1,0:T(8,128)(2,1)S(1)}, bf16[6,48,128]{2,1,0:T(8,128)(2,1)S(1)}, u32[]{:S(2)}, u32[]{:S(2)}) collective-permute-start(bf16[6,48,128]{2,1,0:T(8,128)(2,1)S(1)} %get-tuple-element.21), channel_id=1, source_target_pairs={{1,2},{2,1},{5,6},{6,5},{9,10},{10,9},{13,14},{14,13},{17,18},{18,... | collective-permute-start | bytes 221192 | tf_op jit(solution)/shard_map/ppermute | solution.py:295
  21.6 2.5 %collective-permute-done.3.got_d = bf16[6,48,128]{2,1,0:T(8,128)(2,1)S(1)} collective-permute-done((bf16[6,48,128]{2,1,0:T(8,128)(2,1)S(1)}, bf16[6,48,128]{2,1,0:T(8,128)(2,1)S(1)}, u32[]{:S(2)}, u32[]{:S(2)}) %collective-permute-start.3) | collective-permute-done | bytes 73760 | tf_op jit(solution)/shard_map/ppermute | solution.py:295
  24.1 1.0 %copy-done = bf16[3,128,512]{2,1,0:T(8,128)(2,1)S(1)} copy-done((bf16[3,128,512]{2,1,0:T(8,128)(2,1)S(1)}, bf16[3,128,512]{2,1,0:T(8,128)(2,1)}, u32[]{:S(2)}) %copy-start) | copy-done | bytes 393240
  25.1 1.0 %copy-done.2 = bf16[3,128,512]{2,1,0:T(8,128)(2,1)S(1)} copy-done((bf16[3,128,512]{2,1,0:T(8,128)(2,1)S(1)}, bf16[3,128,512]{2,1,0:T(8,128)(2,1)}, u32[]{:S(2)}) %copy-start.2) | copy-done | bytes 393240
  26.1 1.0 %copy-done.4 = bf16[3,512,128]{2,1,0:T(8,128)(2,1)S(1)} copy-done((bf16[3,512,128]{2,1,0:T(8,128)(2,1)S(1)}, bf16[3,512,128]{2,1,0:T(8,128)(2,1)}, u32[]{:S(2)}) %copy-start.4) | copy-done | bytes 393240
  27.1 0.8 copy-done.12
  27.8 0.7 copy-done.15
  28.5 14.7 %first_step.1 = (bf16[4,2,128,128]{3,2,1,0:T(8,128)(2,1)S(1)}, bf16[8,16,2048]{2,1,0:T(8,128)(2,1)S(1)}, bf16[4,128,128]{2,1,0:T(8,128)(2,1)S(1)}, bf16[4,128,128]{2,1,0:T(8,128)(2,1)S(1)}) custom-call(bf16[2,2,48,128]{3,2,1,0:T(8,128)(2,1)S(1)} %get-tuple-element.17.own, bf16[2,128,128]{2,1,0:T(8,128)(2,1)S(1)} %collective-permute-done.got_a, ...), custom_call_target="tpu_custom_call" | custom-call | tf_op jit(solution)/shard_map/first_step/pallas_call | solution.py:276
  43.4 3.1 %collective-permute-start.5 = (bf16[4,128,128]{2,1,0:T(8,128)(2,1)S(1)}, bf16[4,128,128]{2,1,0:T(8,128)(2,1)S(1)}, u32[]{:S(2)}, u32[]{:S(2)}) collective-permute-start(bf16[4,128,128]{2,1,0:T(8,128)(2,1)S(1)} %get-tuple-element.25), channel_id=1, source_target_pairs={{1,2},{2,1},{5,6},{6,5},{9,10},{10,9},{13,14},{14,13},{17,18},{18,... | collective-permute-start | bytes 393224 | tf_op jit(solution)/shard_map/ppermute | solution.py:295
  46.5 3.1 %collective-permute-done.5.got_d = bf16[4,128,128]{2,1,0:T(8,128)(2,1)S(1)} collective-permute-done((bf16[4,128,128]{2,1,0:T(8,128)(2,1)S(1)}, bf16[4,128,128]{2,1,0:T(8,128)(2,1)S(1)}, u32[]{:S(2)}, u32[]{:S(2)}) %collective-permute-start.5) | collective-permute-done | bytes 131104 | tf_op jit(solution)/shard_map/ppermute | solution.py:295
  49.7 5.9 %middle_step.1 = (bf16[2,2,128,128]{3,2,1,0:T(8,128)(2,1)S(1)}, bf16[2,128,128]{2,1,0:T(8,128)(2,1)S(1)}, bf16[2,128,128]{2,1,0:T(8,128)(2,1)S(1)}) custom-call(bf16[4,2,128,128]{3,2,1,0:T(8,128)(2,1)S(1)} %get-tuple-element.23.wide, bf16[4,128,128]{2,1,0:T(8,128)(2,1)S(1)} %collective-permute-done.4.got_c, ...), custom_call_target="tpu_custom_call" | custom-call | tf_op jit(solution)/shard_map/middle_step/pallas_call | solution.py:276
  55.7 8.9 %collective-permute-start.7 = (bf16[2,128,128]{2,1,0:T(8,128)(2,1)S(1)}, bf16[2,128,128]{2,1,0:T(8,128)(2,1)S(1)}, u32[]{:S(2)}, u32[]{:S(2)}) collective-permute-start(bf16[2,128,128]{2,1,0:T(8,128)(2,1)S(1)} %get-tuple-element.29), channel_id=1, source_target_pairs={{4,8},{8,4},{12,16},{16,12},{20,24},{24,20},{28,32},{32,28},{36,40... | collective-permute-start | bytes 196616 | tf_op jit(solution)/shard_map/ppermute | solution.py:295
  64.6 1.8 %collective-permute-done.7.got_b = bf16[2,128,128]{2,1,0:T(8,128)(2,1)S(1)} collective-permute-done((bf16[2,128,128]{2,1,0:T(8,128)(2,1)S(1)}, bf16[2,128,128]{2,1,0:T(8,128)(2,1)S(1)}, u32[]{:S(2)}, u32[]{:S(2)}) %collective-permute-start.7) | collective-permute-done | bytes 65568 | tf_op jit(solution)/shard_map/ppermute | solution.py:295
  66.6 4.5 %collective-permute-start.9 = (bf16[4,128,128]{2,1,0:T(8,128)(2,1)S(1)}, bf16[4,128,128]{2,1,0:T(8,128)(2,1)S(1)}, u32[]{:S(2)}, u32[]{:S(2)}) collective-permute-start(bf16[4,128,128]{2,1,0:T(8,128)(2,1)S(1)} %get-tuple-element.31), channel_id=1, source_target_pairs={{1,2},{2,1},{5,6},{6,5},{9,10},{10,9},{13,14},{14,13},{17,18},{18,... | collective-permute-start | bytes 393224 | tf_op jit(solution)/shard_map/ppermute | solution.py:295
  71.3 2.3 %collective-permute-done.9.got_d = bf16[4,128,128]{2,1,0:T(8,128)(2,1)S(1)} collective-permute-done((bf16[4,128,128]{2,1,0:T(8,128)(2,1)S(1)}, bf16[4,128,128]{2,1,0:T(8,128)(2,1)S(1)}, u32[]{:S(2)}, u32[]{:S(2)}) %collective-permute-start.9) | collective-permute-done | bytes 131104 | tf_op jit(solution)/shard_map/ppermute | solution.py:295
  73.6 7.4 %last_step.1 = (f32[2,2,2,128]{3,2,1,0:T(2,128)}, f32[2,2,2,128]{3,2,1,0:T(2,128)}) custom-call(bf16[2,2,128,128]{3,2,1,0:T(8,128)(2,1)S(1)} %get-tuple-element.27.own, bf16[2,128,128]{2,1,0:T(8,128)(2,1)S(1)} %collective-permute-done.6.got_a, bf16[2,128,128]{2,1,0:T(8,128)(2,1)S(1)} %collective-permute-done.7.got_b, ...), custom_call_target="tpu_custom_call" | custom-call | tf_op jit(solution)/shard_map/last_step/pallas_call | solution.py:276
  (44 shorter events, 1.1 us)
Async XLA Ops:
  0.6 23.4 %copy-start.6 = (bf16[3,256,128]{2,1,0:T(8,128)(2,1)S(1)}, bf16[3,256,128]{2,1,0:T(8,128)(2,1)}, u32[]{:S(2)}) copy-start(bf16[3,256,128]{2,1,0:T(8,128)(2,1)} %first_w.5) | copy-start | bytes 589828
  4.2 19.9 %copy-start.7 = (bf16[3,128,128]{2,1,0:T(8,128)(2,1)S(1)}, bf16[3,128,128]{2,1,0:T(8,128)(2,1)}, u32[]{:S(2)}) copy-start(bf16[3,128,128]{2,1,0:T(8,128)(2,1)} %second_w.5) | copy-start | bytes 294916
  4.2 10.1 %collective-permute-start = (bf16[2,128,128]{2,1,0:T(8,128)(2,1)S(1)}, bf16[2,128,128]{2,1,0:T(8,128)(2,1)S(1)}, u32[]{:S(2)}, u32[]{:S(2)}) collective-permute-start(bf16[2,128,128]{2,1,0:T(8,128)(2,1)S(1)} %get-tuple-element.18), channel_id=1, source_target_pairs={{0,4},{4,0},{8,12},{12,8},{16,20},{20,16},{24,28},{28,24},{32,36},... | collective-permute-start | bytes 196616 | tf_op jit(solution)/shard_map/ppermute | solution.py:295
  5.5 10.7 %collective-permute-start.1 = (bf16[2,128,128]{2,1,0:T(8,128)(2,1)S(1)}, bf16[2,128,128]{2,1,0:T(8,128)(2,1)S(1)}, u32[]{:S(2)}, u32[]{:S(2)}) collective-permute-start(bf16[2,128,128]{2,1,0:T(8,128)(2,1)S(1)} %get-tuple-element.19), channel_id=1, source_target_pairs={{4,8},{8,4},{12,16},{16,12},{20,24},{24,20},{28,32},{32,28},{36,40... | collective-permute-start | bytes 196616 | tf_op jit(solution)/shard_map/ppermute | solution.py:295
  16.2 7.9 %copy-start.8 = (f32[3,3,512]{2,1,0:T(4,128)S(1)}, f32[3,3,512]{2,1,0:T(4,128)}, u32[]{:S(2)}) copy-start(f32[3,3,512]{2,1,0:T(4,128)} %geo_w.5) | copy-start | bytes 55300
  16.2 5.3 %collective-permute-start.2 = (bf16[6,48,128]{2,1,0:T(8,128)(2,1)S(1)}, bf16[6,48,128]{2,1,0:T(8,128)(2,1)S(1)}, u32[]{:S(2)}, u32[]{:S(2)}) collective-permute-start(bf16[6,48,128]{2,1,0:T(8,128)(2,1)S(1)} %get-tuple-element.20), channel_id=1, source_target_pairs={{0,1},{1,0},{2,3},{3,2},{4,5},{5,4},{6,7},{7,6},{8,9},{9,8},{10,11... | collective-permute-start | bytes 221192 | tf_op jit(solution)/shard_map/ppermute | solution.py:295
  18.4 5.7 %collective-permute-start.3 = (bf16[6,48,128]{2,1,0:T(8,128)(2,1)S(1)}, bf16[6,48,128]{2,1,0:T(8,128)(2,1)S(1)}, u32[]{:S(2)}, u32[]{:S(2)}) collective-permute-start(bf16[6,48,128]{2,1,0:T(8,128)(2,1)S(1)} %get-tuple-element.21), channel_id=1, source_target_pairs={{1,2},{2,1},{5,6},{6,5},{9,10},{10,9},{13,14},{14,13},{17,18},{18,... | collective-permute-start | bytes 221192 | tf_op jit(solution)/shard_map/ppermute | solution.py:295
  24.1 1.0 %copy-start = (bf16[3,128,512]{2,1,0:T(8,128)(2,1)S(1)}, bf16[3,128,512]{2,1,0:T(8,128)(2,1)}, u32[]{:S(2)}) copy-start(bf16[3,128,512]{2,1,0:T(8,128)(2,1)} %recv_w.5) | copy-start | bytes 1179652
  25.1 1.0 %copy-start.2 = (bf16[3,128,512]{2,1,0:T(8,128)(2,1)S(1)}, bf16[3,128,512]{2,1,0:T(8,128)(2,1)}, u32[]{:S(2)}) copy-start(bf16[3,128,512]{2,1,0:T(8,128)(2,1)} %send_w.5) | copy-start | bytes 1179652
  26.1 1.0 %copy-start.4 = (bf16[3,512,128]{2,1,0:T(8,128)(2,1)S(1)}, bf16[3,512,128]{2,1,0:T(8,128)(2,1)}, u32[]{:S(2)}) copy-start(bf16[3,512,128]{2,1,0:T(8,128)(2,1)} %out_w.5) | copy-start | bytes 1179652
  28.5 21.1 %copy-start.1 = (bf16[3,128,512]{2,1,0:T(8,128)(2,1)S(1)}, bf16[3,128,512]{2,1,0:T(8,128)(2,1)}, u32[]{:S(2)}) copy-start(bf16[3,128,512]{2,1,0:T(8,128)(2,1)} %recv_w.5) | copy-start | bytes 1179652
  28.5 21.1 %copy-start.3 = (bf16[3,128,512]{2,1,0:T(8,128)(2,1)S(1)}, bf16[3,128,512]{2,1,0:T(8,128)(2,1)}, u32[]{:S(2)}) copy-start(bf16[3,128,512]{2,1,0:T(8,128)(2,1)} %send_w.5) | copy-start | bytes 1179652
  28.5 21.1 %copy-start.5 = (bf16[3,512,128]{2,1,0:T(8,128)(2,1)S(1)}, bf16[3,512,128]{2,1,0:T(8,128)(2,1)}, u32[]{:S(2)}) copy-start(bf16[3,512,128]{2,1,0:T(8,128)(2,1)} %out_w.5) | copy-start | bytes 1179652
  43.3 3.3 %collective-permute-start.4 = (bf16[4,128,128]{2,1,0:T(8,128)(2,1)S(1)}, bf16[4,128,128]{2,1,0:T(8,128)(2,1)S(1)}, u32[]{:S(2)}, u32[]{:S(2)}) collective-permute-start(bf16[4,128,128]{2,1,0:T(8,128)(2,1)S(1)} %get-tuple-element.24), channel_id=1, source_target_pairs={{0,1},{1,0},{2,3},{3,2},{4,5},{5,4},{6,7},{7,6},{8,9},{9,8},{10,11... | collective-permute-start | bytes 393224 | tf_op jit(solution)/shard_map/ppermute | solution.py:295
  43.4 6.3 %collective-permute-start.5 = (bf16[4,128,128]{2,1,0:T(8,128)(2,1)S(1)}, bf16[4,128,128]{2,1,0:T(8,128)(2,1)S(1)}, u32[]{:S(2)}, u32[]{:S(2)}) collective-permute-start(bf16[4,128,128]{2,1,0:T(8,128)(2,1)S(1)} %get-tuple-element.25), channel_id=1, source_target_pairs={{1,2},{2,1},{5,6},{6,5},{9,10},{10,9},{13,14},{14,13},{17,18},{18,... | collective-permute-start | bytes 393224 | tf_op jit(solution)/shard_map/ppermute | solution.py:295
  55.6 9.0 %collective-permute-start.6 = (bf16[2,128,128]{2,1,0:T(8,128)(2,1)S(1)}, bf16[2,128,128]{2,1,0:T(8,128)(2,1)S(1)}, u32[]{:S(2)}, u32[]{:S(2)}) collective-permute-start(bf16[2,128,128]{2,1,0:T(8,128)(2,1)S(1)} %get-tuple-element.28), channel_id=1, source_target_pairs={{0,4},{4,0},{8,12},{12,8},{16,20},{20,16},{24,28},{28,24},{32,36},... | collective-permute-start | bytes 196616 | tf_op jit(solution)/shard_map/ppermute | solution.py:295
  55.7 10.7 %collective-permute-start.7 = (bf16[2,128,128]{2,1,0:T(8,128)(2,1)S(1)}, bf16[2,128,128]{2,1,0:T(8,128)(2,1)S(1)}, u32[]{:S(2)}, u32[]{:S(2)}) collective-permute-start(bf16[2,128,128]{2,1,0:T(8,128)(2,1)S(1)} %get-tuple-element.29), channel_id=1, source_target_pairs={{4,8},{8,4},{12,16},{16,12},{20,24},{24,20},{28,32},{32,28},{36,40... | collective-permute-start | bytes 196616 | tf_op jit(solution)/shard_map/ppermute | solution.py:295
  66.4 4.7 %copy-start.19 = (bf16[128,2]{0,1:T(2,128)(2,1)S(1)}, bf16[128,2]{0,1:T(2,128)(2,1)}, u32[]{:S(2)}) copy-start(bf16[128,2]{0,1:T(2,128)(2,1)} %param.31) | copy-start | bytes 1540
  66.4 7.2 %copy-start.17 = (s32[2,2]{1,0:T(2,128)S(1)}, s32[2,2]{1,0:T(2,128)}, u32[]{:S(2)}) copy-start(s32[2,2]{1,0:T(2,128)} %occupancy.3) | copy-start | bytes 52
  66.4 7.2 %copy-start.18 = (f32[2,2,2,128]{3,2,1,0:T(2,128)S(1)}, f32[2,2,2,128]{3,2,1,0:T(2,128)}, u32[]{:S(2)}) copy-start(f32[2,2,2,128]{3,2,1,0:T(2,128)} %velocity.1) | copy-start | bytes 12292
  66.5 7.1 %copy-start.9 = (bf16[128,128]{1,0:T(8,128)(2,1)S(1)}, bf16[128,128]{1,0:T(8,128)(2,1)}, u32[]{:S(2)}) copy-start(bf16[128,128]{1,0:T(8,128)(2,1)} %dec_first.1) | copy-start | bytes 98308
  66.5 4.8 %collective-permute-start.8 = (bf16[4,128,128]{2,1,0:T(8,128)(2,1)S(1)}, bf16[4,128,128]{2,1,0:T(8,128)(2,1)S(1)}, u32[]{:S(2)}, u32[]{:S(2)}) collective-permute-start(bf16[4,128,128]{2,1,0:T(8,128)(2,1)S(1)} %get-tuple-element.30), channel_id=1, source_target_pairs={{0,1},{1,0},{2,3},{3,2},{4,5},{5,4},{6,7},{7,6},{8,9},{9,8},{10,11... | collective-permute-start | bytes 393224 | tf_op jit(solution)/shard_map/ppermute | solution.py:295
  66.6 7.0 %copy-start.14 = (f32[2,2,2,128]{3,2,1,0:T(2,128)S(1)}, f32[2,2,2,128]{3,2,1,0:T(2,128)}, u32[]{:S(2)}) copy-start(f32[2,2,2,128]{3,2,1,0:T(2,128)} %position.3) | copy-start | bytes 12292
  66.6 7.0 %collective-permute-start.9 = (bf16[4,128,128]{2,1,0:T(8,128)(2,1)S(1)}, bf16[4,128,128]{2,1,0:T(8,128)(2,1)S(1)}, u32[]{:S(2)}, u32[]{:S(2)}) collective-permute-start(bf16[4,128,128]{2,1,0:T(8,128)(2,1)S(1)} %get-tuple-element.31), channel_id=1, source_target_pairs={{1,2},{2,1},{5,6},{6,5},{9,10},{10,9},{13,14},{14,13},{17,18},{18,... | collective-permute-start | bytes 393224 | tf_op jit(solution)/shard_map/ppermute | solution.py:295
  (6 other events, 4.4 us)

commit v3 on v2

v3 whole, which is shorter than its diff:
```python
import functools

import jax
import jax.numpy as jnp
from jax import lax
from jax.experimental import pallas as pl
from jax.experimental.pallas import tpu as pltpu
from jax.sharding import PartitionSpec as P

time_step = 0.5
LAT = 128
EH = 512
INF = 30
KNB = 16
SLOTS = 128
PACK = 48
GEO = 16
WIDE = 8
BLOCKED = -(2.0**40)
bf16 = jnp.bfloat16
f32 = jnp.float32
i32 = jnp.int32


def tdot(left, right):
    return lax.dot_general(left, right, (((0,), (0,)), ((), ())), preferred_element_type=f32)


def split3(values):
    high = values.astype(bf16).astype(f32)
    rest = values - high
    mid = rest.astype(bf16).astype(f32)
    return [high, mid, rest - mid]


def norm_rows(values):
    center = values - jnp.mean(values, axis=0, keepdims=True)
    spread = jnp.mean(center * center, axis=0, keepdims=True)
    return center * lax.rsqrt(spread + 1e-05)


def parities():
    return lax.rem(lax.axis_index("slab"), 2), lax.rem(lax.axis_index("cross"), 2)


def lane_rows(values, first, count):
    return jnp.concatenate([values[k : k + 1] for k in range(first, first + count)], axis=1)


def repeated(values, count):
    return jnp.concatenate([values] * count, axis=1)


def prepare_kernel(features_in, position_in, occupancy_in, codes_in, mask_in, raw, own_codes, send_a, send_b,
                   features, position, occupancy, codes, mask, sems):
    pairs = ((features_in, features), (position_in, position), (occupancy_in, occupancy), (codes_in, codes), (mask_in, mask))
    copies = [pltpu.make_async_copy(source, target, sems.at[k]) for k, (source, target) in enumerate(pairs)]
    for copy in copies:
        copy.start()
    p, q = parities()
    lane = lax.broadcasted_iota(i32, (1, SLOTS), 1)
    for copy in copies:
        copy.wait()
    for a in range(2):
        for c in range(2):
            live = (lane < occupancy[a, c]).astype(f32)
            rows = [features[a, c].astype(f32), jnp.zeros((2, SLOTS), f32)]
            rows += split3(position[a, c, 0:1]) + split3(position[a, c, 1:2])
            rows += [live, jnp.zeros((PACK - 39, SLOTS), f32)]
            raw[a, c] = jnp.concatenate(rows, axis=0).astype(bf16)
            own_codes[a, c] = jnp.where(mask[a, c] > 0, codes[a, c], (codes[a, c] & (SLOTS - 1)) - SLOTS)
    for near, far, out in ((1 - p, p, send_a), (p, 1 - p, send_b)):
        for c in range(2):
            out[c, 0:PACK] = raw[near, c]
            out[c, PACK : 2 * PACK] = raw[far, c]
            code = own_codes[near, c]
            out[c, 2 * PACK : 2 * PACK + KNB] = (code >> 7).astype(f32).astype(bf16)
            out[c, 2 * PACK + KNB :] = (code & (SLOTS - 1)).astype(f32).astype(bf16)


def weights_kernel(token, *refs):
    sources, outs, (geo_w, sems) = refs[:9], refs[9:17], refs[17:]
    full_w = outs[0]
    targets = (full_w.at[:, 0:LAT, :], geo_w, *outs[1:])
    copies = [pltpu.make_async_copy(source, target, sems.at[k]) for k, (source, target) in enumerate(zip(sources, targets))]
    for copy in copies:
        copy.start()
    for copy in copies:
        copy.wait()
    for t in range(full_w.shape[0]):
        values = geo_w[t]
        high = values.astype(bf16).astype(f32)
        low = values - high
        rows = []
        for c in range(3):
            rows += [high[c : c + 1], high[c : c + 1], low[c : c + 1], low[c : c + 1]]
        rows.append(jnp.full((1, EH), BLOCKED, f32))
        rows.append(jnp.zeros((GEO - 13, EH), f32))
        full_w[t, LAT:, :] = jnp.concatenate(rows, axis=0).astype(bf16)


def pack_raw_kernel(own, got_a, got_b, send_c, send_d):
    p, q = parities()
    for j, out in ((1 - q, send_c), (q, send_d)):
        out[2] = own[0, j]
        out[3] = own[1, j]
        for side, got in ((1 - p, got_a), (p, got_b)):
            out[1 + 3 * side] = got[j, 0:PACK]
            out[5 * side] = got[j, PACK : 2 * PACK]


def pack_kernel(own, got_a, got_b, send_c, send_d):
    p, q = parities()
    for j, out in ((1 - q, send_c), (q, send_d)):
        out[1] = own[0, j]
        out[2] = own[1, j]
        out[3 * (1 - p)] = got_a[j]
        out[3 * p] = got_b[j]


def one_hot(codes, windows):
    wide = codes.shape[1]
    window = codes >> 7
    slot = codes & (SLOTS - 1)
    iota = lax.broadcasted_iota(i32, (SLOTS, wide), 0).astype(jnp.int16)
    parts = []
    for w in windows:
        wanted = jnp.where(window == w, slot, -1).astype(jnp.int16)
        hit = iota == jnp.broadcast_to(wanted, (SLOTS, wide))
        parts.append(jnp.where(hit, jnp.ones((), bf16), jnp.zeros((), bf16)))
    return jnp.concatenate(parts, axis=0)


def geometry_rows(got, own_x, own_y, own_live):
    delta_x = got[0:1] + got[1:2] + got[2:3] - own_x
    delta_y = got[3:4] + got[4:5] + got[5:6] - own_y
    distance = delta_x * delta_x + delta_y * delta_y
    pieces = []
    for v in (delta_x, delta_y, distance):
        high = v.astype(bf16).astype(f32)
        pieces += [high, v - high, high, v - high]
    pieces.append(1.0 - own_live * got[6:7])
    pieces.append(jnp.zeros((GEO - 13, got.shape[1]), f32))
    return jnp.concatenate(pieces, axis=0).astype(bf16)


def edge_sum(full_w, right_side, bound, total):
    hidden = tdot(full_w, right_side)
    for k in range(right_side.shape[1] // SLOTS):
        part = jnp.maximum(hidden[:, k * SLOTS : (k + 1) * SLOTS], bound)
        total = part if total is None else total + part
    return total


def node_update(own_all, sums, out_w, first_w, second_w):
    summed = tdot(out_w, sums).astype(bf16)
    joined = tdot(first_w, jnp.concatenate([own_all, summed], axis=0))
    joined = jnp.maximum(joined, 0.0).astype(bf16)
    update = norm_rows(tdot(second_w, joined))
    return (own_all.astype(f32) + update).astype(bf16)


def encoded(rows, enc_first, enc_second):
    weight = jnp.concatenate([enc_first[...], jnp.zeros((PACK - INF, LAT), bf16)], axis=0)
    raw = jnp.concatenate(rows, axis=1)
    hidden = jnp.maximum(tdot(weight, raw), 0.0).astype(bf16)
    return norm_rows(tdot(enc_second[...], hidden)).astype(bf16)


def encode_kernel(own, got_a, got_b, own_codes, enc_first, enc_second, recv_w, pack, codes_all, latents, bounds):
    p, q = parities()
    for c in range(2):
        for a in range(2):
            pack[2 + a, c] = own[a, c]
            codes_all[1 + a, c] = own_codes[a, c]
        for side, got in ((1 - p, got_a), (p, got_b)):
            pack[1 + 3 * side, c] = got[c, 0:PACK]
            pack[5 * side, c] = got[c, PACK : 2 * PACK]
            window = got[c, 2 * PACK : 2 * PACK + KNB].astype(f32)
            slot = got[c, 2 * PACK + KNB :].astype(f32)
            codes_all[3 * side, c] = (window * SLOTS + slot).astype(i32)
    for i in range(0, 6, 2):
        latent = encoded([pack[i + j // 2, j % 2] for j in range(4)], enc_first, enc_second)
        for j in range(4):
            latents[i + j // 2, j % 2] = latent[:, j * SLOTS : (j + 1) * SLOTS]
    own_all = jnp.concatenate([latents[1 + b // 2, b % 2] for b in range(8)], axis=1)
    bounds[...] = -tdot(recv_w[0], own_all)


def first_kernel(
    pack_own, codes_all, latents, bounds, got_c, got_d, enc_first, enc_second, full_w, out_w, first_w, second_w,
    latent_out, geo_out, send_c, send_d, pack, win, sums,
):
    p, q = parities()
    for i in range(6):
        for c in range(2):
            pack[i, 1 + c] = pack_own[i, c]
            win[i, 1 + c] = latents[i, c]
        pack[i, 3 * (1 - q)] = got_c[i]
        pack[i, 3 * q] = got_d[i]
    for i in range(0, 6, 2):
        latent = encoded([pack[i + j // 2, 3 * (j % 2)] for j in range(4)], enc_first, enc_second)
        for j in range(4):
            win[i + j // 2, 3 * (j % 2)] = latent[:, j * SLOTS : (j + 1) * SLOTS]

    def one_bin(b, carry):
        a, c = lax.div(b, 2), lax.rem(b, 2)
        codes = codes_all[a, c]
        lats = jnp.concatenate([win[a + w // 3, c + w % 3] for w in range(9)], axis=1)
        geos = jnp.concatenate([pack[a + w // 3, c + w % 3, 32:PACK, :] for w in range(9)], axis=1)
        stacked = jnp.concatenate([lats, geos], axis=0)
        me = pack[a + 1, c + 1, 32:PACK, :].astype(f32)
        own_x = repeated(me[0:1] + me[1:2] + me[2:3], WIDE)
        own_y = repeated(me[3:4] + me[4:5] + me[5:6], WIDE)
        own_live = repeated(me[6:7], WIDE)
        columns = pl.ds(pl.multiple_of(b * SLOTS, SLOTS), SLOTS)
        bound = bounds[:, columns]
        total = None
        for part in range(KNB // WIDE):
            hot = one_hot(lane_rows(codes, part * WIDE, WIDE), range(9))
            got = jnp.dot(stacked, hot, preferred_element_type=f32)
            geo = geometry_rows(got[LAT:], own_x, own_y, own_live)
            geo_out[b, :, part * WIDE * SLOTS : (part + 1) * WIDE * SLOTS] = geo
            total = edge_sum(full_w[0], jnp.concatenate([got[:LAT].astype(bf16), geo], axis=0), bound, total)
        sums[:, columns] = (total - KNB * bound).astype(bf16)
        return carry

    lax.fori_loop(0, 8, one_bin, 0)
    own_all = jnp.concatenate([win[1 + b // 2, 1 + b % 2] for b in range(8)], axis=1)
    latent = node_update(own_all, sums[...], out_w[0], first_w[0], second_w[0])
    for b in range(8):
        latent_out[b // 2, b % 2] = latent[:, b * SLOTS : (b + 1) * SLOTS]
    for i in range(4):
        send_c[i] = latent_out[i, 1 - q]
        send_d[i] = latent_out[i, q]


def inner_windows(c):
    return [w for w in range(9) if c + w % 3 in (1, 2)]


def outer_windows(c):
    return [w for w in range(9) if c + w % 3 in (0, 3)]


def early_part(t, win, own_codes, recv_w, gathered, bounds):
    own_all = jnp.concatenate([win[1 + b // 2, b % 2] for b in range(4)], axis=1)
    bounds[...] = -tdot(recv_w[t], own_all)
    for b in range(4):
        a, c = b // 2, b % 2
        windows = inner_windows(c)
        lats = jnp.concatenate([win[a + w // 3, c + w % 3 - 1] for w in windows], axis=1)
        for part in range(KNB // WIDE):
            hot = one_hot(lane_rows(own_codes[a, c], part * WIDE, WIDE), windows)
            got = jnp.dot(lats, hot, preferred_element_type=f32).astype(bf16)
            gathered[b, :, part * WIDE * SLOTS : (part + 1) * WIDE * SLOTS] = got


def middle_early_kernel(wide, own_codes, recv_w, gathered, bounds):
    early_part(1, wide, own_codes, recv_w, gathered, bounds)


def last_early_kernel(own, got_a, got_b, own_codes, recv_w, gathered, bounds, win):
    p, q = parities()
    for c in range(2):
        win[1, c] = own[0, c]
        win[2, c] = own[1, c]
        win[3 * (1 - p), c] = got_a[c]
        win[3 * p, c] = got_b[c]
    early_part(2, win, own_codes, recv_w, gathered, bounds)


def late_part(t, own_all, got_c, got_d, own_codes, geo, gathered, bounds, full_w, out_w, first_w, second_w, edge, sums):
    p, q = parities()
    for i in range(4):
        edge[1 - q, i] = got_c[i]
        edge[q, i] = got_d[i]
    for b in range(4):
        a, c = b // 2, b % 2
        windows = outer_windows(c)
        lats = jnp.concatenate([edge[c, a + w // 3] for w in windows], axis=1)
        bound = bounds[:, b * SLOTS : (b + 1) * SLOTS]
        total = None
        for part in range(KNB // WIDE):
            columns = slice(part * WIDE * SLOTS, (part + 1) * WIDE * SLOTS)
            hot = one_hot(lane_rows(own_codes[a, c], part * WIDE, WIDE), windows)
            got = jnp.dot(lats, hot, preferred_element_type=f32).astype(bf16) + gathered[b, :, columns]
            total = edge_sum(full_w[t], jnp.concatenate([got, geo[2 + b, :, columns]], axis=0), bound, total)
        sums[:, b * SLOTS : (b + 1) * SLOTS] = (total - KNB * bound).astype(bf16)
    return node_update(own_all, sums[...], out_w[t], first_w[t], second_w[t])


def middle_kernel(
    wide, got_c, got_d, own_codes, geo, gathered, bounds, full_w, out_w, first_w, second_w,
    latent_out, send_a, send_b, edge, sums,
):
    p, q = parities()
    own_all = jnp.concatenate([wide[1 + b // 2, b % 2] for b in range(4)], axis=1)
    latent = late_part(1, own_all, got_c, got_d, own_codes, geo, gathered, bounds, full_w, out_w, first_w, second_w, edge, sums)
    for b in range(4):
        latent_out[b // 2, b % 2] = latent[:, b * SLOTS : (b + 1) * SLOTS]
    for c in range(2):
        send_a[c] = latent_out[1 - p, c]
        send_b[c] = latent_out[p, c]


def last_kernel(
    own, got_c, got_d, own_codes, geo, gathered, bounds, full_w, out_w, first_w, second_w,
    raw, position, velocity, dec_first, dec_second, out_velocity, out_position, edge, sums,
):
    own_all = jnp.concatenate([own[b // 2, b % 2] for b in range(4)], axis=1)
    latent = late_part(2, own_all, got_c, got_d, own_codes, geo, gathered, bounds, full_w, out_w, first_w, second_w, edge, sums)
    hidden = jnp.maximum(tdot(dec_first[...], latent), 0.0).astype(bf16)
    accel = tdot(dec_second[...], hidden)
    for b in range(4):
        a, c = b // 2, b % 2
        live = raw[a, c, 32:PACK].astype(f32)[6:7]
        speed = velocity[a, c] + time_step * (accel[:, b * SLOTS : (b + 1) * SLOTS] * live)
        out_velocity[a, c] = speed
        out_position[a, c] = position[a, c] + time_step * speed


def run(kernel, name, out, scratch, operands, outside=(), work=None):
    vmem = pl.BlockSpec(memory_space=pltpu.VMEM)
    far = pl.BlockSpec(memory_space=pltpu.HBM)
    operands = [
        pltpu.with_memory_space_constraint(x, pltpu.HBM) if k in outside else x for k, x in enumerate(operands)
    ]
    return pl.pallas_call(
        kernel,
        out_shape=[jax.ShapeDtypeStruct(shape, dtype) for shape, dtype in out],
        in_specs=[far if k in outside else vmem for k in range(len(operands))],
        out_specs=[vmem] * len(out),
        scratch_shapes=[pltpu.VMEM(*entry) if isinstance(entry, tuple) else entry for entry in scratch],
        compiler_params=pltpu.CompilerParams(vmem_limit_bytes=32 << 20),
        cost_estimate=None if work is None else pl.CostEstimate(flops=work, bytes_accessed=4 << 20, transcendentals=0),
        name=name,
    )(*operands)


def swaps(count, start):
    pairs = []
    for low in range(start, count - 1, 2):
        pairs += [(low, low + 1), (low + 1, low)]
    return pairs


def swap(block, axis, start):
    return lax.ppermute(block, axis, swaps(lax.axis_size(axis), start))


def shards(
    features,
    position,
    velocity,
    occupancy,
    neighbor_codes,
    edge_mask,
    enc_first,
    enc_second,
    edge_recv,
    edge_send,
    edge_geo,
    edge_out,
    node_first,
    node_second,
    dec_first,
    dec_second,
):
    tile = (LAT, SLOTS)
    side = ((2, *tile), bf16)
    column = ((4, *tile), bf16)
    raw_column = ((6, PACK, SLOTS), bf16)
    steps = edge_recv.shape[0]
    whole = lambda values: (values.shape, values.dtype)
    gathered = ((4, LAT, KNB * SLOTS), bf16)
    bounds = ((EH, 4 * SLOTS), f32)

    inputs = (features, position, occupancy, neighbor_codes, edge_mask)
    raw, own_codes, send_a, send_b = run(
        prepare_kernel,
        "prepare",
        [((2, 2, PACK, SLOTS), bf16), ((2, 2, KNB, SLOTS), i32), side, side],
        [
            whole(features),
            whole(position),
            pltpu.SMEM(occupancy.shape, i32),
            whole(neighbor_codes),
            whole(edge_mask),
            pltpu.SemaphoreType.DMA((5,)),
        ],
        inputs,
        range(5),
    )
    got_b, got_a = swap(send_b, "slab", 1), swap(send_a, "slab", 0)
    plain = (edge_recv, edge_out, node_first, node_second, enc_first, enc_second, dec_first)
    full_w, recv_w, out_w, first_w, second_w, enc_one, enc_two, dec_one = run(
        weights_kernel,
        "weights",
        [((steps, LAT + GEO, EH), bf16), *[whole(w) for w in plain]],
        [whole(edge_geo), pltpu.SemaphoreType.DMA((9,))],
        (own_codes, edge_send, edge_geo, *plain),
        range(1, 10),
        1 << 30,
    )
    send_c, send_d = run(pack_raw_kernel, "pack_raw", [raw_column] * 2, [], (raw, got_a, got_b))
    got_d, got_c = swap(send_d, "cross", 1), swap(send_c, "cross", 0)
    pack_own, codes_all, latents, all_bounds = run(
        encode_kernel,
        "encode",
        [((6, 2, PACK, SLOTS), bf16), ((4, 2, KNB, SLOTS), i32), ((6, 2, *tile), bf16), ((EH, 8 * SLOTS), f32)],
        [],
        (raw, got_a, got_b, own_codes, enc_one, enc_two, recv_w),
        (),
        1 << 30,
    )
    wide, geo, send_c, send_d = run(
        first_kernel,
        "first_step",
        [((4, 2, *tile), bf16), ((8, GEO, KNB * SLOTS), bf16), column, column],
        [((6, 4, PACK, SLOTS), bf16), ((6, 4, *tile), bf16), ((EH, 8 * SLOTS), bf16)],
        (pack_own, codes_all, latents, all_bounds, got_c, got_d, enc_one, enc_two, full_w, out_w, first_w, second_w),
    )
    got_d, got_c = swap(send_d, "cross", 1), swap(send_c, "cross", 0)
    part, bound = run(middle_early_kernel, "middle_early", [gathered, bounds], [], (wide, own_codes, recv_w), (), 1 << 31)
    late = [((2, *column[0]), bf16), ((EH, 4 * SLOTS), bf16)]
    latent, send_a, send_b = run(
        middle_kernel,
        "middle_step",
        [((2, 2, *tile), bf16), side, side],
        late,
        (wide, got_c, got_d, own_codes, geo, part, bound, full_w, out_w, first_w, second_w),
    )
    got_b, got_a = swap(send_b, "slab", 1), swap(send_a, "slab", 0)
    send_c, send_d = run(pack_kernel, "pack", [column] * 2, [], (latent, got_a, got_b))
    got_d, got_c = swap(send_d, "cross", 1), swap(send_c, "cross", 0)
    part, bound = run(
        last_early_kernel,
        "last_early",
        [gathered, bounds],
        [((4, 2, *tile), bf16)],
        (latent, got_a, got_b, own_codes, recv_w),
        (),
        1 << 31,
    )
    operands = (latent, got_c, got_d, own_codes, geo, part, bound, full_w, out_w, first_w, second_w)
    return tuple(
        run(
            last_kernel,
            "last_step",
            [((2, 2, 2, SLOTS), f32)] * 2,
            late,
            (*operands, raw, position, velocity, dec_one, dec_second),
        )
    )


def solution(mesh):
    tile = P("slab", "cross", None, None)
    return jax.shard_map(
        shards,
        mesh=mesh,
        in_specs=(tile, tile, tile, P("slab", "cross"), tile, tile) + (P(),) * 10,
        out_specs=(tile, tile),
        check_vma=False,
    )
```

time: 81.8 us -> 71.9 us (0.88)
  waiting for transfers between devices: 11.7 us -> 5.3 us
  local copies, waits for them, and re-layouts: 7.54 us -> 1.52 us
  Pallas kernels: 28.6 us -> 31.5 us
    ppermute x10, waiting for transfers between devices: 11.7 us -> 5.3 us  [swap(): return lax.ppermute(block, axis, swaps(lax.axis_size(axis), start))]
    unnamed x42 -> x8, local copies, waits for them, and re-layouts: 7.54 us -> 1.52 us
    pallas_call x6 -> x10, Pallas kernels: 28.6 us -> 31.5 us  [run(): pl.pallas_call(kernel, out_shape=[jax.ShapeDtypeStruct(shape, dtype) for...]
  transfers between devices with their start and end apart: 10 -> 10, of which waited for: 5 -> 5; matrix products, arithmetic and copies ran while one was open for 0% -> 0% of each run, Pallas kernels for 0% -> 9%
where the time goes in v3:
time: 71.9 us; the launch traced here: 71.4 us
  starting transfers between devices  32.2 us (45%)
  Pallas kernels  31.5 us (44%)
  waiting for transfers between devices  5.3 us (7%)
  local copies, waits for them, and re-layouts  1.52 us (2%)
  between operations  0.81 us (1%)
    ppermute x10, starting transfers between devices, swap(): return lax.ppermute(block, axis, swaps(lax.axis_size(axis), start))  32.2 us
    pallas_call x10, Pallas kernels, run(): pl.pallas_call(kernel, out_shape=[jax.ShapeDtypeStruct(shape, dtype) for...  31.5 us
    ppermute x10, waiting for transfers between devices, swap(): return lax.ppermute(block, axis, swaps(lax.axis_size(axis), start))  5.3 us
    unnamed x8, local copies, waits for them, and re-layouts  1.52 us
  transfers between devices with their start and end apart: 10, of which 5 were waited for; matrix products, arithmetic and copies ran while one was open for 0% of the time, Pallas kernels for 9%

profile of v3, /device:TPU:17, one launch (start us, length us, event | category | flops | bytes accessed | tf_op | source)
XLA Modules:
  0.0 71.4 jit_solution(9471251472618609542)
XLA Ops:
  0.6 1.4 %copy.18.features_in = bf16[2,2,30,128]{3,2,1,0:T(8,128)(2,1)} copy(bf16[2,2,30,128]{3,1,2,0:T(2,128)(2,1)} %param.16) | data formatting | bytes 61440 | tf_op args[0]
  2.0 0.9 %prepare.1 = (bf16[2,2,48,128]{3,2,1,0:T(8,128)(2,1)S(1)}, s32[2,2,16,128]{3,2,1,0:T(8,128)S(1)}, bf16[2,128,128]{2,1,0:T(8,128)(2,1)S(1)}, bf16[2,128,128]{2,1,0:T(8,128)(2,1)S(1)}) custom-call(bf16[2,2,30,128]{3,2,1,0:T(8,128)(2,1)} %copy.18.features_in, f32[2,2,2,128]{3,2,1,0:T(2,128)} %position.1, s32[2,2]{1,0:T(2,128)} %occupancy_in.1, ...), custom_call_target="tpu_custom_call" | custom-call | tf_op jit(solution)/shard_map/prepare/pallas_call | solution.py:329
  2.9 1.3 %collective-permute-start = (bf16[2,128,128]{2,1,0:T(8,128)(2,1)S(1)}, bf16[2,128,128]{2,1,0:T(8,128)(2,1)S(1)}, u32[]{:S(2)}, u32[]{:S(2)}) collective-permute-start(bf16[2,128,128]{2,1,0:T(8,128)(2,1)S(1)} %get-tuple-element.34), channel_id=1, source_target_pairs={{0,4},{4,0},{8,12},{12,8},{16,20},{20,16},{24,28},{28,24},{32,36},... | collective-permute-start | bytes 196616 | tf_op jit(solution)/shard_map/ppermute | solution.py:349
  4.2 8.8 %collective-permute-start.1 = (bf16[2,128,128]{2,1,0:T(8,128)(2,1)S(1)}, bf16[2,128,128]{2,1,0:T(8,128)(2,1)S(1)}, u32[]{:S(2)}, u32[]{:S(2)}) collective-permute-start(bf16[2,128,128]{2,1,0:T(8,128)(2,1)S(1)} %get-tuple-element.35), channel_id=1, source_target_pairs={{4,8},{8,4},{12,16},{16,12},{20,24},{24,20},{28,32},{32,28},{36,40... | collective-permute-start | bytes 196616 | tf_op jit(solution)/shard_map/ppermute | solution.py:349
  13.0 1.5 %weights.1 = (bf16[3,144,512]{2,1,0:T(8,128)(2,1)S(1)}, bf16[3,128,512]{2,1,0:T(8,128)(2,1)S(1)}, bf16[3,512,128]{2,1,0:T(8,128)(2,1)S(1)}, bf16[3,256,128]{2,1,...) custom-call(s32[2,2,16,128]{3,2,1,0:T(8,128)S(1)} %get-tuple-element, ...), custom_call_target="tpu_custom_call" | custom-call | flops 1073741824 | bytes 4194304 | tf_op jit(solution)/shard_map/weights/pallas_call | solution.py:329
  14.5 0.5 collective-permute-done.1.got_b
  15.0 2.2 %collective-permute-start.2 = (bf16[6,48,128]{2,1,0:T(8,128)(2,1)S(1)}, bf16[6,48,128]{2,1,0:T(8,128)(2,1)S(1)}, u32[]{:S(2)}, u32[]{:S(2)}) collective-permute-start(bf16[6,48,128]{2,1,0:T(8,128)(2,1)S(1)} %get-tuple-element.44), channel_id=1, source_target_pairs={{0,1},{1,0},{2,3},{3,2},{4,5},{5,4},{6,7},{7,6},{8,9},{9,8},{10,11... | collective-permute-start | bytes 221192 | tf_op jit(solution)/shard_map/ppermute | solution.py:349
  17.1 3.1 %collective-permute-start.3 = (bf16[6,48,128]{2,1,0:T(8,128)(2,1)S(1)}, bf16[6,48,128]{2,1,0:T(8,128)(2,1)S(1)}, u32[]{:S(2)}, u32[]{:S(2)}) collective-permute-start(bf16[6,48,128]{2,1,0:T(8,128)(2,1)S(1)} %get-tuple-element.45), channel_id=1, source_target_pairs={{1,2},{2,1},{5,6},{6,5},{9,10},{10,9},{13,14},{14,13},{17,18},{18,... | collective-permute-start | bytes 221192 | tf_op jit(solution)/shard_map/ppermute | solution.py:349
  20.3 1.2 %encode.1 = (bf16[6,2,48,128]{3,2,1,0:T(8,128)(2,1)S(1)}, s32[4,2,16,128]{3,2,1,0:T(8,128)S(1)}, bf16[6,2,128,128]{3,2,1,0:T(8,128)(2,1)S(1)}, f32[512,1024]{1,0:T(8,128)S(1)}) custom-call(bf16[2,2,48,128]{3,2,1,0:T(8,128)(2,1)S(1)} %get-tuple-element.33.own.raw, bf16[2,128,128]{2,1,0:T(8,128)(2,1)S(1)} %collective-permute-done.got_a, ...), custom_call_target="tpu_custom_call" | custom-call | flops 1073741824 | bytes 4194304 | tf_op jit(solution)/shard_map/encode/pallas_call | solution.py:329
  21.5 1.3 %collective-permute-done.3.got_d = bf16[6,48,128]{2,1,0:T(8,128)(2,1)S(1)} collective-permute-done((bf16[6,48,128]{2,1,0:T(8,128)(2,1)S(1)}, bf16[6,48,128]{2,1,0:T(8,128)(2,1)S(1)}, u32[]{:S(2)}, u32[]{:S(2)}) %collective-permute-start.3) | collective-permute-done | bytes 73760 | tf_op jit(solution)/shard_map/ppermute | solution.py:349
  22.8 13.9 %first_step.1 = (bf16[4,2,128,128]{3,2,1,0:T(8,128)(2,1)S(1)}, bf16[8,16,2048]{2,1,0:T(8,128)(2,1)S(1)}, bf16[4,128,128]{2,1,0:T(8,128)(2,1)S(1)}, bf16[4,128,128]{2,1,0:T(8,128)(2,1)S(1)}) custom-call(bf16[6,2,48,128]{3,2,1,0:T(8,128)(2,1)S(1)} %get-tuple-element.40.pack_own, s32[4,2,16,128]{3,2,1,0:T(8,128)S(1)} %get-tuple-element.41.codes_all, ...), custom_call_target="tpu_custom_call" | custom-call | tf_op jit(solution)/shard_map/first_step/pallas_call | solution.py:329
  36.8 3.1 %collective-permute-start.5 = (bf16[4,128,128]{2,1,0:T(8,128)(2,1)S(1)}, bf16[4,128,128]{2,1,0:T(8,128)(2,1)S(1)}, u32[]{:S(2)}, u32[]{:S(2)}) collective-permute-start(bf16[4,128,128]{2,1,0:T(8,128)(2,1)S(1)} %get-tuple-element.52), channel_id=1, source_target_pairs={{1,2},{2,1},{5,6},{6,5},{9,10},{10,9},{13,14},{14,13},{17,18},{18,... | collective-permute-start | bytes 393224 | tf_op jit(solution)/shard_map/ppermute | solution.py:349
  40.0 2.0 %middle_early.1 = (bf16[4,128,2048]{2,1,0:T(8,128)(2,1)S(1)}, f32[512,512]{1,0:T(8,128)S(1)}) custom-call(bf16[4,2,128,128]{3,2,1,0:T(8,128)(2,1)S(1)} %get-tuple-element.50.wide, s32[2,2,16,128]{3,2,1,0:T(8,128)S(1)} %get-tuple-element.36.token.own_codes, bf16[3,128,512]{2,1,0:T(8,128)(2,1)S(1)} %get-tuple-element.39.recv_w), custom_call_target="tpu_custom_call" | custom-call | flops 2147483648 | bytes 4194304 | tf_op jit(solution)/shard_map/middle_early/pallas_call | solution.py:329
  41.9 1.2 %collective-permute-done.5.got_d = bf16[4,128,128]{2,1,0:T(8,128)(2,1)S(1)} collective-permute-done((bf16[4,128,128]{2,1,0:T(8,128)(2,1)S(1)}, bf16[4,128,128]{2,1,0:T(8,128)(2,1)S(1)}, u32[]{:S(2)}, u32[]{:S(2)}) %collective-permute-start.5) | collective-permute-done | bytes 131104 | tf_op jit(solution)/shard_map/ppermute | solution.py:349
  43.1 4.6 %middle_step.1 = (bf16[2,2,128,128]{3,2,1,0:T(8,128)(2,1)S(1)}, bf16[2,128,128]{2,1,0:T(8,128)(2,1)S(1)}, bf16[2,128,128]{2,1,0:T(8,128)(2,1)S(1)}) custom-call(bf16[4,2,128,128]{3,2,1,0:T(8,128)(2,1)S(1)} %get-tuple-element.50.wide, bf16[4,128,128]{2,1,0:T(8,128)(2,1)S(1)} %collective-permute-done.4.got_c, ...), custom_call_target="tpu_custom_call" | custom-call | tf_op jit(solution)/shard_map/middle_step/pallas_call | solution.py:329
  47.7 0.1 collective-permute-start.6
  47.8 8.9 %collective-permute-start.7 = (bf16[2,128,128]{2,1,0:T(8,128)(2,1)S(1)}, bf16[2,128,128]{2,1,0:T(8,128)(2,1)S(1)}, u32[]{:S(2)}, u32[]{:S(2)}) collective-permute-start(bf16[2,128,128]{2,1,0:T(8,128)(2,1)S(1)} %get-tuple-element.58), channel_id=1, source_target_pairs={{4,8},{8,4},{12,16},{16,12},{20,24},{24,20},{28,32},{32,28},{36,40... | collective-permute-start | bytes 196616 | tf_op jit(solution)/shard_map/ppermute | solution.py:349
  56.7 0.1 copy.19.dec_second
  56.9 1.7 %collective-permute-done.7.got_b = bf16[2,128,128]{2,1,0:T(8,128)(2,1)S(1)} collective-permute-done((bf16[2,128,128]{2,1,0:T(8,128)(2,1)S(1)}, bf16[2,128,128]{2,1,0:T(8,128)(2,1)S(1)}, u32[]{:S(2)}, u32[]{:S(2)}) %collective-permute-start.7) | collective-permute-done | bytes 65568 | tf_op jit(solution)/shard_map/ppermute | solution.py:349
  58.6 0.3 collective-permute-start.8
  58.9 4.4 %collective-permute-start.9 = (bf16[4,128,128]{2,1,0:T(8,128)(2,1)S(1)}, bf16[4,128,128]{2,1,0:T(8,128)(2,1)S(1)}, u32[]{:S(2)}, u32[]{:S(2)}) collective-permute-start(bf16[4,128,128]{2,1,0:T(8,128)(2,1)S(1)} %get-tuple-element.60), channel_id=1, source_target_pairs={{1,2},{2,1},{5,6},{6,5},{9,10},{10,9},{13,14},{14,13},{17,18},{18,... | collective-permute-start | bytes 393224 | tf_op jit(solution)/shard_map/ppermute | solution.py:349
  63.2 2.0 %last_early.1 = (bf16[4,128,2048]{2,1,0:T(8,128)(2,1)S(1)}, f32[512,512]{1,0:T(8,128)S(1)}) custom-call(bf16[2,2,128,128]{3,2,1,0:T(8,128)(2,1)S(1)} %get-tuple-element.56.own, bf16[2,128,128]{2,1,0:T(8,128)(2,1)S(1)} %collective-permute-done.6.got_a, bf16[2,128,128]{2,1,0:T(8,128)(2,1)S(1)} %collective-permute-done.7.got_b, ...), custom_call_target="tpu_custom_call" | custom-call | flops 2147483648 | bytes 4194304 | tf_op jit(solution)/shard_map/last_early/pallas_call | solution.py:329
  65.2 0.7 collective-permute-done.9.got_d
  65.9 5.5 %last_step.1 = (f32[2,2,2,128]{3,2,1,0:T(2,128)}, f32[2,2,2,128]{3,2,1,0:T(2,128)}) custom-call(bf16[2,2,128,128]{3,2,1,0:T(8,128)(2,1)S(1)} %get-tuple-element.56.own, bf16[4,128,128]{2,1,0:T(8,128)(2,1)S(1)} %collective-permute-done.8.got_c, bf16[4,128,128]{2,1,0:T(8,128)(2,1)S(1)} %collective-permute-done.9.got_d, ...), custom_call_target="tpu_custom_call" | custom-call | tf_op jit(solution)/shard_map/last_step/pallas_call | solution.py:329
  (14 shorter events, 0.2 us)
Async XLA Ops:
  2.9 11.6 %collective-permute-start = (bf16[2,128,128]{2,1,0:T(8,128)(2,1)S(1)}, bf16[2,128,128]{2,1,0:T(8,128)(2,1)S(1)}, u32[]{:S(2)}, u32[]{:S(2)}) collective-permute-start(bf16[2,128,128]{2,1,0:T(8,128)(2,1)S(1)} %get-tuple-element.34), channel_id=1, source_target_pairs={{0,4},{4,0},{8,12},{12,8},{16,20},{20,16},{24,28},{28,24},{32,36},... | collective-permute-start | bytes 196616 | tf_op jit(solution)/shard_map/ppermute | solution.py:349
  4.2 10.7 %collective-permute-start.1 = (bf16[2,128,128]{2,1,0:T(8,128)(2,1)S(1)}, bf16[2,128,128]{2,1,0:T(8,128)(2,1)S(1)}, u32[]{:S(2)}, u32[]{:S(2)}) collective-permute-start(bf16[2,128,128]{2,1,0:T(8,128)(2,1)S(1)} %get-tuple-element.35), channel_id=1, source_target_pairs={{4,8},{8,4},{12,16},{16,12},{20,24},{24,20},{28,32},{32,28},{36,40... | collective-permute-start | bytes 196616 | tf_op jit(solution)/shard_map/ppermute | solution.py:349
  15.0 6.5 %collective-permute-start.2 = (bf16[6,48,128]{2,1,0:T(8,128)(2,1)S(1)}, bf16[6,48,128]{2,1,0:T(8,128)(2,1)S(1)}, u32[]{:S(2)}, u32[]{:S(2)}) collective-permute-start(bf16[6,48,128]{2,1,0:T(8,128)(2,1)S(1)} %get-tuple-element.44), channel_id=1, source_target_pairs={{0,1},{1,0},{2,3},{3,2},{4,5},{5,4},{6,7},{7,6},{8,9},{9,8},{10,11... | collective-permute-start | bytes 221192 | tf_op jit(solution)/shard_map/ppermute | solution.py:349
  17.1 5.7 %collective-permute-start.3 = (bf16[6,48,128]{2,1,0:T(8,128)(2,1)S(1)}, bf16[6,48,128]{2,1,0:T(8,128)(2,1)S(1)}, u32[]{:S(2)}, u32[]{:S(2)}) collective-permute-start(bf16[6,48,128]{2,1,0:T(8,128)(2,1)S(1)} %get-tuple-element.45), channel_id=1, source_target_pairs={{1,2},{2,1},{5,6},{6,5},{9,10},{10,9},{13,14},{14,13},{17,18},{18,... | collective-permute-start | bytes 221192 | tf_op jit(solution)/shard_map/ppermute | solution.py:349
  36.7 5.2 %collective-permute-start.4 = (bf16[4,128,128]{2,1,0:T(8,128)(2,1)S(1)}, bf16[4,128,128]{2,1,0:T(8,128)(2,1)S(1)}, u32[]{:S(2)}, u32[]{:S(2)}) collective-permute-start(bf16[4,128,128]{2,1,0:T(8,128)(2,1)S(1)} %get-tuple-element.51), channel_id=1, source_target_pairs={{0,1},{1,0},{2,3},{3,2},{4,5},{5,4},{6,7},{7,6},{8,9},{9,8},{10,11... | collective-permute-start | bytes 393224 | tf_op jit(solution)/shard_map/ppermute | solution.py:349
  36.8 6.3 %collective-permute-start.5 = (bf16[4,128,128]{2,1,0:T(8,128)(2,1)S(1)}, bf16[4,128,128]{2,1,0:T(8,128)(2,1)S(1)}, u32[]{:S(2)}, u32[]{:S(2)}) collective-permute-start(bf16[4,128,128]{2,1,0:T(8,128)(2,1)S(1)} %get-tuple-element.52), channel_id=1, source_target_pairs={{1,2},{2,1},{5,6},{6,5},{9,10},{10,9},{13,14},{14,13},{17,18},{18,... | collective-permute-start | bytes 393224 | tf_op jit(solution)/shard_map/ppermute | solution.py:349
  43.1 13.6 %copy-start.2 = (bf16[128,2]{0,1:T(2,128)(2,1)S(1)}, bf16[128,2]{0,1:T(2,128)(2,1)}, u32[]{:S(2)}) copy-start(bf16[128,2]{0,1:T(2,128)(2,1)} %param.31) | copy-start | bytes 1540
  47.7 9.1 %collective-permute-start.6 = (bf16[2,128,128]{2,1,0:T(8,128)(2,1)S(1)}, bf16[2,128,128]{2,1,0:T(8,128)(2,1)S(1)}, u32[]{:S(2)}, u32[]{:S(2)}) collective-permute-start(bf16[2,128,128]{2,1,0:T(8,128)(2,1)S(1)} %get-tuple-element.57), channel_id=1, source_target_pairs={{0,4},{4,0},{8,12},{12,8},{16,20},{20,16},{24,28},{28,24},{32,36},... | collective-permute-start | bytes 196616 | tf_op jit(solution)/shard_map/ppermute | solution.py:349
  47.8 10.7 %collective-permute-start.7 = (bf16[2,128,128]{2,1,0:T(8,128)(2,1)S(1)}, bf16[2,128,128]{2,1,0:T(8,128)(2,1)S(1)}, u32[]{:S(2)}, u32[]{:S(2)}) collective-permute-start(bf16[2,128,128]{2,1,0:T(8,128)(2,1)S(1)} %get-tuple-element.58), channel_id=1, source_target_pairs={{4,8},{8,4},{12,16},{16,12},{20,24},{24,20},{28,32},{32,28},{36,40... | collective-permute-start | bytes 196616 | tf_op jit(solution)/shard_map/ppermute | solution.py:349
  58.6 6.6 %collective-permute-start.8 = (bf16[4,128,128]{2,1,0:T(8,128)(2,1)S(1)}, bf16[4,128,128]{2,1,0:T(8,128)(2,1)S(1)}, u32[]{:S(2)}, u32[]{:S(2)}) collective-permute-start(bf16[4,128,128]{2,1,0:T(8,128)(2,1)S(1)} %get-tuple-element.59), channel_id=1, source_target_pairs={{0,1},{1,0},{2,3},{3,2},{4,5},{5,4},{6,7},{7,6},{8,9},{9,8},{10,11... | collective-permute-start | bytes 393224 | tf_op jit(solution)/shard_map/ppermute | solution.py:349
  58.9 7.0 %copy-start = (f32[2,2,2,128]{3,2,1,0:T(2,128)S(1)}, f32[2,2,2,128]{3,2,1,0:T(2,128)}, u32[]{:S(2)}) copy-start(f32[2,2,2,128]{3,2,1,0:T(2,128)} %position.1) | copy-start | bytes 12292
  58.9 7.0 %copy-start.1 = (f32[2,2,2,128]{3,2,1,0:T(2,128)S(1)}, f32[2,2,2,128]{3,2,1,0:T(2,128)}, u32[]{:S(2)}) copy-start(f32[2,2,2,128]{3,2,1,0:T(2,128)} %velocity.1) | copy-start | bytes 12292
  58.9 7.0 %collective-permute-start.9 = (bf16[4,128,128]{2,1,0:T(8,128)(2,1)S(1)}, bf16[4,128,128]{2,1,0:T(8,128)(2,1)S(1)}, u32[]{:S(2)}, u32[]{:S(2)}) collective-permute-start(bf16[4,128,128]{2,1,0:T(8,128)(2,1)S(1)} %get-tuple-element.60), channel_id=1, source_target_pairs={{1,2},{2,1},{5,6},{6,5},{9,10},{10,9},{13,14},{14,13},{17,18},{18,... | collective-permute-start | bytes 393224 | tf_op jit(solution)/shard_map/ppermute | solution.py:349

commit v4 on v3

v4 whole, which is shorter than its diff:
```python
import functools

import jax
import jax.numpy as jnp
from jax import lax
from jax.experimental import pallas as pl
from jax.experimental.pallas import tpu as pltpu
from jax.sharding import PartitionSpec as P

time_step = 0.5
LAT = 128
EH = 512
INF = 30
KNB = 16
SLOTS = 128
PACK = 48
GEO = 16
WIDE = 8
BLOCKED = -(2.0**40)
bf16 = jnp.bfloat16
f32 = jnp.float32
i32 = jnp.int32


def tdot(left, right):
    return lax.dot_general(left, right, (((0,), (0,)), ((), ())), preferred_element_type=f32)


def split3(values):
    high = values.astype(bf16).astype(f32)
    rest = values - high
    mid = rest.astype(bf16).astype(f32)
    return [high, mid, rest - mid]


def norm_rows(values):
    center = values - jnp.mean(values, axis=0, keepdims=True)
    spread = jnp.mean(center * center, axis=0, keepdims=True)
    return center * lax.rsqrt(spread + 1e-05)


def parities():
    return lax.rem(lax.axis_index("slab"), 2), lax.rem(lax.axis_index("cross"), 2)


def lane_rows(values, first, count):
    return jnp.concatenate([values[k : k + 1] for k in range(first, first + count)], axis=1)


def repeated(values, count):
    return jnp.concatenate([values] * count, axis=1)


def prepare_kernel(features_in, position_in, occupancy_in, codes_in, mask_in, raw, own_codes, send_a, send_b,
                   features, position, occupancy, codes, mask, sems):
    pairs = ((features_in, features), (position_in, position), (occupancy_in, occupancy), (codes_in, codes), (mask_in, mask))
    copies = [pltpu.make_async_copy(source, target, sems.at[k]) for k, (source, target) in enumerate(pairs)]
    for copy in copies:
        copy.start()
    p, q = parities()
    lane = lax.broadcasted_iota(i32, (1, SLOTS), 1)
    for copy in copies:
        copy.wait()
    for a in range(2):
        for c in range(2):
            live = (lane < occupancy[a, c]).astype(f32)
            rows = [features[a, :, c, :].astype(f32), jnp.zeros((2, SLOTS), f32)]
            rows += split3(position[a, c, 0:1]) + split3(position[a, c, 1:2])
            rows += [live, jnp.zeros((PACK - 39, SLOTS), f32)]
            raw[a, c] = jnp.concatenate(rows, axis=0).astype(bf16)
            own_codes[a, c] = jnp.where(mask[a, c] > 0, codes[a, c], (codes[a, c] & (SLOTS - 1)) - SLOTS)
    for near, far, out in ((1 - p, p, send_a), (p, 1 - p, send_b)):
        for c in range(2):
            out[c, 0:PACK] = raw[near, c]
            out[c, PACK : 2 * PACK] = raw[far, c]
            code = own_codes[near, c]
            out[c, 2 * PACK : 2 * PACK + KNB] = (code >> 7).astype(f32).astype(bf16)
            out[c, 2 * PACK + KNB :] = (code & (SLOTS - 1)).astype(f32).astype(bf16)


def weights_kernel(token, *refs):
    sources, outs, (geo_w, sems) = refs[:9], refs[9:17], refs[17:]
    full_w = outs[0]
    targets = (full_w.at[:, 0:LAT, :], geo_w, *outs[1:])
    copies = [pltpu.make_async_copy(source, target, sems.at[k]) for k, (source, target) in enumerate(zip(sources, targets))]
    for copy in copies:
        copy.start()
    for copy in copies:
        copy.wait()
    for t in range(full_w.shape[0]):
        values = geo_w[t]
        high = values.astype(bf16).astype(f32)
        low = values - high
        rows = []
        for c in range(3):
            rows += [high[c : c + 1], high[c : c + 1], low[c : c + 1], low[c : c + 1]]
        rows.append(jnp.full((1, EH), BLOCKED, f32))
        rows.append(jnp.zeros((GEO - 13, EH), f32))
        full_w[t, LAT:, :] = jnp.concatenate(rows, axis=0).astype(bf16)


def pack_raw_kernel(own, got_a, got_b, token, send_c, send_d):
    p, q = parities()
    for j, out in ((1 - q, send_c), (q, send_d)):
        out[2] = own[0, j]
        out[3] = own[1, j]
        for side, got in ((1 - p, got_a), (p, got_b)):
            out[1 + 3 * side] = got[j, 0:PACK]
            out[5 * side] = got[j, PACK : 2 * PACK]


def pack_kernel(own, got_a, got_b, send_c, send_d):
    p, q = parities()
    for j, out in ((1 - q, send_c), (q, send_d)):
        out[1] = own[0, j]
        out[2] = own[1, j]
        out[3 * (1 - p)] = got_a[j]
        out[3 * p] = got_b[j]


def one_hot(window, slot, numbers):
    wide = slot.shape[1]
    iota = lax.broadcasted_iota(i32, (SLOTS, wide), 0).astype(jnp.int16)
    parts = []
    for number in numbers:
        wanted = jnp.where(window == number, slot, -1).astype(jnp.int16)
        hit = iota == jnp.broadcast_to(wanted, (SLOTS, wide))
        parts.append(jnp.where(hit, jnp.ones((), bf16), jnp.zeros((), bf16)))
    return jnp.concatenate(parts, axis=0)


def pick(codes, tiles, direct):
    window = codes >> 7
    slot = codes & (SLOTS - 1)
    hot = one_hot(window, slot, [number for number, _ in tiles])
    got = jnp.dot(jnp.concatenate([tile for _, tile in tiles], axis=1), hot, preferred_element_type=f32)
    if direct is None:
        return got
    number, tile = direct
    tile = tile.astype(f32)
    parts = []
    for k in range(codes.shape[1] // SLOTS):
        lanes = slice(k * SLOTS, (k + 1) * SLOTS)
        index = jnp.broadcast_to(slot[:, lanes], tile.shape)
        here = jnp.broadcast_to(window[:, lanes], tile.shape) == number
        moved = jnp.take_along_axis(tile, index, axis=1, mode="promise_in_bounds")
        parts.append(jnp.where(here, moved, got[:, lanes]))
    return jnp.concatenate(parts, axis=1)


def inner_tiles(s, a, tile_of):
    return [(3 * d + 1 - s + j, tile_of(a + d, j)) for d in range(3) for j in range(2)]


def outer_tiles(s, a, tile_of):
    return [(3 * d + 2 * s, tile_of(a + d)) for d in range(3)]


def geometry_rows(got, own_x, own_y, own_live):
    delta_x = got[0:1] + got[1:2] + got[2:3] - own_x
    delta_y = got[3:4] + got[4:5] + got[5:6] - own_y
    distance = delta_x * delta_x + delta_y * delta_y
    pieces = []
    for v in (delta_x, delta_y, distance):
        high = v.astype(bf16).astype(f32)
        pieces += [high, v - high, high, v - high]
    pieces.append(1.0 - own_live * got[6:7])
    pieces.append(jnp.zeros((GEO - 13, got.shape[1]), f32))
    return jnp.concatenate(pieces, axis=0).astype(bf16)


def edge_sum(full_w, right_side, bound, total):
    hidden = tdot(full_w, right_side)
    for k in range(right_side.shape[1] // SLOTS):
        part = jnp.maximum(hidden[:, k * SLOTS : (k + 1) * SLOTS], bound)
        total = part if total is None else total + part
    return total


def node_update(own_all, sums, out_w, first_w, second_w):
    summed = tdot(out_w, sums).astype(bf16)
    joined = tdot(first_w, jnp.concatenate([own_all, summed], axis=0))
    joined = jnp.maximum(joined, 0.0).astype(bf16)
    update = norm_rows(tdot(second_w, joined))
    return (own_all.astype(f32) + update).astype(bf16)


def encoded(rows, enc_first, enc_second):
    weight = jnp.concatenate([enc_first[...], jnp.zeros((PACK - INF, LAT), bf16)], axis=0)
    raw = jnp.concatenate(rows, axis=1)
    hidden = jnp.maximum(tdot(weight, raw), 0.0).astype(bf16)
    return norm_rows(tdot(enc_second[...], hidden)).astype(bf16)


def first_bins(s, inner, pack_inner, outer, pack_outer, codes_all, bounds, full_w, sums, geo_out):
    def inner_tile(i, j):
        return jnp.concatenate([inner[i, j], pack_inner[i, j, 32:PACK, :]], axis=0)

    def outer_tile(i):
        return jnp.concatenate([outer[i], pack_outer[i, 32:PACK, :]], axis=0)

    def one_bin(a, carry):
        codes = codes_all[a, s]
        tiles = outer_tiles(s, a, outer_tile) + inner_tiles(s, a, inner_tile)
        me = pack_inner[a + 1, s, 32:PACK, :].astype(f32)
        own_x = repeated(me[0:1] + me[1:2] + me[2:3], WIDE)
        own_y = repeated(me[3:4] + me[4:5] + me[5:6], WIDE)
        own_live = repeated(me[6:7], WIDE)
        columns = pl.ds(pl.multiple_of(a * SLOTS, SLOTS), SLOTS)
        bound = bounds[:, columns]
        total = None
        for part in range(KNB // WIDE):
            got = pick(lane_rows(codes, part * WIDE, WIDE), tiles[:-1], tiles[-1])
            geo = geometry_rows(got[LAT:], own_x, own_y, own_live)
            geo_out[a, :, part * WIDE * SLOTS : (part + 1) * WIDE * SLOTS] = geo
            total = edge_sum(full_w[0], jnp.concatenate([got[:LAT].astype(bf16), geo], axis=0), bound, total)
        sums[:, columns] = (total - KNB * bound).astype(bf16)
        return carry

    lax.fori_loop(0, 4, one_bin, 0)


def first_early_kernel(
    own, got_a, got_b, got_c, own_codes, enc_first, enc_second, recv_w, full_w,
    pack, codes_all, inner, bounds_d, sums_c, geo_c, outer, bounds_c,
):
    p, q = parities()
    for c in range(2):
        for a in range(2):
            pack[2 + a, c] = own[a, c]
            codes_all[1 + a, c] = own_codes[a, c]
        for side, got in ((1 - p, got_a), (p, got_b)):
            pack[1 + 3 * side, c] = got[c, 0:PACK]
            pack[5 * side, c] = got[c, PACK : 2 * PACK]
            window = got[c, 2 * PACK : 2 * PACK + KNB].astype(f32)
            slot = got[c, 2 * PACK + KNB :].astype(f32)
            codes_all[3 * side, c] = (window * SLOTS + slot).astype(i32)
    for i in range(0, 6, 2):
        rows = [pack[i + j // 2, j % 2] for j in range(4)] + [got_c[i], got_c[i + 1]]
        latent = encoded(rows, enc_first, enc_second)
        for j in range(4):
            inner[i + j // 2, j % 2] = latent[:, j * SLOTS : (j + 1) * SLOTS]
        for j in range(2):
            outer[i + j] = latent[:, (4 + j) * SLOTS : (5 + j) * SLOTS]
    for s, bounds in ((1 - q, bounds_c), (q, bounds_d)):
        bounds[...] = -tdot(recv_w[0], jnp.concatenate([inner[1 + a, s] for a in range(4)], axis=1))
    first_bins(1 - q, inner, pack, outer, got_c, codes_all, bounds_c, full_w, sums_c, geo_c)


def first_kernel(
    pack, codes_all, inner, bounds_d, sums_c, got_d, enc_first, enc_second, full_w, out_w, first_w, second_w,
    latent_out, geo_d, send_c, send_d, outer, sums_d,
):
    p, q = parities()
    latent = encoded([got_d[i] for i in range(6)], enc_first, enc_second)
    for i in range(6):
        outer[i] = latent[:, i * SLOTS : (i + 1) * SLOTS]
    first_bins(q, inner, pack, outer, got_d, codes_all, bounds_d, full_w, sums_d, geo_d)
    own_all = jnp.concatenate([inner[1 + a, s] for s in (1 - q, q) for a in range(4)], axis=1)
    sums = jnp.concatenate([sums_c[...], sums_d[...]], axis=1)
    latent = node_update(own_all, sums, out_w[0], first_w[0], second_w[0])
    for i in range(4):
        for s, send, at in ((1 - q, send_c, i), (q, send_d, 4 + i)):
            tile = latent[:, at * SLOTS : (at + 1) * SLOTS]
            send[i] = tile
            latent_out[i, s] = tile


def early_part(t, inner, got_c, own_codes, geo_c, recv_w, full_w, sums_c, gathered_d, bounds_d):
    p, q = parities()
    outs = [-tdot(recv_w[t], jnp.concatenate([inner[1, s], inner[2, s]], axis=1)) for s in (1 - q, q)]
    bounds_d[...] = outs[1]
    for a in range(2):
        bound = outs[0][:, a * SLOTS : (a + 1) * SLOTS]
        tiles = outer_tiles(1 - q, a, lambda i: got_c[i]) + inner_tiles(1 - q, a, lambda i, j: inner[i, j])
        total = None
        for part in range(KNB // WIDE):
            columns = slice(part * WIDE * SLOTS, (part + 1) * WIDE * SLOTS)
            got = pick(lane_rows(own_codes[a, 1 - q], part * WIDE, WIDE), tiles[:-1], tiles[-1]).astype(bf16)
            total = edge_sum(full_w[t], jnp.concatenate([got, geo_c[1 + a, :, columns]], axis=0), bound, total)
        sums_c[:, a * SLOTS : (a + 1) * SLOTS] = (total - KNB * bound).astype(bf16)
    for a in range(2):
        tiles = inner_tiles(q, a, lambda i, j: inner[i, j])
        for part in range(KNB // WIDE):
            columns = slice(part * WIDE * SLOTS, (part + 1) * WIDE * SLOTS)
            gathered_d[a, :, columns] = pick(lane_rows(own_codes[a, q], part * WIDE, WIDE), tiles, None).astype(bf16)


def middle_early_kernel(wide, got_c, own_codes, geo_c, recv_w, full_w, sums_c, gathered_d, bounds_d):
    early_part(1, wide, got_c, own_codes, geo_c, recv_w, full_w, sums_c, gathered_d, bounds_d)


def last_early_kernel(own, got_a, got_b, got_c, own_codes, geo_c, recv_w, full_w, sums_c, gathered_d, bounds_d, inner):
    p, q = parities()
    for c in range(2):
        inner[1, c] = own[0, c]
        inner[2, c] = own[1, c]
        inner[3 * (1 - p), c] = got_a[c]
        inner[3 * p, c] = got_b[c]
    early_part(2, inner, got_c, own_codes, geo_c, recv_w, full_w, sums_c, gathered_d, bounds_d)


def late_part(t, own_all, got_d, own_codes, geo_d, sums_c, gathered_d, bounds_d, full_w, out_w, first_w, second_w):
    p, q = parities()
    sums = [sums_c[...]]
    for a in range(2):
        tiles = outer_tiles(q, a, lambda i: got_d[i])
        bound = bounds_d[:, a * SLOTS : (a + 1) * SLOTS]
        total = None
        for part in range(KNB // WIDE):
            columns = slice(part * WIDE * SLOTS, (part + 1) * WIDE * SLOTS)
            got = pick(lane_rows(own_codes[a, q], part * WIDE, WIDE), tiles[:-1], tiles[-1]).astype(bf16)
            rows = jnp.concatenate([got + gathered_d[a, :, columns], geo_d[1 + a, :, columns]], axis=0)
            total = edge_sum(full_w[t], rows, bound, total)
        sums.append((total - KNB * bound).astype(bf16))
    return node_update(own_all, jnp.concatenate(sums, axis=1), out_w[t], first_w[t], second_w[t])


def middle_kernel(
    wide, got_d, own_codes, geo_d, sums_c, gathered_d, bounds_d, full_w, out_w, first_w, second_w,
    latent_out, send_a, send_b,
):
    p, q = parities()
    own_all = jnp.concatenate([wide[1 + a, s] for s in (1 - q, q) for a in range(2)], axis=1)
    latent = late_part(1, own_all, got_d, own_codes, geo_d, sums_c, gathered_d, bounds_d, full_w, out_w, first_w, second_w)
    for a in range(2):
        latent_out[a, 1 - q] = latent[:, a * SLOTS : (a + 1) * SLOTS]
        latent_out[a, q] = latent[:, (2 + a) * SLOTS : (3 + a) * SLOTS]
    for c in range(2):
        send_a[c] = latent_out[1 - p, c]
        send_b[c] = latent_out[p, c]


def last_kernel(
    own, got_d, own_codes, geo_d, sums_c, gathered_d, bounds_d, full_w, out_w, first_w, second_w,
    raw, position, velocity, dec_first, dec_second, out_velocity, out_position,
):
    p, q = parities()
    own_all = jnp.concatenate([own[a, s] for s in (1 - q, q) for a in range(2)], axis=1)
    latent = late_part(2, own_all, got_d, own_codes, geo_d, sums_c, gathered_d, bounds_d, full_w, out_w, first_w, second_w)
    hidden = jnp.maximum(tdot(dec_first[...], latent), 0.0).astype(bf16)
    accel = tdot(dec_second[...], hidden)
    for b in range(4):
        a, c = b % 2, (1 - q, q)[b // 2]
        live = raw[a, c, 32:PACK].astype(f32)[6:7]
        speed = velocity[a, c] + time_step * (accel[:, b * SLOTS : (b + 1) * SLOTS] * live)
        out_velocity[a, c] = speed
        out_position[a, c] = position[a, c] + time_step * speed


def run(kernel, name, out, scratch, operands, outside=(), work=None):
    vmem = pl.BlockSpec(memory_space=pltpu.VMEM)
    far = pl.BlockSpec(memory_space=pltpu.HBM)
    operands = [
        pltpu.with_memory_space_constraint(x, pltpu.HBM) if k in outside else x for k, x in enumerate(operands)
    ]
    return pl.pallas_call(
        kernel,
        out_shape=[jax.ShapeDtypeStruct(shape, dtype) for shape, dtype in out],
        in_specs=[far if k in outside else vmem for k in range(len(operands))],
        out_specs=[vmem] * len(out),
        scratch_shapes=[pltpu.VMEM(*entry) if isinstance(entry, tuple) else entry for entry in scratch],
        compiler_params=pltpu.CompilerParams(vmem_limit_bytes=32 << 20),
        cost_estimate=None if work is None else pl.CostEstimate(flops=work, bytes_accessed=4 << 20, transcendentals=0),
        name=name,
    )(*operands)


def swaps(count, start):
    pairs = []
    for low in range(start, count - 1, 2):
        pairs += [(low, low + 1), (low + 1, low)]
    return pairs


def swap(block, axis, start):
    return lax.ppermute(block, axis, swaps(lax.axis_size(axis), start))


def shards(
    features,
    position,
    velocity,
    occupancy,
    neighbor_codes,
    edge_mask,
    enc_first,
    enc_second,
    edge_recv,
    edge_send,
    edge_geo,
    edge_out,
    node_first,
    node_second,
    dec_first,
    dec_second,
):
    tile = (LAT, SLOTS)
    side = ((2, *tile), bf16)
    column = ((4, *tile), bf16)
    raw_column = ((6, PACK, SLOTS), bf16)
    steps = edge_recv.shape[0]
    whole = lambda values: (values.shape, values.dtype)
    geometry = ((4, GEO, KNB * SLOTS), bf16)
    early = [((EH, 2 * SLOTS), bf16), ((2, LAT, KNB * SLOTS), bf16), ((EH, 2 * SLOTS), f32)]

    features = jnp.transpose(features, (0, 2, 1, 3))
    inputs = (features, position, occupancy, neighbor_codes, edge_mask)
    raw, own_codes, send_a, send_b = run(
        prepare_kernel,
        "prepare",
        [((2, 2, PACK, SLOTS), bf16), ((2, 2, KNB, SLOTS), i32), side, side],
        [
            whole(features),
            whole(position),
            pltpu.SMEM(occupancy.shape, i32),
            whole(neighbor_codes),
            whole(edge_mask),
            pltpu.SemaphoreType.DMA((5,)),
        ],
        inputs,
        range(5),
    )
    got_b, got_a = swap(send_b, "slab", 1), swap(send_a, "slab", 0)
    plain = (edge_recv, edge_out, node_first, node_second, enc_first, enc_second, dec_first)
    full_w, recv_w, out_w, first_w, second_w, enc_one, enc_two, dec_one = run(
        weights_kernel,
        "weights",
        [((steps, LAT + GEO, EH), bf16), *[whole(w) for w in plain]],
        [whole(edge_geo), pltpu.SemaphoreType.DMA((9,))],
        (own_codes, edge_send, edge_geo, *plain),
        range(1, 10),
        1 << 30,
    )
    send_c, send_d = run(pack_raw_kernel, "pack_raw", [raw_column] * 2, [], (raw, got_a, got_b, enc_one))
    got_d, got_c = swap(send_d, "cross", 1), swap(send_c, "cross", 0)
    pack, codes_all, inner, bounds_d, sums_c, geo_c = run(
        first_early_kernel,
        "first_early",
        [
            ((6, 2, PACK, SLOTS), bf16),
            ((4, 2, KNB, SLOTS), i32),
            ((6, 2, *tile), bf16),
            ((EH, 4 * SLOTS), f32),
            ((EH, 4 * SLOTS), bf16),
            geometry,
        ],
        [((6, *tile), bf16), ((EH, 4 * SLOTS), f32)],
        (raw, got_a, got_b, got_c, own_codes, enc_one, enc_two, recv_w, full_w),
        (),
        1 << 31,
    )
    wide, geo_d, send_c, send_d = run(
        first_kernel,
        "first_step",
        [((4, 2, *tile), bf16), geometry, column, column],
        [((6, *tile), bf16), ((EH, 4 * SLOTS), bf16)],
        (pack, codes_all, inner, bounds_d, sums_c, got_d, enc_one, enc_two, full_w, out_w, first_w, second_w),
    )
    got_d, got_c = swap(send_d, "cross", 1), swap(send_c, "cross", 0)
    parts = run(
        middle_early_kernel, "middle_early", early, [], (wide, got_c, own_codes, geo_c, recv_w, full_w), (), 1 << 31
    )
    latent, send_a, send_b = run(
        middle_kernel,
        "middle_step",
        [((2, 2, *tile), bf16), side, side],
        [],
        (wide, got_d, own_codes, geo_d, *parts, full_w, out_w, first_w, second_w),
    )
    got_b, got_a = swap(send_b, "slab", 1), swap(send_a, "slab", 0)
    send_c, send_d = run(pack_kernel, "pack", [column] * 2, [], (latent, got_a, got_b))
    got_d, got_c = swap(send_d, "cross", 1), swap(send_c, "cross", 0)
    parts = run(
        last_early_kernel,
        "last_early",
        early,
        [((4, 2, *tile), bf16)],
        (latent, got_a, got_b, got_c, own_codes, geo_c, recv_w, full_w),
        (),
        1 << 31,
    )
    operands = (latent, got_d, own_codes, geo_d, *parts, full_w, out_w, first_w, second_w)
    return tuple(
        run(
            last_kernel,
            "last_step",
            [((2, 2, 2, SLOTS), f32)] * 2,
            [],
            (*operands, raw, position, velocity, dec_one, dec_second),
        )
    )


def solution(mesh):
    tile = P("slab", "cross", None, None)
    return jax.shard_map(
        shards,
        mesh=mesh,
        in_specs=(tile, tile, tile, P("slab", "cross"), tile, tile) + (P(),) * 10,
        out_specs=(tile, tile),
        check_vma=False,
    )
```

time: 71.9 us -> 66.3 us (0.922)
  waiting for transfers between devices: 5.3 us -> 2.53 us
  Pallas kernels: 31.5 us -> 29.7 us
    ppermute x10, waiting for transfers between devices: 5.3 us -> 2.53 us  [swap(): return lax.ppermute(block, axis, swaps(lax.axis_size(axis), start))]
    pallas_call x10, Pallas kernels: 31.5 us -> 29.7 us  [run(): pl.pallas_call(kernel, out_shape=[jax.ShapeDtypeStruct(shape, dtype) for...]
    unnamed x8 -> x7, local copies, waits for them, and re-layouts: 1.52 us -> 1.35 us
  transfers between devices with their start and end apart: 10 -> 10, of which waited for: 5 -> 3; matrix products, arithmetic and copies ran while one was open for 0% -> 0% of each run, Pallas kernels for 9% -> 24%
where the time goes in v4:
time: 66.3 us; the launch traced here: 66 us
  starting transfers between devices  31.5 us (48%)
  Pallas kernels  29.7 us (45%)
  waiting for transfers between devices  2.53 us (4%)
  local copies, waits for them, and re-layouts  1.35 us (2%)
  between operations  0.84 us (1%)
    ppermute x10, starting transfers between devices, swap(): return lax.ppermute(block, axis, swaps(lax.axis_size(axis), start))  31.5 us
    pallas_call x10, Pallas kernels, run(): pl.pallas_call(kernel, out_shape=[jax.ShapeDtypeStruct(shape, dtype) for...  29.7 us
    ppermute x10, waiting for transfers between devices, swap(): return lax.ppermute(block, axis, swaps(lax.axis_size(axis), start))  2.53 us
    unnamed x7, local copies, waits for them, and re-layouts  1.35 us
  transfers between devices with their start and end apart: 10, of which 3 were waited for; matrix products, arithmetic and copies ran while one was open for 0% of the time, Pallas kernels for 24%

profile of v4, /device:TPU:17, one launch (start us, length us, event | category | flops | bytes accessed | tf_op | source)
XLA Modules:
  0.0 66.0 jit_solution(8071561384550949293)
XLA Ops:
  0.6 1.0 %prepare.1 = (bf16[2,2,48,128]{3,2,1,0:T(8,128)(2,1)S(1)}, s32[2,2,16,128]{3,2,1,0:T(8,128)S(1)}, bf16[2,128,128]{2,1,0:T(8,128)(2,1)S(1)}, bf16[2,128,128]{2,1,0:T(8,128)(2,1)S(1)}) custom-call(bf16[2,30,2,128]{3,2,1,0:T(2,128)(2,1)} %bitcast.1, f32[2,2,2,128]{3,2,1,0:T(2,128)} %position.1, s32[2,2]{1,0:T(2,128)} %occupancy_in.1, ...), custom_call_target="tpu_custom_call" | custom-call | tf_op jit(solution)/shard_map/prepare/pallas_call | solution.py:357
  1.6 1.3 %collective-permute-start = (bf16[2,128,128]{2,1,0:T(8,128)(2,1)S(1)}, bf16[2,128,128]{2,1,0:T(8,128)(2,1)S(1)}, u32[]{:S(2)}, u32[]{:S(2)}) collective-permute-start(bf16[2,128,128]{2,1,0:T(8,128)(2,1)S(1)} %get-tuple-element.38), channel_id=1, source_target_pairs={{0,4},{4,0},{8,12},{12,8},{16,20},{20,16},{24,28},{28,24},{32,36},... | collective-permute-start | bytes 196616 | tf_op jit(solution)/shard_map/ppermute | solution.py:377
  2.9 8.8 %collective-permute-start.1 = (bf16[2,128,128]{2,1,0:T(8,128)(2,1)S(1)}, bf16[2,128,128]{2,1,0:T(8,128)(2,1)S(1)}, u32[]{:S(2)}, u32[]{:S(2)}) collective-permute-start(bf16[2,128,128]{2,1,0:T(8,128)(2,1)S(1)} %get-tuple-element.39), channel_id=1, source_target_pairs={{4,8},{8,4},{12,16},{16,12},{20,24},{24,20},{28,32},{32,28},{36,40... | collective-permute-start | bytes 196616 | tf_op jit(solution)/shard_map/ppermute | solution.py:377
  11.7 1.5 %weights.1 = (bf16[3,144,512]{2,1,0:T(8,128)(2,1)S(1)}, bf16[3,128,512]{2,1,0:T(8,128)(2,1)S(1)}, bf16[3,512,128]{2,1,0:T(8,128)(2,1)S(1)}, bf16[3,256,128]{2,1,...) custom-call(s32[2,2,16,128]{3,2,1,0:T(8,128)S(1)} %get-tuple-element, ...), custom_call_target="tpu_custom_call" | custom-call | flops 1073741824 | bytes 4194304 | tf_op jit(solution)/shard_map/weights/pallas_call | solution.py:357
  13.2 0.5 collective-permute-done.1.got_b
  13.6 2.2 %collective-permute-start.2 = (bf16[6,48,128]{2,1,0:T(8,128)(2,1)S(1)}, bf16[6,48,128]{2,1,0:T(8,128)(2,1)S(1)}, u32[]{:S(2)}, u32[]{:S(2)}) collective-permute-start(bf16[6,48,128]{2,1,0:T(8,128)(2,1)S(1)} %get-tuple-element.42), channel_id=1, source_target_pairs={{0,1},{1,0},{2,3},{3,2},{4,5},{5,4},{6,7},{7,6},{8,9},{9,8},{10,11... | collective-permute-start | bytes 221192 | tf_op jit(solution)/shard_map/ppermute | solution.py:377
  15.8 3.1 %collective-permute-start.3 = (bf16[6,48,128]{2,1,0:T(8,128)(2,1)S(1)}, bf16[6,48,128]{2,1,0:T(8,128)(2,1)S(1)}, u32[]{:S(2)}, u32[]{:S(2)}) collective-permute-start(bf16[6,48,128]{2,1,0:T(8,128)(2,1)S(1)} %get-tuple-element.51), channel_id=1, source_target_pairs={{1,2},{2,1},{5,6},{6,5},{9,10},{10,9},{13,14},{14,13},{17,18},{18,... | collective-permute-start | bytes 221192 | tf_op jit(solution)/shard_map/ppermute | solution.py:377
  19.0 7.3 %first_early.1 = (bf16[6,2,48,128]{3,2,1,0:T(8,128)(2,1)S(1)}, s32[4,2,16,128]{3,2,1,0:T(8,128)S(1)}, bf16[6,2,128,128]{3,2,1,0:T(8,128)(2,1)S(1)}, f32[512,512]...) custom-call(bf16[2,2,48,128]{3,2,1,0:T(8,128)(2,1)S(1)} %get-tuple-element.37.own.raw, ...), custom_call_target="tpu_custom_call" | custom-call | flops 2147483648 | bytes 4194304 | tf_op jit(solution)/shard_map/first_early/pallas_call | solution.py:357
  26.3 7.1 %first_step.1 = (bf16[4,2,128,128]{3,2,1,0:T(8,128)(2,1)S(1)}, bf16[4,16,2048]{2,1,0:T(8,128)(2,1)S(1)}, bf16[4,128,128]{2,1,0:T(8,128)(2,1)S(1)}, bf16[4,128,128]{2,1,0:T(8,128)(2,1)S(1)}) custom-call(bf16[6,2,48,128]{3,2,1,0:T(8,128)(2,1)S(1)} %get-tuple-element.46.pack, s32[4,2,16,128]{3,2,1,0:T(8,128)S(1)} %get-tuple-element.47.codes_all, ...), custom_call_target="tpu_custom_call" | custom-call | tf_op jit(solution)/shard_map/first_step/pallas_call | solution.py:357
  33.4 0.1 collective-permute-start.5
  33.5 2.6 %collective-permute-start.4 = (bf16[4,128,128]{2,1,0:T(8,128)(2,1)S(1)}, bf16[4,128,128]{2,1,0:T(8,128)(2,1)S(1)}, u32[]{:S(2)}, u32[]{:S(2)}) collective-permute-start(bf16[4,128,128]{2,1,0:T(8,128)(2,1)S(1)} %get-tuple-element.56), channel_id=1, source_target_pairs={{1,2},{2,1},{5,6},{6,5},{9,10},{10,9},{13,14},{14,13},{17,18},{18,... | collective-permute-start | bytes 393224 | tf_op jit(solution)/shard_map/ppermute | solution.py:377
  36.1 3.5 %middle_early.1 = (bf16[512,256]{1,0:T(8,128)(2,1)S(1)}, bf16[2,128,2048]{2,1,0:T(8,128)(2,1)S(1)}, f32[512,256]{1,0:T(8,128)S(1)}) custom-call(bf16[4,2,128,128]{3,2,1,0:T(8,128)(2,1)S(1)} %get-tuple-element.55.wide, bf16[4,128,128]{2,1,0:T(8,128)(2,1)S(1)} %collective-permute-done.5.got_c, s32[2,2,16,128]{3,2,1,0:T(8,128)S(1)} %get-tuple-element.40.token.own_codes, ...), custom_call_target="tpu_custom_call" | custom-call | flops 2147483648 | bytes 4194304 | tf_op jit(solution)/shard_map/middle_early/pallas_call | solution.py:357
  39.6 0.2 collective-permute-done.4.got_d
  39.8 2.5 %middle_step.1 = (bf16[2,2,128,128]{3,2,1,0:T(8,128)(2,1)S(1)}, bf16[2,128,128]{2,1,0:T(8,128)(2,1)S(1)}, bf16[2,128,128]{2,1,0:T(8,128)(2,1)S(1)}) custom-call(bf16[4,2,128,128]{3,2,1,0:T(8,128)(2,1)S(1)} %get-tuple-element.55.wide, bf16[4,128,128]{2,1,0:T(8,128)(2,1)S(1)} %collective-permute-done.4.got_d, ...), custom_call_target="tpu_custom_call" | custom-call | tf_op jit(solution)/shard_map/middle_step/pallas_call | solution.py:357
  42.3 0.1 collective-permute-start.6
  42.4 8.8 %collective-permute-start.7 = (bf16[2,128,128]{2,1,0:T(8,128)(2,1)S(1)}, bf16[2,128,128]{2,1,0:T(8,128)(2,1)S(1)}, u32[]{:S(2)}, u32[]{:S(2)}) collective-permute-start(bf16[2,128,128]{2,1,0:T(8,128)(2,1)S(1)} %get-tuple-element.65), channel_id=1, source_target_pairs={{4,8},{8,4},{12,16},{16,12},{20,24},{24,20},{28,32},{32,28},{36,40... | collective-permute-start | bytes 196616 | tf_op jit(solution)/shard_map/ppermute | solution.py:377
  51.3 1.9 %collective-permute-done.7.got_b = bf16[2,128,128]{2,1,0:T(8,128)(2,1)S(1)} collective-permute-done((bf16[2,128,128]{2,1,0:T(8,128)(2,1)S(1)}, bf16[2,128,128]{2,1,0:T(8,128)(2,1)S(1)}, u32[]{:S(2)}, u32[]{:S(2)}) %collective-permute-start.7) | collective-permute-done | bytes 65568 | tf_op jit(solution)/shard_map/ppermute | solution.py:377
  53.2 0.1 collective-permute-start.9
  53.3 0.5 copy-done.2
  53.8 0.1 copy.18.dec_second
  54.0 4.4 %collective-permute-start.8 = (bf16[4,128,128]{2,1,0:T(8,128)(2,1)S(1)}, bf16[4,128,128]{2,1,0:T(8,128)(2,1)S(1)}, u32[]{:S(2)}, u32[]{:S(2)}) collective-permute-start(bf16[4,128,128]{2,1,0:T(8,128)(2,1)S(1)} %get-tuple-element.66), channel_id=1, source_target_pairs={{1,2},{2,1},{5,6},{6,5},{9,10},{10,9},{13,14},{14,13},{17,18},{18,... | collective-permute-start | bytes 393224 | tf_op jit(solution)/shard_map/ppermute | solution.py:377
  58.4 3.5 %last_early.1 = (bf16[512,256]{1,0:T(8,128)(2,1)S(1)}, bf16[2,128,2048]{2,1,0:T(8,128)(2,1)S(1)}, f32[512,256]{1,0:T(8,128)S(1)}) custom-call(bf16[2,2,128,128]{3,2,1,0:T(8,128)(2,1)S(1)} %get-tuple-element.63.own, bf16[2,128,128]{2,1,0:T(8,128)(2,1)S(1)} %collective-permute-done.6.got_a, bf16[2,128,128]{2,1,0:T(8,128)(2,1)S(1)} %collective-permute-done.7.got_b, ...), custom_call_target="tpu_custom_call" | custom-call | flops 2147483648 | bytes 4194304 | tf_op jit(solution)/shard_map/last_early/pallas_call | solution.py:357
  61.9 0.7 copy-done
  62.6 3.4 %last_step.1 = (f32[2,2,2,128]{3,2,1,0:T(2,128)}, f32[2,2,2,128]{3,2,1,0:T(2,128)}) custom-call(bf16[2,2,128,128]{3,2,1,0:T(8,128)(2,1)S(1)} %get-tuple-element.63.own, bf16[4,128,128]{2,1,0:T(8,128)(2,1)S(1)} %collective-permute-done.8.got_d, s32[2,2,16,128]{3,2,1,0:T(8,128)S(1)} %get-tuple-element.40.token.own_codes, ...), custom_call_target="tpu_custom_call" | custom-call | tf_op jit(solution)/shard_map/last_step/pallas_call | solution.py:357
  (13 shorter events, 0.1 us)
Async XLA Ops:
  1.6 11.6 %collective-permute-start = (bf16[2,128,128]{2,1,0:T(8,128)(2,1)S(1)}, bf16[2,128,128]{2,1,0:T(8,128)(2,1)S(1)}, u32[]{:S(2)}, u32[]{:S(2)}) collective-permute-start(bf16[2,128,128]{2,1,0:T(8,128)(2,1)S(1)} %get-tuple-element.38), channel_id=1, source_target_pairs={{0,4},{4,0},{8,12},{12,8},{16,20},{20,16},{24,28},{28,24},{32,36},... | collective-permute-start | bytes 196616 | tf_op jit(solution)/shard_map/ppermute | solution.py:377
  2.9 10.7 %collective-permute-start.1 = (bf16[2,128,128]{2,1,0:T(8,128)(2,1)S(1)}, bf16[2,128,128]{2,1,0:T(8,128)(2,1)S(1)}, u32[]{:S(2)}, u32[]{:S(2)}) collective-permute-start(bf16[2,128,128]{2,1,0:T(8,128)(2,1)S(1)} %get-tuple-element.39), channel_id=1, source_target_pairs={{4,8},{8,4},{12,16},{16,12},{20,24},{24,20},{28,32},{32,28},{36,40... | collective-permute-start | bytes 196616 | tf_op jit(solution)/shard_map/ppermute | solution.py:377
  13.6 5.3 %collective-permute-start.2 = (bf16[6,48,128]{2,1,0:T(8,128)(2,1)S(1)}, bf16[6,48,128]{2,1,0:T(8,128)(2,1)S(1)}, u32[]{:S(2)}, u32[]{:S(2)}) collective-permute-start(bf16[6,48,128]{2,1,0:T(8,128)(2,1)S(1)} %get-tuple-element.42), channel_id=1, source_target_pairs={{0,1},{1,0},{2,3},{3,2},{4,5},{5,4},{6,7},{7,6},{8,9},{9,8},{10,11... | collective-permute-start | bytes 221192 | tf_op jit(solution)/shard_map/ppermute | solution.py:377
  15.8 10.4 %collective-permute-start.3 = (bf16[6,48,128]{2,1,0:T(8,128)(2,1)S(1)}, bf16[6,48,128]{2,1,0:T(8,128)(2,1)S(1)}, u32[]{:S(2)}, u32[]{:S(2)}) collective-permute-start(bf16[6,48,128]{2,1,0:T(8,128)(2,1)S(1)} %get-tuple-element.51), channel_id=1, source_target_pairs={{1,2},{2,1},{5,6},{6,5},{9,10},{10,9},{13,14},{14,13},{17,18},{18,... | collective-permute-start | bytes 221192 | tf_op jit(solution)/shard_map/ppermute | solution.py:377
  33.4 2.7 %collective-permute-start.5 = (bf16[4,128,128]{2,1,0:T(8,128)(2,1)S(1)}, bf16[4,128,128]{2,1,0:T(8,128)(2,1)S(1)}, u32[]{:S(2)}, u32[]{:S(2)}) collective-permute-start(bf16[4,128,128]{2,1,0:T(8,128)(2,1)S(1)} %get-tuple-element.58), channel_id=1, source_target_pairs={{0,1},{1,0},{2,3},{3,2},{4,5},{5,4},{6,7},{7,6},{8,9},{9,8},{10,11... | collective-permute-start | bytes 393224 | tf_op jit(solution)/shard_map/ppermute | solution.py:377
  33.5 6.3 %collective-permute-start.4 = (bf16[4,128,128]{2,1,0:T(8,128)(2,1)S(1)}, bf16[4,128,128]{2,1,0:T(8,128)(2,1)S(1)}, u32[]{:S(2)}, u32[]{:S(2)}) collective-permute-start(bf16[4,128,128]{2,1,0:T(8,128)(2,1)S(1)} %get-tuple-element.56), channel_id=1, source_target_pairs={{1,2},{2,1},{5,6},{6,5},{9,10},{10,9},{13,14},{14,13},{17,18},{18,... | collective-permute-start | bytes 393224 | tf_op jit(solution)/shard_map/ppermute | solution.py:377
  42.3 8.9 %collective-permute-start.6 = (bf16[2,128,128]{2,1,0:T(8,128)(2,1)S(1)}, bf16[2,128,128]{2,1,0:T(8,128)(2,1)S(1)}, u32[]{:S(2)}, u32[]{:S(2)}) collective-permute-start(bf16[2,128,128]{2,1,0:T(8,128)(2,1)S(1)} %get-tuple-element.64), channel_id=1, source_target_pairs={{0,4},{4,0},{8,12},{12,8},{16,20},{20,16},{24,28},{28,24},{32,36},... | collective-permute-start | bytes 196616 | tf_op jit(solution)/shard_map/ppermute | solution.py:377
  42.4 10.7 %collective-permute-start.7 = (bf16[2,128,128]{2,1,0:T(8,128)(2,1)S(1)}, bf16[2,128,128]{2,1,0:T(8,128)(2,1)S(1)}, u32[]{:S(2)}, u32[]{:S(2)}) collective-permute-start(bf16[2,128,128]{2,1,0:T(8,128)(2,1)S(1)} %get-tuple-element.65), channel_id=1, source_target_pairs={{4,8},{8,4},{12,16},{16,12},{20,24},{24,20},{28,32},{32,28},{36,40... | collective-permute-start | bytes 196616 | tf_op jit(solution)/shard_map/ppermute | solution.py:377
  53.2 0.7 copy-start.2
  53.2 5.2 %collective-permute-start.9 = (bf16[4,128,128]{2,1,0:T(8,128)(2,1)S(1)}, bf16[4,128,128]{2,1,0:T(8,128)(2,1)S(1)}, u32[]{:S(2)}, u32[]{:S(2)}) collective-permute-start(bf16[4,128,128]{2,1,0:T(8,128)(2,1)S(1)} %get-tuple-element.67), channel_id=1, source_target_pairs={{0,1},{1,0},{2,3},{3,2},{4,5},{5,4},{6,7},{7,6},{8,9},{9,8},{10,11... | collective-permute-start | bytes 393224 | tf_op jit(solution)/shard_map/ppermute | solution.py:377
  54.0 7.9 %collective-permute-start.8 = (bf16[4,128,128]{2,1,0:T(8,128)(2,1)S(1)}, bf16[4,128,128]{2,1,0:T(8,128)(2,1)S(1)}, u32[]{:S(2)}, u32[]{:S(2)}) collective-permute-start(bf16[4,128,128]{2,1,0:T(8,128)(2,1)S(1)} %get-tuple-element.66), channel_id=1, source_target_pairs={{1,2},{2,1},{5,6},{6,5},{9,10},{10,9},{13,14},{14,13},{17,18},{18,... | collective-permute-start | bytes 393224 | tf_op jit(solution)/shard_map/ppermute | solution.py:377
  58.4 3.5 %copy-start.1 = (f32[2,2,2,128]{3,2,1,0:T(2,128)S(1)}, f32[2,2,2,128]{3,2,1,0:T(2,128)}, u32[]{:S(2)}) copy-start(f32[2,2,2,128]{3,2,1,0:T(2,128)} %velocity.1) | copy-start | bytes 12292
  61.9 0.7 %copy-start = (f32[2,2,2,128]{3,2,1,0:T(2,128)S(1)}, f32[2,2,2,128]{3,2,1,0:T(2,128)}, u32[]{:S(2)}) copy-start(f32[2,2,2,128]{3,2,1,0:T(2,128)} %position.1) | copy-start | bytes 12292

commit v5 on v4

--- a/solution.py
+++ b/solution.py
@@ -16,6 +16,7 @@
 PACK = 48
 GEO = 16
 WIDE = 8
+UNROLL = 4
 BLOCKED = -(2.0**40)
 bf16 = jnp.bfloat16
 f32 = jnp.float32
@@ -79,7 +80,8 @@
 
 
 def weights_kernel(token, *refs):
-    sources, outs, (geo_w, sems) = refs[:9], refs[9:17], refs[17:]
+    count = len(refs) // 2
+    sources, outs, (geo_w, sems) = refs[:count], refs[count:-2], refs[-2:]
     full_w = outs[0]
     targets = (full_w.at[:, 0:LAT, :], geo_w, *outs[1:])
     copies = [pltpu.make_async_copy(source, target, sems.at[k]) for k, (source, target) in enumerate(zip(sources, targets))]
@@ -134,17 +136,16 @@
     slot = codes & (SLOTS - 1)
     hot = one_hot(window, slot, [number for number, _ in tiles])
     got = jnp.dot(jnp.concatenate([tile for _, tile in tiles], axis=1), hot, preferred_element_type=f32)
-    if direct is None:
-        return got
-    number, tile = direct
-    tile = tile.astype(f32)
     parts = []
     for k in range(codes.shape[1] // SLOTS):
         lanes = slice(k * SLOTS, (k + 1) * SLOTS)
-        index = jnp.broadcast_to(slot[:, lanes], tile.shape)
-        here = jnp.broadcast_to(window[:, lanes], tile.shape) == number
-        moved = jnp.take_along_axis(tile, index, axis=1, mode="promise_in_bounds")
-        parts.append(jnp.where(here, moved, got[:, lanes]))
+        part = got[:, lanes]
+        index = jnp.broadcast_to(slot[:, lanes], part.shape)
+        for number, tile in direct:
+            here = jnp.broadcast_to(window[:, lanes], part.shape) == number
+            moved = jnp.take_along_axis(tile.astype(f32), index, axis=1, mode="promise_in_bounds")
+            part = jnp.where(here, moved, part)
+        parts.append(part)
     return jnp.concatenate(parts, axis=1)
 
 
@@ -210,14 +211,14 @@
         bound = bounds[:, columns]
         total = None
         for part in range(KNB // WIDE):
-            got = pick(lane_rows(codes, part * WIDE, WIDE), tiles[:-1], tiles[-1])
+            got = pick(lane_rows(codes, part * WIDE, WIDE), tiles[:-1], tiles[-1:])
             geo = geometry_rows(got[LAT:], own_x, own_y, own_live)
             geo_out[a, :, part * WIDE * SLOTS : (part + 1) * WIDE * SLOTS] = geo
             total = edge_sum(full_w[0], jnp.concatenate([got[:LAT].astype(bf16), geo], axis=0), bound, total)
         sums[:, columns] = (total - KNB * bound).astype(bf16)
         return carry
 
-    lax.fori_loop(0, 4, one_bin, 0)
+    lax.fori_loop(0, 4, one_bin, 0, unroll=UNROLL)
 
 
 def first_early_kernel(
@@ -276,14 +277,14 @@
         total = None
         for part in range(KNB // WIDE):
             columns = slice(part * WIDE * SLOTS, (part + 1) * WIDE * SLOTS)
-            got = pick(lane_rows(own_codes[a, 1 - q], part * WIDE, WIDE), tiles[:-1], tiles[-1]).astype(bf16)
+            got = pick(lane_rows(own_codes[a, 1 - q], part * WIDE, WIDE), tiles[:-1], tiles[-1:]).astype(bf16)
             total = edge_sum(full_w[t], jnp.concatenate([got, geo_c[1 + a, :, columns]], axis=0), bound, total)
         sums_c[:, a * SLOTS : (a + 1) * SLOTS] = (total - KNB * bound).astype(bf16)
     for a in range(2):
         tiles = inner_tiles(q, a, lambda i, j: inner[i, j])
         for part in range(KNB // WIDE):
             columns = slice(part * WIDE * SLOTS, (part + 1) * WIDE * SLOTS)
-            gathered_d[a, :, columns] = pick(lane_rows(own_codes[a, q], part * WIDE, WIDE), tiles, None).astype(bf16)
+            gathered_d[a, :, columns] = pick(lane_rows(own_codes[a, q], part * WIDE, WIDE), tiles, []).astype(bf16)
 
 
 def middle_early_kernel(wide, got_c, own_codes, geo_c, recv_w, full_w, sums_c, gathered_d, bounds_d):
@@ -309,7 +310,7 @@
         total = None
         for part in range(KNB // WIDE):
             columns = slice(part * WIDE * SLOTS, (part + 1) * WIDE * SLOTS)
-            got = pick(lane_rows(own_codes[a, q], part * WIDE, WIDE), tiles[:-1], tiles[-1]).astype(bf16)
+            got = pick(lane_rows(own_codes[a, q], part * WIDE, WIDE), tiles[:-1], tiles[-1:]).astype(bf16)
             rows = jnp.concatenate([got + gathered_d[a, :, columns], geo_d[1 + a, :, columns]], axis=0)
             total = edge_sum(full_w[t], rows, bound, total)
         sums.append((total - KNB * bound).astype(bf16))
@@ -339,7 +340,7 @@
     own_all = jnp.concatenate([own[a, s] for s in (1 - q, q) for a in range(2)], axis=1)
     latent = late_part(2, own_all, got_d, own_codes, geo_d, sums_c, gathered_d, bounds_d, full_w, out_w, first_w, second_w)
     hidden = jnp.maximum(tdot(dec_first[...], latent), 0.0).astype(bf16)
-    accel = tdot(dec_second[...], hidden)
+    accel = jnp.dot(dec_second[...], hidden, preferred_element_type=f32)
     for b in range(4):
         a, c = b % 2, (1 - q, q)[b // 2]
         live = raw[a, c, 32:PACK].astype(f32)[6:7]
@@ -421,15 +422,17 @@
         inputs,
         range(5),
     )
-    got_b, got_a = swap(send_b, "slab", 1), swap(send_a, "slab", 0)
-    plain = (edge_recv, edge_out, node_first, node_second, enc_first, enc_second, dec_first)
-    full_w, recv_w, out_w, first_w, second_w, enc_one, enc_two, dec_one = run(
+    got_a, got_b = swap(send_a, "slab", 0), swap(send_b, "slab", 1)
+    plain = (
+        edge_recv, edge_out, node_first, node_second, enc_first, enc_second, dec_first, dec_second.T, position, velocity
+    )
+    full_w, recv_w, out_w, first_w, second_w, enc_one, enc_two, dec_one, dec_two, place, speed = run(
         weights_kernel,
         "weights",
         [((steps, LAT + GEO, EH), bf16), *[whole(w) for w in plain]],
-        [whole(edge_geo), pltpu.SemaphoreType.DMA((9,))],
+        [whole(edge_geo), pltpu.SemaphoreType.DMA((2 + len(plain),))],
         (own_codes, edge_send, edge_geo, *plain),
-        range(1, 10),
+        range(1, 3 + len(plain)),
         1 << 30,
     )
     send_c, send_d = run(pack_raw_kernel, "pack_raw", [raw_column] * 2, [], (raw, got_a, got_b, enc_one))
@@ -468,7 +471,7 @@
         [],
         (wide, got_d, own_codes, geo_d, *parts, full_w, out_w, first_w, second_w),
     )
-    got_b, got_a = swap(send_b, "slab", 1), swap(send_a, "slab", 0)
+    got_a, got_b = swap(send_a, "slab", 0), swap(send_b, "slab", 1)
     send_c, send_d = run(pack_kernel, "pack", [column] * 2, [], (latent, got_a, got_b))
     got_d, got_c = swap(send_d, "cross", 1), swap(send_c, "cross", 0)
     parts = run(
@@ -487,7 +490,7 @@
             "last_step",
             [((2, 2, 2, SLOTS), f32)] * 2,
             [],
-            (*operands, raw, position, velocity, dec_one, dec_second),
+            (*operands, raw, place, speed, dec_one, dec_two),
         )
     )
 

time: 66.3 us -> 63.2 us (0.953)
  Pallas kernels: 29.7 us -> 28 us
  local copies, waits for them, and re-layouts: 1.35 us -> 0 us
    pallas_call x10, Pallas kernels: 29.7 us -> 28 us  [run(): pl.pallas_call(kernel, out_shape=[jax.ShapeDtypeStruct(shape, dtype) for...]
    unnamed x7 -> x0, local copies, waits for them, and re-layouts: 1.35 us -> none
where the time goes in v5:
time: 63.2 us; the launch traced here: 62.9 us
  starting transfers between devices  31.4 us (50%)
  Pallas kernels  28 us (44%)
  waiting for transfers between devices  2.68 us (4%)
  between operations  0.81 us (1%)
    ppermute x10, starting transfers between devices, swap(): return lax.ppermute(block, axis, swaps(lax.axis_size(axis), start))  31.4 us
    pallas_call x10, Pallas kernels, run(): pl.pallas_call(kernel, out_shape=[jax.ShapeDtypeStruct(shape, dtype) for...  28 us
    ppermute x10, waiting for transfers between devices, swap(): return lax.ppermute(block, axis, swaps(lax.axis_size(axis), start))  2.68 us
  transfers between devices with their start and end apart: 10, of which 3 were waited for; matrix products, arithmetic and copies ran while one was open for 0% of the time, Pallas kernels for 24%

profile of v5, /device:TPU:17, one launch (start us, length us, event | category | flops | bytes accessed | tf_op | source)
XLA Modules:
  0.0 62.9 jit_solution(15042540570154636701)
XLA Ops:
  0.6 1.0 %prepare.1 = (bf16[2,2,48,128]{3,2,1,0:T(8,128)(2,1)S(1)}, s32[2,2,16,128]{3,2,1,0:T(8,128)S(1)}, bf16[2,128,128]{2,1,0:T(8,128)(2,1)S(1)}, bf16[2,128,128]{2,1,0:T(8,128)(2,1)S(1)}) custom-call(bf16[2,30,2,128]{3,2,1,0:T(2,128)(2,1)} %bitcast.2, f32[2,2,2,128]{3,2,1,0:T(2,128)} %refs_10_.1, s32[2,2]{1,0:T(2,128)} %occupancy_in.1, ...), custom_call_target="tpu_custom_call" | custom-call | tf_op jit(solution)/shard_map/prepare/pallas_call | solution.py:358
  1.6 1.3 %collective-permute-start = (bf16[2,128,128]{2,1,0:T(8,128)(2,1)S(1)}, bf16[2,128,128]{2,1,0:T(8,128)(2,1)S(1)}, u32[]{:S(2)}, u32[]{:S(2)}) collective-permute-start(bf16[2,128,128]{2,1,0:T(8,128)(2,1)S(1)} %get-tuple-element.41), channel_id=1, source_target_pairs={{0,4},{4,0},{8,12},{12,8},{16,20},{20,16},{24,28},{28,24},{32,36},... | collective-permute-start | bytes 196616 | tf_op jit(solution)/shard_map/ppermute | solution.py:378
  2.9 8.8 %collective-permute-start.1 = (bf16[2,128,128]{2,1,0:T(8,128)(2,1)S(1)}, bf16[2,128,128]{2,1,0:T(8,128)(2,1)S(1)}, u32[]{:S(2)}, u32[]{:S(2)}) collective-permute-start(bf16[2,128,128]{2,1,0:T(8,128)(2,1)S(1)} %get-tuple-element.42), channel_id=1, source_target_pairs={{4,8},{8,4},{12,16},{16,12},{20,24},{24,20},{28,32},{32,28},{36,40... | collective-permute-start | bytes 196616 | tf_op jit(solution)/shard_map/ppermute | solution.py:378
  11.7 1.5 %weights.1 = (bf16[3,144,512]{2,1,0:T(8,128)(2,1)S(1)}, bf16[3,128,512]{2,1,0:T(8,128)(2,1)S(1)}, bf16[3,512,128]{2,1,0:T(8,128)(2,1)S(1)}, bf16[3,256,128]{2,1,...) custom-call(s32[2,2,16,128]{3,2,1,0:T(8,128)S(1)} %get-tuple-element, ...), custom_call_target="tpu_custom_call" | custom-call | flops 1073741824 | bytes 4194304 | tf_op jit(solution)/shard_map/weights/pallas_call | solution.py:358
  13.2 0.4 collective-permute-done.1.got_b
  13.6 2.2 %collective-permute-start.2 = (bf16[6,48,128]{2,1,0:T(8,128)(2,1)S(1)}, bf16[6,48,128]{2,1,0:T(8,128)(2,1)S(1)}, u32[]{:S(2)}, u32[]{:S(2)}) collective-permute-start(bf16[6,48,128]{2,1,0:T(8,128)(2,1)S(1)} %get-tuple-element.45), channel_id=1, source_target_pairs={{0,1},{1,0},{2,3},{3,2},{4,5},{5,4},{6,7},{7,6},{8,9},{9,8},{10,11... | collective-permute-start | bytes 221192 | tf_op jit(solution)/shard_map/ppermute | solution.py:378
  15.8 3.1 %collective-permute-start.3 = (bf16[6,48,128]{2,1,0:T(8,128)(2,1)S(1)}, bf16[6,48,128]{2,1,0:T(8,128)(2,1)S(1)}, u32[]{:S(2)}, u32[]{:S(2)}) collective-permute-start(bf16[6,48,128]{2,1,0:T(8,128)(2,1)S(1)} %get-tuple-element.54), channel_id=1, source_target_pairs={{1,2},{2,1},{5,6},{6,5},{9,10},{10,9},{13,14},{14,13},{17,18},{18,... | collective-permute-start | bytes 221192 | tf_op jit(solution)/shard_map/ppermute | solution.py:378
  19.0 0.0 collective-permute-done.2.got_c
  19.0 6.5 %first_early.1 = (bf16[6,2,48,128]{3,2,1,0:T(8,128)(2,1)S(1)}, s32[4,2,16,128]{3,2,1,0:T(8,128)S(1)}, bf16[6,2,128,128]{3,2,1,0:T(8,128)(2,1)S(1)}, f32[512,512]...) custom-call(bf16[2,2,48,128]{3,2,1,0:T(8,128)(2,1)S(1)} %get-tuple-element.40.own.raw, ...), custom_call_target="tpu_custom_call" | custom-call | flops 2147483648 | bytes 4194304 | tf_op jit(solution)/shard_map/first_early/pallas_call | solution.py:358
  25.5 0.0 collective-permute-done.3.got_d
  25.5 6.2 %first_step.1 = (bf16[4,2,128,128]{3,2,1,0:T(8,128)(2,1)S(1)}, bf16[4,16,2048]{2,1,0:T(8,128)(2,1)S(1)}, bf16[4,128,128]{2,1,0:T(8,128)(2,1)S(1)}, bf16[4,128,128]{2,1,0:T(8,128)(2,1)S(1)}) custom-call(bf16[6,2,48,128]{3,2,1,0:T(8,128)(2,1)S(1)} %get-tuple-element.49.pack, s32[4,2,16,128]{3,2,1,0:T(8,128)S(1)} %get-tuple-element.50.codes_all, ...), custom_call_target="tpu_custom_call" | custom-call | tf_op jit(solution)/shard_map/first_step/pallas_call | solution.py:358
  31.7 0.3 collective-permute-start.5
  32.0 2.4 %collective-permute-start.4 = (bf16[4,128,128]{2,1,0:T(8,128)(2,1)S(1)}, bf16[4,128,128]{2,1,0:T(8,128)(2,1)S(1)}, u32[]{:S(2)}, u32[]{:S(2)}) collective-permute-start(bf16[4,128,128]{2,1,0:T(8,128)(2,1)S(1)} %get-tuple-element.59), channel_id=1, source_target_pairs={{1,2},{2,1},{5,6},{6,5},{9,10},{10,9},{13,14},{14,13},{17,18},{18,... | collective-permute-start | bytes 393224 | tf_op jit(solution)/shard_map/ppermute | solution.py:378
  34.4 3.5 %middle_early.1 = (bf16[512,256]{1,0:T(8,128)(2,1)S(1)}, bf16[2,128,2048]{2,1,0:T(8,128)(2,1)S(1)}, f32[512,256]{1,0:T(8,128)S(1)}) custom-call(bf16[4,2,128,128]{3,2,1,0:T(8,128)(2,1)S(1)} %get-tuple-element.58.wide, bf16[4,128,128]{2,1,0:T(8,128)(2,1)S(1)} %collective-permute-done.5.got_c, s32[2,2,16,128]{3,2,1,0:T(8,128)S(1)} %get-tuple-element.43.token.own_codes, ...), custom_call_target="tpu_custom_call" | custom-call | flops 2147483648 | bytes 4194304 | tf_op jit(solution)/shard_map/middle_early/pallas_call | solution.py:358
  37.9 0.4 collective-permute-done.4.got_d
  38.3 2.5 %middle_step.1 = (bf16[2,2,128,128]{3,2,1,0:T(8,128)(2,1)S(1)}, bf16[2,128,128]{2,1,0:T(8,128)(2,1)S(1)}, bf16[2,128,128]{2,1,0:T(8,128)(2,1)S(1)}) custom-call(bf16[4,2,128,128]{3,2,1,0:T(8,128)(2,1)S(1)} %get-tuple-element.58.wide, bf16[4,128,128]{2,1,0:T(8,128)(2,1)S(1)} %collective-permute-done.4.got_d, ...), custom_call_target="tpu_custom_call" | custom-call | tf_op jit(solution)/shard_map/middle_step/pallas_call | solution.py:358
  40.8 0.1 collective-permute-start.6
  40.9 8.8 %collective-permute-start.7 = (bf16[2,128,128]{2,1,0:T(8,128)(2,1)S(1)}, bf16[2,128,128]{2,1,0:T(8,128)(2,1)S(1)}, u32[]{:S(2)}, u32[]{:S(2)}) collective-permute-start(bf16[2,128,128]{2,1,0:T(8,128)(2,1)S(1)} %get-tuple-element.68), channel_id=1, source_target_pairs={{4,8},{8,4},{12,16},{16,12},{20,24},{24,20},{28,32},{32,28},{36,40... | collective-permute-start | bytes 196616 | tf_op jit(solution)/shard_map/ppermute | solution.py:378
  49.7 0.0 collective-permute-done.6.got_a
  49.7 1.9 %collective-permute-done.7.got_b = bf16[2,128,128]{2,1,0:T(8,128)(2,1)S(1)} collective-permute-done((bf16[2,128,128]{2,1,0:T(8,128)(2,1)S(1)}, bf16[2,128,128]{2,1,0:T(8,128)(2,1)S(1)}, u32[]{:S(2)}, u32[]{:S(2)}) %collective-permute-start.7) | collective-permute-done | bytes 65568 | tf_op jit(solution)/shard_map/ppermute | solution.py:378
  51.6 0.1 collective-permute-start.9
  51.7 4.2 %collective-permute-start.8 = (bf16[4,128,128]{2,1,0:T(8,128)(2,1)S(1)}, bf16[4,128,128]{2,1,0:T(8,128)(2,1)S(1)}, u32[]{:S(2)}, u32[]{:S(2)}) collective-permute-start(bf16[4,128,128]{2,1,0:T(8,128)(2,1)S(1)} %get-tuple-element.69), channel_id=1, source_target_pairs={{1,2},{2,1},{5,6},{6,5},{9,10},{10,9},{13,14},{14,13},{17,18},{18,... | collective-permute-start | bytes 393224 | tf_op jit(solution)/shard_map/ppermute | solution.py:378
  56.0 3.5 %last_early.1 = (bf16[512,256]{1,0:T(8,128)(2,1)S(1)}, bf16[2,128,2048]{2,1,0:T(8,128)(2,1)S(1)}, f32[512,256]{1,0:T(8,128)S(1)}) custom-call(bf16[2,2,128,128]{3,2,1,0:T(8,128)(2,1)S(1)} %get-tuple-element.66.own, bf16[2,128,128]{2,1,0:T(8,128)(2,1)S(1)} %collective-permute-done.6.got_a, bf16[2,128,128]{2,1,0:T(8,128)(2,1)S(1)} %collective-permute-done.7.got_b, ...), custom_call_target="tpu_custom_call" | custom-call | flops 2147483648 | bytes 4194304 | tf_op jit(solution)/shard_map/last_early/pallas_call | solution.py:358
  59.5 3.4 %last_step.1 = (f32[2,2,2,128]{3,2,1,0:T(2,128)}, f32[2,2,2,128]{3,2,1,0:T(2,128)}) custom-call(bf16[2,2,128,128]{3,2,1,0:T(8,128)(2,1)S(1)} %get-tuple-element.66.own, bf16[4,128,128]{2,1,0:T(8,128)(2,1)S(1)} %collective-permute-done.8.got_d, s32[2,2,16,128]{3,2,1,0:T(8,128)S(1)} %get-tuple-element.43.token.own_codes, ...), custom_call_target="tpu_custom_call" | custom-call | tf_op jit(solution)/shard_map/last_step/pallas_call | solution.py:358
  (6 shorter events, 0.0 us)
Async XLA Ops:
  1.6 11.6 %collective-permute-start = (bf16[2,128,128]{2,1,0:T(8,128)(2,1)S(1)}, bf16[2,128,128]{2,1,0:T(8,128)(2,1)S(1)}, u32[]{:S(2)}, u32[]{:S(2)}) collective-permute-start(bf16[2,128,128]{2,1,0:T(8,128)(2,1)S(1)} %get-tuple-element.41), channel_id=1, source_target_pairs={{0,4},{4,0},{8,12},{12,8},{16,20},{20,16},{24,28},{28,24},{32,36},... | collective-permute-start | bytes 196616 | tf_op jit(solution)/shard_map/ppermute | solution.py:378
  2.9 10.7 %collective-permute-start.1 = (bf16[2,128,128]{2,1,0:T(8,128)(2,1)S(1)}, bf16[2,128,128]{2,1,0:T(8,128)(2,1)S(1)}, u32[]{:S(2)}, u32[]{:S(2)}) collective-permute-start(bf16[2,128,128]{2,1,0:T(8,128)(2,1)S(1)} %get-tuple-element.42), channel_id=1, source_target_pairs={{4,8},{8,4},{12,16},{16,12},{20,24},{24,20},{28,32},{32,28},{36,40... | collective-permute-start | bytes 196616 | tf_op jit(solution)/shard_map/ppermute | solution.py:378
  13.6 5.3 %collective-permute-start.2 = (bf16[6,48,128]{2,1,0:T(8,128)(2,1)S(1)}, bf16[6,48,128]{2,1,0:T(8,128)(2,1)S(1)}, u32[]{:S(2)}, u32[]{:S(2)}) collective-permute-start(bf16[6,48,128]{2,1,0:T(8,128)(2,1)S(1)} %get-tuple-element.45), channel_id=1, source_target_pairs={{0,1},{1,0},{2,3},{3,2},{4,5},{5,4},{6,7},{7,6},{8,9},{9,8},{10,11... | collective-permute-start | bytes 221192 | tf_op jit(solution)/shard_map/ppermute | solution.py:378
  15.8 9.6 %collective-permute-start.3 = (bf16[6,48,128]{2,1,0:T(8,128)(2,1)S(1)}, bf16[6,48,128]{2,1,0:T(8,128)(2,1)S(1)}, u32[]{:S(2)}, u32[]{:S(2)}) collective-permute-start(bf16[6,48,128]{2,1,0:T(8,128)(2,1)S(1)} %get-tuple-element.54), channel_id=1, source_target_pairs={{1,2},{2,1},{5,6},{6,5},{9,10},{10,9},{13,14},{14,13},{17,18},{18,... | collective-permute-start | bytes 221192 | tf_op jit(solution)/shard_map/ppermute | solution.py:378
  31.7 2.7 %collective-permute-start.5 = (bf16[4,128,128]{2,1,0:T(8,128)(2,1)S(1)}, bf16[4,128,128]{2,1,0:T(8,128)(2,1)S(1)}, u32[]{:S(2)}, u32[]{:S(2)}) collective-permute-start(bf16[4,128,128]{2,1,0:T(8,128)(2,1)S(1)} %get-tuple-element.61), channel_id=1, source_target_pairs={{0,1},{1,0},{2,3},{3,2},{4,5},{5,4},{6,7},{7,6},{8,9},{9,8},{10,11... | collective-permute-start | bytes 393224 | tf_op jit(solution)/shard_map/ppermute | solution.py:378
  32.0 6.3 %collective-permute-start.4 = (bf16[4,128,128]{2,1,0:T(8,128)(2,1)S(1)}, bf16[4,128,128]{2,1,0:T(8,128)(2,1)S(1)}, u32[]{:S(2)}, u32[]{:S(2)}) collective-permute-start(bf16[4,128,128]{2,1,0:T(8,128)(2,1)S(1)} %get-tuple-element.59), channel_id=1, source_target_pairs={{1,2},{2,1},{5,6},{6,5},{9,10},{10,9},{13,14},{14,13},{17,18},{18,... | collective-permute-start | bytes 393224 | tf_op jit(solution)/shard_map/ppermute | solution.py:378
  40.8 9.0 %collective-permute-start.6 = (bf16[2,128,128]{2,1,0:T(8,128)(2,1)S(1)}, bf16[2,128,128]{2,1,0:T(8,128)(2,1)S(1)}, u32[]{:S(2)}, u32[]{:S(2)}) collective-permute-start(bf16[2,128,128]{2,1,0:T(8,128)(2,1)S(1)} %get-tuple-element.67), channel_id=1, source_target_pairs={{0,4},{4,0},{8,12},{12,8},{16,20},{20,16},{24,28},{28,24},{32,36},... | collective-permute-start | bytes 196616 | tf_op jit(solution)/shard_map/ppermute | solution.py:378
  40.9 10.7 %collective-permute-start.7 = (bf16[2,128,128]{2,1,0:T(8,128)(2,1)S(1)}, bf16[2,128,128]{2,1,0:T(8,128)(2,1)S(1)}, u32[]{:S(2)}, u32[]{:S(2)}) collective-permute-start(bf16[2,128,128]{2,1,0:T(8,128)(2,1)S(1)} %get-tuple-element.68), channel_id=1, source_target_pairs={{4,8},{8,4},{12,16},{16,12},{20,24},{24,20},{28,32},{32,28},{36,40... | collective-permute-start | bytes 196616 | tf_op jit(solution)/shard_map/ppermute | solution.py:378
  51.6 4.4 %collective-permute-start.9 = (bf16[4,128,128]{2,1,0:T(8,128)(2,1)S(1)}, bf16[4,128,128]{2,1,0:T(8,128)(2,1)S(1)}, u32[]{:S(2)}, u32[]{:S(2)}) collective-permute-start(bf16[4,128,128]{2,1,0:T(8,128)(2,1)S(1)} %get-tuple-element.70), channel_id=1, source_target_pairs={{0,1},{1,0},{2,3},{3,2},{4,5},{5,4},{6,7},{7,6},{8,9},{9,8},{10,11... | collective-permute-start | bytes 393224 | tf_op jit(solution)/shard_map/ppermute | solution.py:378
  51.7 7.7 %collective-permute-start.8 = (bf16[4,128,128]{2,1,0:T(8,128)(2,1)S(1)}, bf16[4,128,128]{2,1,0:T(8,128)(2,1)S(1)}, u32[]{:S(2)}, u32[]{:S(2)}) collective-permute-start(bf16[4,128,128]{2,1,0:T(8,128)(2,1)S(1)} %get-tuple-element.69), channel_id=1, source_target_pairs={{1,2},{2,1},{5,6},{6,5},{9,10},{10,9},{13,14},{14,13},{17,18},{18,... | collective-permute-start | bytes 393224 | tf_op jit(solution)/shard_map/ppermute | solution.py:378

commit v6 on v5

--- a/solution.py
+++ b/solution.py
@@ -52,9 +52,9 @@
     return jnp.concatenate([values] * count, axis=1)
 
 
-def prepare_kernel(features_in, position_in, occupancy_in, codes_in, mask_in, raw, own_codes, send_a, send_b,
-                   features, position, occupancy, codes, mask, sems):
-    pairs = ((features_in, features), (position_in, position), (occupancy_in, occupancy), (codes_in, codes), (mask_in, mask))
+def prepare_kernel(features, position_in, occupancy_in, codes_in, mask_in, raw, own_codes, send_a, send_b,
+                   position, occupancy, codes, mask, sems):
+    pairs = ((position_in, position), (occupancy_in, occupancy), (codes_in, codes), (mask_in, mask))
     copies = [pltpu.make_async_copy(source, target, sems.at[k]) for k, (source, target) in enumerate(pairs)]
     for copy in copies:
         copy.start()
@@ -412,21 +412,20 @@
         "prepare",
         [((2, 2, PACK, SLOTS), bf16), ((2, 2, KNB, SLOTS), i32), side, side],
         [
-            whole(features),
             whole(position),
             pltpu.SMEM(occupancy.shape, i32),
             whole(neighbor_codes),
             whole(edge_mask),
-            pltpu.SemaphoreType.DMA((5,)),
+            pltpu.SemaphoreType.DMA((4,)),
         ],
         inputs,
-        range(5),
+        range(1, 5),
     )
     got_a, got_b = swap(send_a, "slab", 0), swap(send_b, "slab", 1)
     plain = (
-        edge_recv, edge_out, node_first, node_second, enc_first, enc_second, dec_first, dec_second.T, position, velocity
-    )
-    full_w, recv_w, out_w, first_w, second_w, enc_one, enc_two, dec_one, dec_two, place, speed = run(
+        edge_recv, edge_out, node_first, node_second, enc_second, dec_first, position, velocity
+    )
+    full_w, recv_w, out_w, first_w, second_w, enc_two, dec_one, place, speed = run(
         weights_kernel,
         "weights",
         [((steps, LAT + GEO, EH), bf16), *[whole(w) for w in plain]],
@@ -435,7 +434,7 @@
         range(1, 3 + len(plain)),
         1 << 30,
     )
-    send_c, send_d = run(pack_raw_kernel, "pack_raw", [raw_column] * 2, [], (raw, got_a, got_b, enc_one))
+    send_c, send_d = run(pack_raw_kernel, "pack_raw", [raw_column] * 2, [], (raw, got_a, got_b, enc_two))
     got_d, got_c = swap(send_d, "cross", 1), swap(send_c, "cross", 0)
     pack, codes_all, inner, bounds_d, sums_c, geo_c = run(
         first_early_kernel,
@@ -449,7 +448,7 @@
             geometry,
         ],
         [((6, *tile), bf16), ((EH, 4 * SLOTS), f32)],
-        (raw, got_a, got_b, got_c, own_codes, enc_one, enc_two, recv_w, full_w),
+        (raw, got_a, got_b, got_c, own_codes, enc_first, enc_two, recv_w, full_w),
         (),
         1 << 31,
     )
@@ -458,7 +457,7 @@
         "first_step",
         [((4, 2, *tile), bf16), geometry, column, column],
         [((6, *tile), bf16), ((EH, 4 * SLOTS), bf16)],
-        (pack, codes_all, inner, bounds_d, sums_c, got_d, enc_one, enc_two, full_w, out_w, first_w, second_w),
+        (pack, codes_all, inner, bounds_d, sums_c, got_d, enc_first, enc_two, full_w, out_w, first_w, second_w),
     )
     got_d, got_c = swap(send_d, "cross", 1), swap(send_c, "cross", 0)
     parts = run(
@@ -490,7 +489,7 @@
             "last_step",
             [((2, 2, 2, SLOTS), f32)] * 2,
             [],
-            (*operands, raw, place, speed, dec_one, dec_two),
+            (*operands, raw, place, speed, dec_one, dec_second.T),
         )
     )
 

time: 63.2 us -> 64.7 us (1.024)
  local copies, waits for them, and re-layouts: 0 us -> 1.4 us
    unnamed x0 -> x6, local copies, waits for them, and re-layouts: none -> 1.4 us
  transfers between devices with their start and end apart: 10 -> 10, of which waited for: 3 -> 3; matrix products, arithmetic and copies ran while one was open for 0% -> 0% of each run, Pallas kernels for 24% -> 23%
where the time goes in v6:
time: 64.7 us; the launch traced here: 64.3 us
  starting transfers between devices  31.4 us (49%)
  Pallas kernels  28 us (43%)
  waiting for transfers between devices  2.7 us (4%)
  local copies, waits for them, and re-layouts  1.4 us (2%)
  between operations  0.83 us (1%)
    ppermute x10, starting transfers between devices, swap(): return lax.ppermute(block, axis, swaps(lax.axis_size(axis), start))  31.4 us
    pallas_call x10, Pallas kernels, run(): pl.pallas_call(kernel, out_shape=[jax.ShapeDtypeStruct(shape, dtype) for...  28 us
    ppermute x10, waiting for transfers between devices, swap(): return lax.ppermute(block, axis, swaps(lax.axis_size(axis), start))  2.7 us
    unnamed x6, local copies, waits for them, and re-layouts  1.4 us
  transfers between devices with their start and end apart: 10, of which 3 were waited for; matrix products, arithmetic and copies ran while one was open for 0% of the time, Pallas kernels for 23%

profile of v6, /device:TPU:17, one launch (start us, length us, event | category | flops | bytes accessed | tf_op | source)
XLA Modules:
  0.0 64.3 jit_solution(1541781111158338716)
XLA Ops:
  0.6 0.7 %copy-done = bf16[2,2,30,128]{3,1,2,0:T(2,128)(2,1)S(1)} copy-done((bf16[2,2,30,128]{3,1,2,0:T(2,128)(2,1)S(1)}, bf16[2,2,30,128]{3,1,2,0:T(2,128)(2,1)}, u32[]{:S(2)}) %copy-start) | copy-done | bytes 30744
  1.4 1.0 %prepare.1 = (bf16[2,2,48,128]{3,2,1,0:T(8,128)(2,1)S(1)}, s32[2,2,16,128]{3,2,1,0:T(8,128)S(1)}, bf16[2,128,128]{2,1,0:T(8,128)(2,1)S(1)}, bf16[2,128,128]{2,1,0:T(8,128)(2,1)S(1)}) custom-call(bf16[2,30,2,128]{3,2,1,0:T(2,128)(2,1)S(1)} %bitcast.2, f32[2,2,2,128]{3,2,1,0:T(2,128)} %refs_8_.1, s32[2,2]{1,0:T(2,128)} %occupancy_in.1, ...), custom_call_target="tpu_custom_call" | custom-call | tf_op jit(solution)/shard_map/prepare/pallas_call | solution.py:358
  2.4 1.3 %collective-permute-start = (bf16[2,128,128]{2,1,0:T(8,128)(2,1)S(1)}, bf16[2,128,128]{2,1,0:T(8,128)(2,1)S(1)}, u32[]{:S(2)}, u32[]{:S(2)}) collective-permute-start(bf16[2,128,128]{2,1,0:T(8,128)(2,1)S(1)} %get-tuple-element.39), channel_id=1, source_target_pairs={{0,4},{4,0},{8,12},{12,8},{16,20},{20,16},{24,28},{28,24},{32,36},... | collective-permute-start | bytes 196616 | tf_op jit(solution)/shard_map/ppermute | solution.py:378
  3.7 8.8 %collective-permute-start.1 = (bf16[2,128,128]{2,1,0:T(8,128)(2,1)S(1)}, bf16[2,128,128]{2,1,0:T(8,128)(2,1)S(1)}, u32[]{:S(2)}, u32[]{:S(2)}) collective-permute-start(bf16[2,128,128]{2,1,0:T(8,128)(2,1)S(1)} %get-tuple-element.40), channel_id=1, source_target_pairs={{4,8},{8,4},{12,16},{16,12},{20,24},{24,20},{28,32},{32,28},{36,40... | collective-permute-start | bytes 196616 | tf_op jit(solution)/shard_map/ppermute | solution.py:378
  12.4 1.5 %weights.1 = (bf16[3,144,512]{2,1,0:T(8,128)(2,1)S(1)}, bf16[3,128,512]{2,1,0:T(8,128)(2,1)S(1)}, bf16[3,512,128]{2,1,0:T(8,128)(2,1)S(1)}, bf16[3,256,128]{2,1,...) custom-call(s32[2,2,16,128]{3,2,1,0:T(8,128)S(1)} %get-tuple-element, ...), custom_call_target="tpu_custom_call" | custom-call | flops 1073741824 | bytes 4194304 | tf_op jit(solution)/shard_map/weights/pallas_call | solution.py:358
  13.9 0.4 collective-permute-done.1.got_b
  14.4 2.2 %collective-permute-start.2 = (bf16[6,48,128]{2,1,0:T(8,128)(2,1)S(1)}, bf16[6,48,128]{2,1,0:T(8,128)(2,1)S(1)}, u32[]{:S(2)}, u32[]{:S(2)}) collective-permute-start(bf16[6,48,128]{2,1,0:T(8,128)(2,1)S(1)} %get-tuple-element.43), channel_id=1, source_target_pairs={{0,1},{1,0},{2,3},{3,2},{4,5},{5,4},{6,7},{7,6},{8,9},{9,8},{10,11... | collective-permute-start | bytes 221192 | tf_op jit(solution)/shard_map/ppermute | solution.py:378
  16.6 3.1 %collective-permute-start.3 = (bf16[6,48,128]{2,1,0:T(8,128)(2,1)S(1)}, bf16[6,48,128]{2,1,0:T(8,128)(2,1)S(1)}, u32[]{:S(2)}, u32[]{:S(2)}) collective-permute-start(bf16[6,48,128]{2,1,0:T(8,128)(2,1)S(1)} %get-tuple-element.51), channel_id=1, source_target_pairs={{1,2},{2,1},{5,6},{6,5},{9,10},{10,9},{13,14},{14,13},{17,18},{18,... | collective-permute-start | bytes 221192 | tf_op jit(solution)/shard_map/ppermute | solution.py:378
  19.7 6.5 %first_early.1 = (bf16[6,2,48,128]{3,2,1,0:T(8,128)(2,1)S(1)}, s32[4,2,16,128]{3,2,1,0:T(8,128)S(1)}, bf16[6,2,128,128]{3,2,1,0:T(8,128)(2,1)S(1)}, f32[512,512]...) custom-call(bf16[2,2,48,128]{3,2,1,0:T(8,128)(2,1)S(1)} %get-tuple-element.38.own.raw, ...), custom_call_target="tpu_custom_call" | custom-call | flops 2147483648 | bytes 4194304 | tf_op jit(solution)/shard_map/first_early/pallas_call | solution.py:358
  26.2 6.2 %first_step.1 = (bf16[4,2,128,128]{3,2,1,0:T(8,128)(2,1)S(1)}, bf16[4,16,2048]{2,1,0:T(8,128)(2,1)S(1)}, bf16[4,128,128]{2,1,0:T(8,128)(2,1)S(1)}, bf16[4,128,128]{2,1,0:T(8,128)(2,1)S(1)}) custom-call(bf16[6,2,48,128]{3,2,1,0:T(8,128)(2,1)S(1)} %get-tuple-element.46.pack, s32[4,2,16,128]{3,2,1,0:T(8,128)S(1)} %get-tuple-element.47.codes_all, ...), custom_call_target="tpu_custom_call" | custom-call | tf_op jit(solution)/shard_map/first_step/pallas_call | solution.py:358
  32.4 0.3 collective-permute-start.5
  32.7 2.4 %collective-permute-start.4 = (bf16[4,128,128]{2,1,0:T(8,128)(2,1)S(1)}, bf16[4,128,128]{2,1,0:T(8,128)(2,1)S(1)}, u32[]{:S(2)}, u32[]{:S(2)}) collective-permute-start(bf16[4,128,128]{2,1,0:T(8,128)(2,1)S(1)} %get-tuple-element.56), channel_id=1, source_target_pairs={{1,2},{2,1},{5,6},{6,5},{9,10},{10,9},{13,14},{14,13},{17,18},{18,... | collective-permute-start | bytes 393224 | tf_op jit(solution)/shard_map/ppermute | solution.py:378
  35.2 3.5 %middle_early.1 = (bf16[512,256]{1,0:T(8,128)(2,1)S(1)}, bf16[2,128,2048]{2,1,0:T(8,128)(2,1)S(1)}, f32[512,256]{1,0:T(8,128)S(1)}) custom-call(bf16[4,2,128,128]{3,2,1,0:T(8,128)(2,1)S(1)} %get-tuple-element.55.wide, bf16[4,128,128]{2,1,0:T(8,128)(2,1)S(1)} %collective-permute-done.5.got_c, s32[2,2,16,128]{3,2,1,0:T(8,128)S(1)} %get-tuple-element.41.token.own_codes, ...), custom_call_target="tpu_custom_call" | custom-call | flops 2147483648 | bytes 4194304 | tf_op jit(solution)/shard_map/middle_early/pallas_call | solution.py:358
  38.7 0.4 collective-permute-done.4.got_d
  39.0 2.5 %middle_step.1 = (bf16[2,2,128,128]{3,2,1,0:T(8,128)(2,1)S(1)}, bf16[2,128,128]{2,1,0:T(8,128)(2,1)S(1)}, bf16[2,128,128]{2,1,0:T(8,128)(2,1)S(1)}) custom-call(bf16[4,2,128,128]{3,2,1,0:T(8,128)(2,1)S(1)} %get-tuple-element.55.wide, bf16[4,128,128]{2,1,0:T(8,128)(2,1)S(1)} %collective-permute-done.4.got_d, ...), custom_call_target="tpu_custom_call" | custom-call | tf_op jit(solution)/shard_map/middle_step/pallas_call | solution.py:358
  41.5 0.1 collective-permute-start.6
  41.6 8.8 %collective-permute-start.7 = (bf16[2,128,128]{2,1,0:T(8,128)(2,1)S(1)}, bf16[2,128,128]{2,1,0:T(8,128)(2,1)S(1)}, u32[]{:S(2)}, u32[]{:S(2)}) collective-permute-start(bf16[2,128,128]{2,1,0:T(8,128)(2,1)S(1)} %get-tuple-element.65), channel_id=1, source_target_pairs={{4,8},{8,4},{12,16},{16,12},{20,24},{24,20},{28,32},{32,28},{36,40... | collective-permute-start | bytes 196616 | tf_op jit(solution)/shard_map/ppermute | solution.py:378
  50.5 1.9 %collective-permute-done.7.got_b = bf16[2,128,128]{2,1,0:T(8,128)(2,1)S(1)} collective-permute-done((bf16[2,128,128]{2,1,0:T(8,128)(2,1)S(1)}, bf16[2,128,128]{2,1,0:T(8,128)(2,1)S(1)}, u32[]{:S(2)}, u32[]{:S(2)}) %collective-permute-start.7) | collective-permute-done | bytes 65568 | tf_op jit(solution)/shard_map/ppermute | solution.py:378
  52.4 0.1 collective-permute-start.9
  52.5 4.2 %collective-permute-start.8 = (bf16[4,128,128]{2,1,0:T(8,128)(2,1)S(1)}, bf16[4,128,128]{2,1,0:T(8,128)(2,1)S(1)}, u32[]{:S(2)}, u32[]{:S(2)}) collective-permute-start(bf16[4,128,128]{2,1,0:T(8,128)(2,1)S(1)} %get-tuple-element.66), channel_id=1, source_target_pairs={{1,2},{2,1},{5,6},{6,5},{9,10},{10,9},{13,14},{14,13},{17,18},{18,... | collective-permute-start | bytes 393224 | tf_op jit(solution)/shard_map/ppermute | solution.py:378
  56.7 3.5 %last_early.1 = (bf16[512,256]{1,0:T(8,128)(2,1)S(1)}, bf16[2,128,2048]{2,1,0:T(8,128)(2,1)S(1)}, f32[512,256]{1,0:T(8,128)S(1)}) custom-call(bf16[2,2,128,128]{3,2,1,0:T(8,128)(2,1)S(1)} %get-tuple-element.63.own, bf16[2,128,128]{2,1,0:T(8,128)(2,1)S(1)} %collective-permute-done.6.got_a, bf16[2,128,128]{2,1,0:T(8,128)(2,1)S(1)} %collective-permute-done.7.got_b, ...), custom_call_target="tpu_custom_call" | custom-call | flops 2147483648 | bytes 4194304 | tf_op jit(solution)/shard_map/last_early/pallas_call | solution.py:358
  60.2 0.0 copy-start.2
  60.2 0.6 %copy-done.2 = bf16[128,2]{0,1:T(2,128)(2,1)S(1)} copy-done((bf16[128,2]{0,1:T(2,128)(2,1)S(1)}, bf16[128,2]{0,1:T(2,128)(2,1)}, u32[]{:S(2)}) %copy-start.2) | copy-done | bytes 536
  60.9 3.4 %last_step.1 = (f32[2,2,2,128]{3,2,1,0:T(2,128)}, f32[2,2,2,128]{3,2,1,0:T(2,128)}) custom-call(bf16[2,2,128,128]{3,2,1,0:T(8,128)(2,1)S(1)} %get-tuple-element.63.own, bf16[4,128,128]{2,1,0:T(8,128)(2,1)S(1)} %collective-permute-done.8.got_d, s32[2,2,16,128]{3,2,1,0:T(8,128)S(1)} %get-tuple-element.41.token.own_codes, ...), custom_call_target="tpu_custom_call" | custom-call | tf_op jit(solution)/shard_map/last_step/pallas_call | solution.py:358
  (12 shorter events, 0.1 us)
Async XLA Ops:
  0.6 0.8 %copy-start = (bf16[2,2,30,128]{3,1,2,0:T(2,128)(2,1)S(1)}, bf16[2,2,30,128]{3,1,2,0:T(2,128)(2,1)}, u32[]{:S(2)}) copy-start(bf16[2,2,30,128]{3,1,2,0:T(2,128)(2,1)} %param.16) | copy-start | bytes 92164
  2.4 11.6 %collective-permute-start = (bf16[2,128,128]{2,1,0:T(8,128)(2,1)S(1)}, bf16[2,128,128]{2,1,0:T(8,128)(2,1)S(1)}, u32[]{:S(2)}, u32[]{:S(2)}) collective-permute-start(bf16[2,128,128]{2,1,0:T(8,128)(2,1)S(1)} %get-tuple-element.39), channel_id=1, source_target_pairs={{0,4},{4,0},{8,12},{12,8},{16,20},{20,16},{24,28},{28,24},{32,36},... | collective-permute-start | bytes 196616 | tf_op jit(solution)/shard_map/ppermute | solution.py:378
  3.7 10.7 %collective-permute-start.1 = (bf16[2,128,128]{2,1,0:T(8,128)(2,1)S(1)}, bf16[2,128,128]{2,1,0:T(8,128)(2,1)S(1)}, u32[]{:S(2)}, u32[]{:S(2)}) collective-permute-start(bf16[2,128,128]{2,1,0:T(8,128)(2,1)S(1)} %get-tuple-element.40), channel_id=1, source_target_pairs={{4,8},{8,4},{12,16},{16,12},{20,24},{24,20},{28,32},{32,28},{36,40... | collective-permute-start | bytes 196616 | tf_op jit(solution)/shard_map/ppermute | solution.py:378
  14.4 5.4 %copy-start.1 = (bf16[30,128]{1,0:T(8,128)(2,1)S(1)}, bf16[30,128]{1,0:T(8,128)(2,1)}, u32[]{:S(2)}) copy-start(bf16[30,128]{1,0:T(8,128)(2,1)} %enc_first.3) | copy-start | bytes 23044
  14.4 5.3 %collective-permute-start.2 = (bf16[6,48,128]{2,1,0:T(8,128)(2,1)S(1)}, bf16[6,48,128]{2,1,0:T(8,128)(2,1)S(1)}, u32[]{:S(2)}, u32[]{:S(2)}) collective-permute-start(bf16[6,48,128]{2,1,0:T(8,128)(2,1)S(1)} %get-tuple-element.43), channel_id=1, source_target_pairs={{0,1},{1,0},{2,3},{3,2},{4,5},{5,4},{6,7},{7,6},{8,9},{9,8},{10,11... | collective-permute-start | bytes 221192 | tf_op jit(solution)/shard_map/ppermute | solution.py:378
  16.6 9.6 %collective-permute-start.3 = (bf16[6,48,128]{2,1,0:T(8,128)(2,1)S(1)}, bf16[6,48,128]{2,1,0:T(8,128)(2,1)S(1)}, u32[]{:S(2)}, u32[]{:S(2)}) collective-permute-start(bf16[6,48,128]{2,1,0:T(8,128)(2,1)S(1)} %get-tuple-element.51), channel_id=1, source_target_pairs={{1,2},{2,1},{5,6},{6,5},{9,10},{10,9},{13,14},{14,13},{17,18},{18,... | collective-permute-start | bytes 221192 | tf_op jit(solution)/shard_map/ppermute | solution.py:378
  32.4 2.7 %collective-permute-start.5 = (bf16[4,128,128]{2,1,0:T(8,128)(2,1)S(1)}, bf16[4,128,128]{2,1,0:T(8,128)(2,1)S(1)}, u32[]{:S(2)}, u32[]{:S(2)}) collective-permute-start(bf16[4,128,128]{2,1,0:T(8,128)(2,1)S(1)} %get-tuple-element.58), channel_id=1, source_target_pairs={{0,1},{1,0},{2,3},{3,2},{4,5},{5,4},{6,7},{7,6},{8,9},{9,8},{10,11... | collective-permute-start | bytes 393224 | tf_op jit(solution)/shard_map/ppermute | solution.py:378
  32.7 6.3 %collective-permute-start.4 = (bf16[4,128,128]{2,1,0:T(8,128)(2,1)S(1)}, bf16[4,128,128]{2,1,0:T(8,128)(2,1)S(1)}, u32[]{:S(2)}, u32[]{:S(2)}) collective-permute-start(bf16[4,128,128]{2,1,0:T(8,128)(2,1)S(1)} %get-tuple-element.56), channel_id=1, source_target_pairs={{1,2},{2,1},{5,6},{6,5},{9,10},{10,9},{13,14},{14,13},{17,18},{18,... | collective-permute-start | bytes 393224 | tf_op jit(solution)/shard_map/ppermute | solution.py:378
  41.5 8.9 %collective-permute-start.6 = (bf16[2,128,128]{2,1,0:T(8,128)(2,1)S(1)}, bf16[2,128,128]{2,1,0:T(8,128)(2,1)S(1)}, u32[]{:S(2)}, u32[]{:S(2)}) collective-permute-start(bf16[2,128,128]{2,1,0:T(8,128)(2,1)S(1)} %get-tuple-element.64), channel_id=1, source_target_pairs={{0,4},{4,0},{8,12},{12,8},{16,20},{20,16},{24,28},{28,24},{32,36},... | collective-permute-start | bytes 196616 | tf_op jit(solution)/shard_map/ppermute | solution.py:378
  41.6 10.7 %collective-permute-start.7 = (bf16[2,128,128]{2,1,0:T(8,128)(2,1)S(1)}, bf16[2,128,128]{2,1,0:T(8,128)(2,1)S(1)}, u32[]{:S(2)}, u32[]{:S(2)}) collective-permute-start(bf16[2,128,128]{2,1,0:T(8,128)(2,1)S(1)} %get-tuple-element.65), channel_id=1, source_target_pairs={{4,8},{8,4},{12,16},{16,12},{20,24},{24,20},{28,32},{32,28},{36,40... | collective-permute-start | bytes 196616 | tf_op jit(solution)/shard_map/ppermute | solution.py:378
  52.4 4.4 %collective-permute-start.9 = (bf16[4,128,128]{2,1,0:T(8,128)(2,1)S(1)}, bf16[4,128,128]{2,1,0:T(8,128)(2,1)S(1)}, u32[]{:S(2)}, u32[]{:S(2)}) collective-permute-start(bf16[4,128,128]{2,1,0:T(8,128)(2,1)S(1)} %get-tuple-element.67), channel_id=1, source_target_pairs={{0,1},{1,0},{2,3},{3,2},{4,5},{5,4},{6,7},{7,6},{8,9},{9,8},{10,11... | collective-permute-start | bytes 393224 | tf_op jit(solution)/shard_map/ppermute | solution.py:378
  52.5 7.7 %collective-permute-start.8 = (bf16[4,128,128]{2,1,0:T(8,128)(2,1)S(1)}, bf16[4,128,128]{2,1,0:T(8,128)(2,1)S(1)}, u32[]{:S(2)}, u32[]{:S(2)}) collective-permute-start(bf16[4,128,128]{2,1,0:T(8,128)(2,1)S(1)} %get-tuple-element.66), channel_id=1, source_target_pairs={{1,2},{2,1},{5,6},{6,5},{9,10},{10,9},{13,14},{14,13},{17,18},{18,... | collective-permute-start | bytes 393224 | tf_op jit(solution)/shard_map/ppermute | solution.py:378
  60.2 0.7 %copy-start.2 = (bf16[128,2]{0,1:T(2,128)(2,1)S(1)}, bf16[128,2]{0,1:T(2,128)(2,1)}, u32[]{:S(2)}) copy-start(bf16[128,2]{0,1:T(2,128)(2,1)} %param.31) | copy-start | bytes 1540

commit v7 on v5

--- a/solution.py
+++ b/solution.py
@@ -14,7 +14,7 @@
 KNB = 16
 SLOTS = 128
 PACK = 48
-GEO = 16
+GEO = 32
 WIDE = 8
 UNROLL = 4
 BLOCKED = -(2.0**40)
@@ -93,11 +93,8 @@
         values = geo_w[t]
         high = values.astype(bf16).astype(f32)
         low = values - high
-        rows = []
-        for c in range(3):
-            rows += [high[c : c + 1], high[c : c + 1], low[c : c + 1], low[c : c + 1]]
-        rows.append(jnp.full((1, EH), BLOCKED, f32))
-        rows.append(jnp.zeros((GEO - 13, EH), f32))
+        blank = jnp.zeros((5, EH), f32)
+        rows = [high, jnp.full((1, EH), BLOCKED, f32), blank[:4], high, blank, low, blank, jnp.zeros((8, EH), f32)]
         full_w[t, LAT:, :] = jnp.concatenate(rows, axis=0).astype(bf16)
 
 
@@ -161,13 +158,10 @@
     delta_x = got[0:1] + got[1:2] + got[2:3] - own_x
     delta_y = got[3:4] + got[4:5] + got[5:6] - own_y
     distance = delta_x * delta_x + delta_y * delta_y
-    pieces = []
-    for v in (delta_x, delta_y, distance):
-        high = v.astype(bf16).astype(f32)
-        pieces += [high, v - high, high, v - high]
-    pieces.append(1.0 - own_live * got[6:7])
-    pieces.append(jnp.zeros((GEO - 13, got.shape[1]), f32))
-    return jnp.concatenate(pieces, axis=0).astype(bf16)
+    blocked = 1.0 - own_live * got[6:7]
+    values = jnp.concatenate([delta_x, delta_y, distance, blocked, jnp.zeros((4, got.shape[1]), f32)], axis=0)
+    high = values.astype(bf16).astype(f32)
+    return jnp.concatenate([high, values - high, high, jnp.zeros_like(high)], axis=0).astype(bf16)
 
 
 def edge_sum(full_w, right_side, bound, total):

time: 63.2 us -> 63.1 us (level)
  no operation moved by 1% of the time
where the time goes in v7:
time: 63.1 us; the launch traced here: 62.8 us
  starting transfers between devices  31.4 us (50%)
  Pallas kernels  27.9 us (44%)
  waiting for transfers between devices  2.71 us (4%)
  between operations  0.81 us (1%)
    ppermute x10, starting transfers between devices, swap(): return lax.ppermute(block, axis, swaps(lax.axis_size(axis), start))  31.4 us
    pallas_call x10, Pallas kernels, run(): pl.pallas_call(kernel, out_shape=[jax.ShapeDtypeStruct(shape, dtype) for...  27.9 us
    ppermute x10, waiting for transfers between devices, swap(): return lax.ppermute(block, axis, swaps(lax.axis_size(axis), start))  2.71 us
  transfers between devices with their start and end apart: 10, of which 3 were waited for; matrix products, arithmetic and copies ran while one was open for 0% of the time, Pallas kernels for 24%

profile of v7, /device:TPU:17, one launch (start us, length us, event | category | flops | bytes accessed | tf_op | source)
XLA Modules:
  0.0 62.8 jit_solution(2281408242381990779)
XLA Ops:
  0.6 1.0 %prepare.1 = (bf16[2,2,48,128]{3,2,1,0:T(8,128)(2,1)S(1)}, s32[2,2,16,128]{3,2,1,0:T(8,128)S(1)}, bf16[2,128,128]{2,1,0:T(8,128)(2,1)S(1)}, bf16[2,128,128]{2,1,0:T(8,128)(2,1)S(1)}) custom-call(bf16[2,30,2,128]{3,2,1,0:T(2,128)(2,1)} %bitcast.2, f32[2,2,2,128]{3,2,1,0:T(2,128)} %refs_10_.1, s32[2,2]{1,0:T(2,128)} %occupancy_in.1, ...), custom_call_target="tpu_custom_call" | custom-call | tf_op jit(solution)/shard_map/prepare/pallas_call | solution.py:352
  1.6 1.3 %collective-permute-start = (bf16[2,128,128]{2,1,0:T(8,128)(2,1)S(1)}, bf16[2,128,128]{2,1,0:T(8,128)(2,1)S(1)}, u32[]{:S(2)}, u32[]{:S(2)}) collective-permute-start(bf16[2,128,128]{2,1,0:T(8,128)(2,1)S(1)} %get-tuple-element.41), channel_id=1, source_target_pairs={{0,4},{4,0},{8,12},{12,8},{16,20},{20,16},{24,28},{28,24},{32,36},... | collective-permute-start | bytes 196616 | tf_op jit(solution)/shard_map/ppermute | solution.py:372
  2.9 8.8 %collective-permute-start.1 = (bf16[2,128,128]{2,1,0:T(8,128)(2,1)S(1)}, bf16[2,128,128]{2,1,0:T(8,128)(2,1)S(1)}, u32[]{:S(2)}, u32[]{:S(2)}) collective-permute-start(bf16[2,128,128]{2,1,0:T(8,128)(2,1)S(1)} %get-tuple-element.42), channel_id=1, source_target_pairs={{4,8},{8,4},{12,16},{16,12},{20,24},{24,20},{28,32},{32,28},{36,40... | collective-permute-start | bytes 196616 | tf_op jit(solution)/shard_map/ppermute | solution.py:372
  11.7 1.5 %weights.1 = (bf16[3,160,512]{2,1,0:T(8,128)(2,1)S(1)}, bf16[3,128,512]{2,1,0:T(8,128)(2,1)S(1)}, bf16[3,512,128]{2,1,0:T(8,128)(2,1)S(1)}, bf16[3,256,128]{2,1,...) custom-call(s32[2,2,16,128]{3,2,1,0:T(8,128)S(1)} %get-tuple-element, ...), custom_call_target="tpu_custom_call" | custom-call | flops 1073741824 | bytes 4194304 | tf_op jit(solution)/shard_map/weights/pallas_call | solution.py:352
  13.2 0.0 collective-permute-done.got_a
  13.2 0.4 collective-permute-done.1.got_b
  13.6 2.2 %collective-permute-start.2 = (bf16[6,48,128]{2,1,0:T(8,128)(2,1)S(1)}, bf16[6,48,128]{2,1,0:T(8,128)(2,1)S(1)}, u32[]{:S(2)}, u32[]{:S(2)}) collective-permute-start(bf16[6,48,128]{2,1,0:T(8,128)(2,1)S(1)} %get-tuple-element.45), channel_id=1, source_target_pairs={{0,1},{1,0},{2,3},{3,2},{4,5},{5,4},{6,7},{7,6},{8,9},{9,8},{10,11... | collective-permute-start | bytes 221192 | tf_op jit(solution)/shard_map/ppermute | solution.py:372
  15.8 3.1 %collective-permute-start.3 = (bf16[6,48,128]{2,1,0:T(8,128)(2,1)S(1)}, bf16[6,48,128]{2,1,0:T(8,128)(2,1)S(1)}, u32[]{:S(2)}, u32[]{:S(2)}) collective-permute-start(bf16[6,48,128]{2,1,0:T(8,128)(2,1)S(1)} %get-tuple-element.54), channel_id=1, source_target_pairs={{1,2},{2,1},{5,6},{6,5},{9,10},{10,9},{13,14},{14,13},{17,18},{18,... | collective-permute-start | bytes 221192 | tf_op jit(solution)/shard_map/ppermute | solution.py:372
  19.0 0.0 collective-permute-done.2.got_c
  19.0 6.4 %first_early.1 = (bf16[6,2,48,128]{3,2,1,0:T(8,128)(2,1)S(1)}, s32[4,2,16,128]{3,2,1,0:T(8,128)S(1)}, bf16[6,2,128,128]{3,2,1,0:T(8,128)(2,1)S(1)}, f32[512,512]...) custom-call(bf16[2,2,48,128]{3,2,1,0:T(8,128)(2,1)S(1)} %get-tuple-element.40.own.raw, ...), custom_call_target="tpu_custom_call" | custom-call | flops 2147483648 | bytes 4194304 | tf_op jit(solution)/shard_map/first_early/pallas_call | solution.py:352
  25.4 6.2 %first_step.1 = (bf16[4,2,128,128]{3,2,1,0:T(8,128)(2,1)S(1)}, bf16[4,32,2048]{2,1,0:T(8,128)(2,1)S(1)}, bf16[4,128,128]{2,1,0:T(8,128)(2,1)S(1)}, bf16[4,128,128]{2,1,0:T(8,128)(2,1)S(1)}) custom-call(bf16[6,2,48,128]{3,2,1,0:T(8,128)(2,1)S(1)} %get-tuple-element.49.pack, s32[4,2,16,128]{3,2,1,0:T(8,128)S(1)} %get-tuple-element.50.codes_all, ...), custom_call_target="tpu_custom_call" | custom-call | tf_op jit(solution)/shard_map/first_step/pallas_call | solution.py:352
  31.6 0.3 collective-permute-start.5
  31.9 2.4 %collective-permute-start.4 = (bf16[4,128,128]{2,1,0:T(8,128)(2,1)S(1)}, bf16[4,128,128]{2,1,0:T(8,128)(2,1)S(1)}, u32[]{:S(2)}, u32[]{:S(2)}) collective-permute-start(bf16[4,128,128]{2,1,0:T(8,128)(2,1)S(1)} %get-tuple-element.59), channel_id=1, source_target_pairs={{1,2},{2,1},{5,6},{6,5},{9,10},{10,9},{13,14},{14,13},{17,18},{18,... | collective-permute-start | bytes 393224 | tf_op jit(solution)/shard_map/ppermute | solution.py:372
  34.3 3.5 %middle_early.1 = (bf16[512,256]{1,0:T(8,128)(2,1)S(1)}, bf16[2,128,2048]{2,1,0:T(8,128)(2,1)S(1)}, f32[512,256]{1,0:T(8,128)S(1)}) custom-call(bf16[4,2,128,128]{3,2,1,0:T(8,128)(2,1)S(1)} %get-tuple-element.58.wide, bf16[4,128,128]{2,1,0:T(8,128)(2,1)S(1)} %collective-permute-done.5.got_c, s32[2,2,16,128]{3,2,1,0:T(8,128)S(1)} %get-tuple-element.43.token.own_codes, ...), custom_call_target="tpu_custom_call" | custom-call | flops 2147483648 | bytes 4194304 | tf_op jit(solution)/shard_map/middle_early/pallas_call | solution.py:352
  37.8 0.4 collective-permute-done.4.got_d
  38.1 2.5 %middle_step.1 = (bf16[2,2,128,128]{3,2,1,0:T(8,128)(2,1)S(1)}, bf16[2,128,128]{2,1,0:T(8,128)(2,1)S(1)}, bf16[2,128,128]{2,1,0:T(8,128)(2,1)S(1)}) custom-call(bf16[4,2,128,128]{3,2,1,0:T(8,128)(2,1)S(1)} %get-tuple-element.58.wide, bf16[4,128,128]{2,1,0:T(8,128)(2,1)S(1)} %collective-permute-done.4.got_d, ...), custom_call_target="tpu_custom_call" | custom-call | tf_op jit(solution)/shard_map/middle_step/pallas_call | solution.py:352
  40.7 0.1 collective-permute-start.6
  40.8 8.8 %collective-permute-start.7 = (bf16[2,128,128]{2,1,0:T(8,128)(2,1)S(1)}, bf16[2,128,128]{2,1,0:T(8,128)(2,1)S(1)}, u32[]{:S(2)}, u32[]{:S(2)}) collective-permute-start(bf16[2,128,128]{2,1,0:T(8,128)(2,1)S(1)} %get-tuple-element.68), channel_id=1, source_target_pairs={{4,8},{8,4},{12,16},{16,12},{20,24},{24,20},{28,32},{32,28},{36,40... | collective-permute-start | bytes 196616 | tf_op jit(solution)/shard_map/ppermute | solution.py:372
  49.6 1.9 %collective-permute-done.7.got_b = bf16[2,128,128]{2,1,0:T(8,128)(2,1)S(1)} collective-permute-done((bf16[2,128,128]{2,1,0:T(8,128)(2,1)S(1)}, bf16[2,128,128]{2,1,0:T(8,128)(2,1)S(1)}, u32[]{:S(2)}, u32[]{:S(2)}) %collective-permute-start.7) | collective-permute-done | bytes 65568 | tf_op jit(solution)/shard_map/ppermute | solution.py:372
  51.5 0.1 collective-permute-start.9
  51.6 4.2 %collective-permute-start.8 = (bf16[4,128,128]{2,1,0:T(8,128)(2,1)S(1)}, bf16[4,128,128]{2,1,0:T(8,128)(2,1)S(1)}, u32[]{:S(2)}, u32[]{:S(2)}) collective-permute-start(bf16[4,128,128]{2,1,0:T(8,128)(2,1)S(1)} %get-tuple-element.69), channel_id=1, source_target_pairs={{1,2},{2,1},{5,6},{6,5},{9,10},{10,9},{13,14},{14,13},{17,18},{18,... | collective-permute-start | bytes 393224 | tf_op jit(solution)/shard_map/ppermute | solution.py:372
  55.9 0.0 collective-permute-done.9.got_c
  55.9 3.5 %last_early.1 = (bf16[512,256]{1,0:T(8,128)(2,1)S(1)}, bf16[2,128,2048]{2,1,0:T(8,128)(2,1)S(1)}, f32[512,256]{1,0:T(8,128)S(1)}) custom-call(bf16[2,2,128,128]{3,2,1,0:T(8,128)(2,1)S(1)} %get-tuple-element.66.own, bf16[2,128,128]{2,1,0:T(8,128)(2,1)S(1)} %collective-permute-done.6.got_a, bf16[2,128,128]{2,1,0:T(8,128)(2,1)S(1)} %collective-permute-done.7.got_b, ...), custom_call_target="tpu_custom_call" | custom-call | flops 2147483648 | bytes 4194304 | tf_op jit(solution)/shard_map/last_early/pallas_call | solution.py:352
  59.4 3.4 %last_step.1 = (f32[2,2,2,128]{3,2,1,0:T(2,128)}, f32[2,2,2,128]{3,2,1,0:T(2,128)}) custom-call(bf16[2,2,128,128]{3,2,1,0:T(8,128)(2,1)S(1)} %get-tuple-element.66.own, bf16[4,128,128]{2,1,0:T(8,128)(2,1)S(1)} %collective-permute-done.8.got_d, s32[2,2,16,128]{3,2,1,0:T(8,128)S(1)} %get-tuple-element.43.token.own_codes, ...), custom_call_target="tpu_custom_call" | custom-call | tf_op jit(solution)/shard_map/last_step/pallas_call | solution.py:352
  (6 shorter events, 0.0 us)
Async XLA Ops:
  1.6 11.6 %collective-permute-start = (bf16[2,128,128]{2,1,0:T(8,128)(2,1)S(1)}, bf16[2,128,128]{2,1,0:T(8,128)(2,1)S(1)}, u32[]{:S(2)}, u32[]{:S(2)}) collective-permute-start(bf16[2,128,128]{2,1,0:T(8,128)(2,1)S(1)} %get-tuple-element.41), channel_id=1, source_target_pairs={{0,4},{4,0},{8,12},{12,8},{16,20},{20,16},{24,28},{28,24},{32,36},... | collective-permute-start | bytes 196616 | tf_op jit(solution)/shard_map/ppermute | solution.py:372
  2.9 10.7 %collective-permute-start.1 = (bf16[2,128,128]{2,1,0:T(8,128)(2,1)S(1)}, bf16[2,128,128]{2,1,0:T(8,128)(2,1)S(1)}, u32[]{:S(2)}, u32[]{:S(2)}) collective-permute-start(bf16[2,128,128]{2,1,0:T(8,128)(2,1)S(1)} %get-tuple-element.42), channel_id=1, source_target_pairs={{4,8},{8,4},{12,16},{16,12},{20,24},{24,20},{28,32},{32,28},{36,40... | collective-permute-start | bytes 196616 | tf_op jit(solution)/shard_map/ppermute | solution.py:372
  13.6 5.3 %collective-permute-start.2 = (bf16[6,48,128]{2,1,0:T(8,128)(2,1)S(1)}, bf16[6,48,128]{2,1,0:T(8,128)(2,1)S(1)}, u32[]{:S(2)}, u32[]{:S(2)}) collective-permute-start(bf16[6,48,128]{2,1,0:T(8,128)(2,1)S(1)} %get-tuple-element.45), channel_id=1, source_target_pairs={{0,1},{1,0},{2,3},{3,2},{4,5},{5,4},{6,7},{7,6},{8,9},{9,8},{10,11... | collective-permute-start | bytes 221192 | tf_op jit(solution)/shard_map/ppermute | solution.py:372
  15.8 9.5 %collective-permute-start.3 = (bf16[6,48,128]{2,1,0:T(8,128)(2,1)S(1)}, bf16[6,48,128]{2,1,0:T(8,128)(2,1)S(1)}, u32[]{:S(2)}, u32[]{:S(2)}) collective-permute-start(bf16[6,48,128]{2,1,0:T(8,128)(2,1)S(1)} %get-tuple-element.54), channel_id=1, source_target_pairs={{1,2},{2,1},{5,6},{6,5},{9,10},{10,9},{13,14},{14,13},{17,18},{18,... | collective-permute-start | bytes 221192 | tf_op jit(solution)/shard_map/ppermute | solution.py:372
  31.6 2.7 %collective-permute-start.5 = (bf16[4,128,128]{2,1,0:T(8,128)(2,1)S(1)}, bf16[4,128,128]{2,1,0:T(8,128)(2,1)S(1)}, u32[]{:S(2)}, u32[]{:S(2)}) collective-permute-start(bf16[4,128,128]{2,1,0:T(8,128)(2,1)S(1)} %get-tuple-element.61), channel_id=1, source_target_pairs={{0,1},{1,0},{2,3},{3,2},{4,5},{5,4},{6,7},{7,6},{8,9},{9,8},{10,11... | collective-permute-start | bytes 393224 | tf_op jit(solution)/shard_map/ppermute | solution.py:372
  31.9 6.3 %collective-permute-start.4 = (bf16[4,128,128]{2,1,0:T(8,128)(2,1)S(1)}, bf16[4,128,128]{2,1,0:T(8,128)(2,1)S(1)}, u32[]{:S(2)}, u32[]{:S(2)}) collective-permute-start(bf16[4,128,128]{2,1,0:T(8,128)(2,1)S(1)} %get-tuple-element.59), channel_id=1, source_target_pairs={{1,2},{2,1},{5,6},{6,5},{9,10},{10,9},{13,14},{14,13},{17,18},{18,... | collective-permute-start | bytes 393224 | tf_op jit(solution)/shard_map/ppermute | solution.py:372
  40.7 9.0 %collective-permute-start.6 = (bf16[2,128,128]{2,1,0:T(8,128)(2,1)S(1)}, bf16[2,128,128]{2,1,0:T(8,128)(2,1)S(1)}, u32[]{:S(2)}, u32[]{:S(2)}) collective-permute-start(bf16[2,128,128]{2,1,0:T(8,128)(2,1)S(1)} %get-tuple-element.67), channel_id=1, source_target_pairs={{0,4},{4,0},{8,12},{12,8},{16,20},{20,16},{24,28},{28,24},{32,36},... | collective-permute-start | bytes 196616 | tf_op jit(solution)/shard_map/ppermute | solution.py:372
  40.8 10.7 %collective-permute-start.7 = (bf16[2,128,128]{2,1,0:T(8,128)(2,1)S(1)}, bf16[2,128,128]{2,1,0:T(8,128)(2,1)S(1)}, u32[]{:S(2)}, u32[]{:S(2)}) collective-permute-start(bf16[2,128,128]{2,1,0:T(8,128)(2,1)S(1)} %get-tuple-element.68), channel_id=1, source_target_pairs={{4,8},{8,4},{12,16},{16,12},{20,24},{24,20},{28,32},{32,28},{36,40... | collective-permute-start | bytes 196616 | tf_op jit(solution)/shard_map/ppermute | solution.py:372
  51.5 4.3 %collective-permute-start.9 = (bf16[4,128,128]{2,1,0:T(8,128)(2,1)S(1)}, bf16[4,128,128]{2,1,0:T(8,128)(2,1)S(1)}, u32[]{:S(2)}, u32[]{:S(2)}) collective-permute-start(bf16[4,128,128]{2,1,0:T(8,128)(2,1)S(1)} %get-tuple-element.70), channel_id=1, source_target_pairs={{0,1},{1,0},{2,3},{3,2},{4,5},{5,4},{6,7},{7,6},{8,9},{9,8},{10,11... | collective-permute-start | bytes 393224 | tf_op jit(solution)/shard_map/ppermute | solution.py:372
  51.6 7.7 %collective-permute-start.8 = (bf16[4,128,128]{2,1,0:T(8,128)(2,1)S(1)}, bf16[4,128,128]{2,1,0:T(8,128)(2,1)S(1)}, u32[]{:S(2)}, u32[]{:S(2)}) collective-permute-start(bf16[4,128,128]{2,1,0:T(8,128)(2,1)S(1)} %get-tuple-element.69), channel_id=1, source_target_pairs={{1,2},{2,1},{5,6},{6,5},{9,10},{10,9},{13,14},{14,13},{17,18},{18,... | collective-permute-start | bytes 393224 | tf_op jit(solution)/shard_map/ppermute | solution.py:372
